TPU v7x, 512 devices: a whole 4x8x8 slice. The times are simulated.
512 devices in a mesh: section: 4 (over y_hi), seq: 32 (over z, y_lo, core), exp: 4 (over x).
Axes of the slice: x: 4, y: 8 (y_hi: 4, y_lo: 2; y = y_hi * 2 + y_lo), z: 8, core: 2. Of those that a mesh axis runs over, the one named last changes fastest.
Arguments:
- latent: bfloat16 [8, 128, 64, 384], P('section', 'seq', 'exp'), may hold values from -6 to 6
- cotangent: bfloat16 [8, 128, 64, 384], P('section', 'seq', 'exp'), may hold values from -6 to 6
- gain_one: float32 [384], replicated, may hold values from 0.5 to 2
- gain_two: float32 [384], replicated, may hold values from 0.5 to 2
- kernel_one: bfloat16 [3, 3, 3, 384, 384], P(None, None, None, 'exp'), may hold values from -0.0625 to 0.0625
- kernel_two: bfloat16 [3, 3, 3, 384, 384], P(None, None, None, 'exp'), may hold values from -0.0625 to 0.0625
Outputs:
- block_out: bfloat16 [8, 128, 64, 384], P('section', 'seq', 'exp')
- latent_grad: bfloat16 [8, 128, 64, 384], P('section', 'seq', 'exp')
All inputs are finite; a program needn't handle non-finite values.
Results may differ from a plain program's by a relative error of at most 0.015.
Values may be sent and summed in bfloat16 or wider, within the bound.
No kernel may reach another device: no remote copies, remote signals or barrier semaphores. Data moves between devices by JAX's collectives and lax.ppermute only.
A program may use at most 64 MiB of HBM per device.

v0:
```python
import jax
import jax.numpy as jnp
from jax import lax
from jax.sharding import PartitionSpec as P

epsilon = 1e-06


def from_behind(shard, axis, by):
    size = lax.axis_size(axis)
    pairs = [(i, i + by) for i in range(size) if 0 <= i + by < size]
    return lax.ppermute(shard, axis, pairs)


def extended_2(block, sides, width):
    for axis, dim in sides:
        count = lax.axis_size(axis)
        forward = [(i, i + 1) for i in range(count - 1)]
        backward = [(target, source) for source, target in forward]
        low = lax.ppermute(
            lax.slice_in_dim(block, block.shape[dim] - width, None, axis=dim), axis, forward
        )
        high = lax.ppermute(lax.slice_in_dim(block, 0, width, axis=dim), axis, backward)
        block = jnp.concatenate([low, block, high], axis=dim)
    return block


def copy_for_each(shard, axis):
    copies = jnp.broadcast_to(shard, (lax.axis_size(axis), *shard.shape))
    return lax.all_to_all(copies, axis, split_axis=0, concat_axis=0, tiled=True)


def joined_along(pieces, dim):
    shape = list(pieces.shape[1:])
    shape[dim] *= pieces.shape[0]
    return jnp.moveaxis(pieces, 0, dim).reshape(shape)


def gathered_copies(shard, axis, dim):
    pieces = copy_for_each(shard, axis)
    return joined_along(pieces, dim)


def cut_along(shard, dim, size):
    before, after = (shard.shape[:dim], shard.shape[dim + 1 :])
    return jnp.moveaxis(shard.reshape(*before, size, -1, *after), dim, 0)


def cut_rows(length, count):
    unit = 8 if length >= 8 * count else 1
    return [length // unit * k // count * unit for k in range(1, count)]


def several_exchanges(shard, axis, pieces, split_dim, concat_dim):
    blocks = cut_along(shard, split_dim, lax.axis_size(axis))
    split_at = max(range(1, max(2, blocks.ndim - 1)), key=lambda d: blocks.shape[d])
    done = []
    for section in jnp.split(blocks, cut_rows(blocks.shape[split_at], pieces), axis=split_at):
        if section.size:
            done.append(lax.all_to_all(section, axis, split_axis=0, concat_axis=0, tiled=True))
    return joined_along(jnp.concatenate(done, axis=split_at), concat_dim)


def sent_and_summed(shard, axis, dim):
    pieces = cut_along(shard, dim, lax.axis_size(axis))
    arrived = lax.all_to_all(pieces, axis, split_axis=0, concat_axis=0, tiled=True)
    return arrived.astype(jnp.float32).sum(axis=0)


def normalize(values, gain):
    inverse = lax.rsqrt(jnp.mean(values * values, axis=-1, keepdims=True) + epsilon)
    return (values * inverse * gain, inverse)


def norm_backward(values, inverse, gain, upstream):
    scaled = upstream * gain
    return inverse * scaled - values * inverse**3 * jnp.mean(
        values * scaled, axis=-1, keepdims=True
    )


def silu_slope(normed):
    sigma = jax.nn.sigmoid(normed)
    return sigma * (1.0 + normed * (1.0 - sigma))


def forward_kernel(weight):
    swapped = jnp.swapaxes(weight, 3, 4)
    return swapped.reshape(3, 3, 3 * swapped.shape[3], swapped.shape[4])


def backward_kernel(weight):
    flipped = weight[::-1, ::-1, ::-1]
    return flipped.reshape(3, 3, 3 * flipped.shape[3], flipped.shape[4])


def conv_taps(padded, kernel, frame_count, row_count, col_count):
    summed = jnp.zeros((frame_count * row_count * col_count, kernel.shape[3]), jnp.float32)
    for time_tap in range(3):
        for row_tap in range(3):
            columns = jnp.concatenate(
                [
                    padded[
                        time_tap : time_tap + frame_count,
                        row_tap : row_tap + row_count,
                        col_tap : col_tap + col_count,
                    ]
                    for col_tap in range(3)
                ],
                axis=-1,
            )
            columns = columns.reshape(frame_count * row_count * col_count, columns.shape[-1])
            summed = summed + jnp.dot(
                columns, kernel[time_tap, row_tap], preferred_element_type=jnp.float32
            )
    return summed.reshape(frame_count, row_count, col_count, kernel.shape[3])


def forward_conv(active, weight):
    frame_count, row_count, col_count = (active.shape[0], active.shape[1], active.shape[2])
    earlier = from_behind(active, "section", 1)
    extended = jnp.concatenate([earlier, active], axis=0)
    bordered = extended_2(extended, (("seq", 1),), 1)
    gathered = gathered_copies(bordered, "exp", 2)
    padded = jnp.pad(gathered, ((0, 0), (0, 0), (1, 1), (0, 0)))
    partial_value = conv_taps(
        padded, forward_kernel(weight), frame_count, row_count, gathered.shape[2]
    )
    return lax.all_to_all(
        partial_value.astype(jnp.bfloat16), "exp", split_axis=2, concat_axis=3, tiled=True
    ).astype(partial_value.dtype)


def backward_conv(upstream, weight):
    frame_count, row_count, col_count = (upstream.shape[0], upstream.shape[1], upstream.shape[2])
    following = from_behind(upstream, "section", -1)
    extended = jnp.concatenate([upstream, following], axis=0)
    regrouped = several_exchanges(extended, "exp", 2, 3, 2)
    bordered = extended_2(regrouped, (("seq", 1),), 1)
    padded = jnp.pad(bordered, ((0, 0), (0, 0), (1, 1), (0, 0)))
    partial_value = conv_taps(
        padded, backward_kernel(weight), frame_count, row_count, regrouped.shape[2]
    )
    return sent_and_summed(partial_value.astype(jnp.bfloat16), "exp", 2)


def body(latent, cotangent, gain_one, gain_two, kernel_one, kernel_two):
    weight_one, weight_two = (kernel_one, kernel_two)
    source = latent.astype(jnp.float32)
    normed_one, inverse_one = normalize(source, gain_one)
    active_one = jax.nn.silu(normed_one).astype(jnp.bfloat16)
    inner = forward_conv(active_one, weight_one)
    normed_two, inverse_two = normalize(inner, gain_two)
    active_two = jax.nn.silu(normed_two).astype(jnp.bfloat16)
    branch = forward_conv(active_two, weight_two)
    block_out = (source + branch).astype(jnp.bfloat16)
    grad_two = backward_conv(cotangent, weight_two)
    grad_inner = norm_backward(
        inner, inverse_two, gain_two, grad_two * silu_slope(normed_two)
    ).astype(jnp.bfloat16)
    grad_one = backward_conv(grad_inner, weight_one)
    latent_grad = cotangent.astype(jnp.float32) + norm_backward(
        source, inverse_one, gain_one, grad_one * silu_slope(normed_one)
    )
    return (block_out, latent_grad.astype(jnp.bfloat16))


def solution(mesh):
    in_specs = (
        P("section", "seq", "exp", None),
        P("section", "seq", "exp", None),
        P(),
        P(),
        P(None, None, None, "exp", None),
        P(None, None, None, "exp", None),
    )
    out_specs = (P("section", "seq", "exp", None), P("section", "seq", "exp", None))
    return jax.shard_map(body, mesh=mesh, in_specs=in_specs, out_specs=out_specs, check_vma=False)
```

profile of v0, /device:TPU:256, one launch (start us, length us, event | category | flops | bytes accessed | tf_op | source)
XLA Modules:
  0.0 185.5 jit_solution(6205475711255388240)
XLA Ops:
  0.6 1.4 collective-permute-start.6
  2.1 1.0 fusion.55
  3.1 1.0 fusion.63
  4.1 5.5 %collective-permute-start = (bf16[2,4,16,384]{3,2,1,0:T(8,128)(2,1)S(1)}, bf16[2,4,16,384]{3,2,1,0:T(8,128)(2,1)S(1)}, u32[]{:S(2)}, u32[]{:S(2)}) collective-permute-start(bf16[2,4,16,384]{3,2,1,0:T(8,128)(2,1)S(1)} %fusion.63), channel_id=1, source_target_pairs={{0,128},{128,256},{256,384},{1,129},{129,257},{257,385},{2,130},{1... | collective-permute-start | bytes 294920 | tf_op jit(solution)/shard_map/ppermute | solution.py:12
  9.6 0.8 collective-permute-done.6
  10.4 0.9 pad_maximum_fusion.34
  11.6 0.7 copy.42
  12.3 4.3 %all-to-all-start.5 = ((bf16[4,4,4,8,96]{4,3,2,1,0:T(8,128)(2,1)}), bf16[4,4,4,8,96]{4,3,2,1,0:T(8,128)(2,1)S(1)}, u32[]{:S(2)}, u32[]{:S(2)}) async-start(bf16[4,4,4,8,96]{4,3,2,1,0:T(8,128)(2,1)} %copy.42), calls=%async_computation.5 | async-start | bytes 262144 | tf_op jit(solution)/shard_map/all_to_all | solution.py:60
  16.6 1.9 %collective-permute-start.2 = (bf16[4,1,16,384]{3,2,1,0:T(8,128)(2,1)S(1)}, bf16[4,1,16,384]{3,2,1,0:T(8,128)(2,1)S(1)}, u32[]{:S(2)}, u32[]{:S(2)}) collective-permute-start(bf16[4,1,16,384]{3,2,1,0:T(8,128)(2,1)S(1)} %get-tuple-element.131), channel_id=1, source_target_pairs={{4,0},{8,4},{12,8},{16,12},{20,16},{24,20},{28,24},{32,28},{36,32}... | collective-permute-start | bytes 147464 | tf_op jit(solution)/shard_map/ppermute | solution.py:23
  18.5 2.4 %collective-permute-start.1 = (bf16[4,1,16,384]{3,2,1,0:T(8,128)(2,1)S(1)}, bf16[4,1,16,384]{3,2,1,0:T(8,128)(2,1)S(1)}, u32[]{:S(2)}, u32[]{:S(2)}) collective-permute-start(bf16[4,1,16,384]{3,2,1,0:T(8,128)(2,1)S(1)} %get-tuple-element.130), channel_id=1, source_target_pairs={{0,4},{4,8},{8,12},{12,16},{16,20},{20,24},{24,28},{28,32},{32,36}... | collective-permute-start | bytes 147464 | tf_op jit(solution)/shard_map/ppermute | solution.py:20
  21.0 1.5 copy.54
  22.5 1.8 rev.6
  24.4 0.7 copy.41
  25.0 4.8 %all-to-all-start.4 = ((bf16[4,4,4,8,96]{4,3,2,1,0:T(8,128)(2,1)}), bf16[4,4,4,8,96]{4,3,2,1,0:T(8,128)(2,1)S(1)}, u32[]{:S(2)}, u32[]{:S(2)}) async-start(bf16[4,4,4,8,96]{4,3,2,1,0:T(8,128)(2,1)} %copy.41), calls=%async_computation.4 | async-start | bytes 262144 | tf_op jit(solution)/shard_map/all_to_all | solution.py:60
  29.9 5.9 %all-to-all-done.4 = bf16[4,4,4,8,96]{4,3,2,1,0:T(8,128)(2,1)S(1)} async-done(((bf16[4,4,4,8,96]{4,3,2,1,0:T(8,128)(2,1)}), bf16[4,4,4,8,96]{4,3,2,1,0:T(8,128)(2,1)S(1)}, u32[]{:S(2)}, u32[]{:S(2)}) %all-to-all-start.4) | async-done | bytes 98336 | tf_op jit(solution)/shard_map/all_to_all | solution.py:60
  35.8 1.1 broadcast_in_dim.4
  36.9 3.5 %all-to-all-start = ((bf16[4,4,6,16,384]{4,3,2,1,0:T(8,128)(2,1)}), bf16[4,4,6,16,384]{4,3,2,1,0:T(8,128)(2,1)S(1)}, u32[]{:S(2)}, u32[]{:S(2)}) async-start(bf16[4,4,6,16,384]{4,3,2,1,0:T(8,128)(2,1)} %broadcast_in_dim.4), calls=%async_computation | async-start | bytes 2359296 | tf_op jit(solution)/shard_map/all_to_all | solution.py:30
  40.6 3.8 %collective-permute-start.8 = (bf16[4,1,64,96]{3,2,1,0:T(8,128)(2,1)S(1)}, bf16[4,1,64,96]{3,2,1,0:T(8,128)(2,1)S(1)}, u32[]{:S(2)}, u32[]{:S(2)}) collective-permute-start(bf16[4,1,64,96]{3,2,1,0:T(8,128)(2,1)S(1)} %get-tuple-element.123), channel_id=1, source_target_pairs={{4,0},{8,4},{12,8},{16,12},{20,16},{24,20},{28,24},{32,28},{36,32}... | collective-permute-start | bytes 147464 | tf_op jit(solution)/shard_map/ppermute | solution.py:23
  44.4 1.9 %collective-permute-start.7 = (bf16[4,1,64,96]{3,2,1,0:T(8,128)(2,1)S(1)}, bf16[4,1,64,96]{3,2,1,0:T(8,128)(2,1)S(1)}, u32[]{:S(2)}, u32[]{:S(2)}) collective-permute-start(bf16[4,1,64,96]{3,2,1,0:T(8,128)(2,1)S(1)} %get-tuple-element.122), channel_id=1, source_target_pairs={{0,4},{4,8},{8,12},{12,16},{16,20},{20,24},{24,28},{28,32},{32,36}... | collective-permute-start | bytes 147464 | tf_op jit(solution)/shard_map/ppermute | solution.py:20
  46.6 5.5 %collective-permute-done.7 = bf16[4,1,64,96]{3,2,1,0:T(8,128)(2,1)S(1)} collective-permute-done((bf16[4,1,64,96]{3,2,1,0:T(8,128)(2,1)S(1)}, bf16[4,1,64,96]{3,2,1,0:T(8,128)(2,1)S(1)}, u32[]{:S(2)}, u32[]{:S(2)}) %collective-permute-start.7) | collective-permute-done | bytes 49184 | tf_op jit(solution)/shard_map/ppermute | solution.py:20
  52.9 0.6 fusion.15
  57.8 0.8 copy.72
  58.6 4.5 %all-to-all-start.6 = ((bf16[4,2,4,16,384]{4,3,2,1,0:T(8,128)(2,1)}), bf16[4,2,4,16,384]{4,3,2,1,0:T(8,128)(2,1)S(1)}, u32[]{:S(2)}, u32[]{:S(2)}) async-start(bf16[4,2,4,16,384]{4,3,2,1,0:T(8,128)(2,1)} %bitcast.238), calls=%async_computation.6 | async-start | bytes 786432 | tf_op jit(solution)/shard_map/all_to_all | solution.py:66
  63.3 0.8 pad_slice_fusion.35
  64.5 0.8 pad_slice_fusion.34
  65.7 1.2 copy-done.2
  67.4 0.5 convolution_add_fusion.31
  68.2 0.5 convolution_add_fusion.30
  69.5 0.5 convolution_add_fusion.28
  70.8 0.5 convolution_add_fusion.26
  72.0 0.5 fusion.2
  72.6 0.8 copy.32
  73.4 4.8 %all-to-all-start.1 = ((bf16[2,4,64,96]{3,1,0,2:T(4,128)(2,1)}), bf16[2,4,64,96]{3,1,0,2:T(4,128)(2,1)S(1)}, u32[]{:S(2)}, u32[]{:S(2)}) async-start(bf16[2,4,64,96]{3,1,0,2:T(4,128)(2,1)} %copy.32), calls=%async_computation.1 | async-start | bytes 262144 | tf_op jit(solution)/shard_map/all_to_all | solution.py:129
  78.4 5.7 %all-to-all-done.1 = bf16[2,4,64,96]{3,1,0,2:T(4,128)(2,1)S(1)} async-done(((bf16[2,4,64,96]{3,1,0,2:T(4,128)(2,1)}), bf16[2,4,64,96]{3,1,0,2:T(4,128)(2,1)S(1)}, u32[]{:S(2)}, u32[]{:S(2)}) %all-to-all-start.1) | async-done | bytes 98336 | tf_op jit(solution)/shard_map/all_to_all | solution.py:129
  85.1 1.3 collective-permute-start.9
  86.4 7.0 %collective-permute-done.9 = bf16[2,4,16,384]{3,2,1,0:T(8,128)(2,1)S(1)} collective-permute-done((bf16[2,4,16,384]{3,2,1,0:T(8,128)(2,1)S(1)}, bf16[2,4,16,384]{3,2,1,0:T(8,128)(2,1)S(1)}, u32[]{:S(2)}, u32[]{:S(2)}) %collective-permute-start.9) | collective-permute-done | bytes 98336 | tf_op jit(solution)/shard_map/ppermute | solution.py:12
  93.7 0.7 copy.48
  94.4 3.3 %all-to-all-start.8 = ((bf16[4,4,4,8,96]{4,3,2,1,0:T(8,128)(2,1)}), bf16[4,4,4,8,96]{4,3,2,1,0:T(8,128)(2,1)S(1)}, u32[]{:S(2)}, u32[]{:S(2)}) async-start(bf16[4,4,4,8,96]{4,3,2,1,0:T(8,128)(2,1)} %copy.48), calls=%async_computation.8 | async-start | bytes 262144 | tf_op jit(solution)/shard_map/all_to_all | solution.py:60
  97.7 0.7 copy.47
  98.4 5.7 %all-to-all-done.8 = bf16[4,4,4,8,96]{4,3,2,1,0:T(8,128)(2,1)S(1)} async-done(((bf16[4,4,4,8,96]{4,3,2,1,0:T(8,128)(2,1)}), bf16[4,4,4,8,96]{4,3,2,1,0:T(8,128)(2,1)S(1)}, u32[]{:S(2)}, u32[]{:S(2)}) %all-to-all-start.8) | async-done | bytes 98336 | tf_op jit(solution)/shard_map/all_to_all | solution.py:60
  104.1 3.3 %all-to-all-start.7 = ((bf16[4,4,4,8,96]{4,3,2,1,0:T(8,128)(2,1)}), bf16[4,4,4,8,96]{4,3,2,1,0:T(8,128)(2,1)S(1)}, u32[]{:S(2)}, u32[]{:S(2)}) async-start(bf16[4,4,4,8,96]{4,3,2,1,0:T(8,128)(2,1)} %copy.47), calls=%async_computation.7 | async-start | bytes 262144 | tf_op jit(solution)/shard_map/all_to_all | solution.py:60
  107.5 1.8 rev.7
  109.2 5.9 %collective-permute-start.3 = (bf16[2,4,16,384]{3,2,1,0:T(8,128)(2,1)S(1)}, bf16[2,4,16,384]{3,2,1,0:T(8,128)(2,1)S(1)}, u32[]{:S(2)}, u32[]{:S(2)}) collective-permute-start(bf16[2,4,16,384]{3,2,1,0:T(8,128)(2,1)S(1)} %get-tuple-element.127), channel_id=1, source_target_pairs={{0,128},{128,256},{256,384},{1,129},{129,257},{257,385},{2,130},{1... | collective-permute-start | bytes 294920 | tf_op jit(solution)/shard_map/ppermute | solution.py:12
  115.2 1.9 %collective-permute-start.11 = (bf16[4,1,64,96]{3,2,1,0:T(8,128)(2,1)S(1)}, bf16[4,1,64,96]{3,2,1,0:T(8,128)(2,1)S(1)}, u32[]{:S(2)}, u32[]{:S(2)}) collective-permute-start(bf16[4,1,64,96]{3,2,1,0:T(8,128)(2,1)S(1)} %get-tuple-element.110), channel_id=1, source_target_pairs={{4,0},{8,4},{12,8},{16,12},{20,16},{24,20},{28,24},{32,28},{36,32}... | collective-permute-start | bytes 147464 | tf_op jit(solution)/shard_map/ppermute | solution.py:23
  117.1 2.6 %collective-permute-start.10 = (bf16[4,1,64,96]{3,2,1,0:T(8,128)(2,1)S(1)}, bf16[4,1,64,96]{3,2,1,0:T(8,128)(2,1)S(1)}, u32[]{:S(2)}, u32[]{:S(2)}) collective-permute-start(bf16[4,1,64,96]{3,2,1,0:T(8,128)(2,1)S(1)} %get-tuple-element.109), channel_id=1, source_target_pairs={{0,4},{4,8},{8,12},{12,16},{16,20},{20,24},{24,28},{28,32},{32,36}... | collective-permute-start | bytes 147464 | tf_op jit(solution)/shard_map/ppermute | solution.py:20
  119.9 5.0 %collective-permute-done.10 = bf16[4,1,64,96]{3,2,1,0:T(8,128)(2,1)S(1)} collective-permute-done((bf16[4,1,64,96]{3,2,1,0:T(8,128)(2,1)S(1)}, bf16[4,1,64,96]{3,2,1,0:T(8,128)(2,1)S(1)}, u32[]{:S(2)}, u32[]{:S(2)}) %collective-permute-start.10) | collective-permute-done | bytes 49184 | tf_op jit(solution)/shard_map/ppermute | solution.py:20
  130.7 0.8 copy.71
  131.5 4.8 %all-to-all-start.9 = ((bf16[4,2,4,16,384]{4,3,2,1,0:T(8,128)(2,1)}), bf16[4,2,4,16,384]{4,3,2,1,0:T(8,128)(2,1)S(1)}, u32[]{:S(2)}, u32[]{:S(2)}) async-start(bf16[4,2,4,16,384]{4,3,2,1,0:T(8,128)(2,1)} %bitcast.237), calls=%async_computation.9 | async-start | bytes 786432 | tf_op jit(solution)/shard_map/all_to_all | solution.py:66
  136.3 1.9 %collective-permute-start.5 = (bf16[4,1,16,384]{3,2,1,0:T(8,128)(2,1)S(1)}, bf16[4,1,16,384]{3,2,1,0:T(8,128)(2,1)S(1)}, u32[]{:S(2)}, u32[]{:S(2)}) collective-permute-start(bf16[4,1,16,384]{3,2,1,0:T(8,128)(2,1)S(1)} %get-tuple-element.129), channel_id=1, source_target_pairs={{4,0},{8,4},{12,8},{16,12},{20,16},{24,20},{28,24},{32,28},{36,32}... | collective-permute-start | bytes 147464 | tf_op jit(solution)/shard_map/ppermute | solution.py:23
  138.2 2.4 %collective-permute-start.4 = (bf16[4,1,16,384]{3,2,1,0:T(8,128)(2,1)S(1)}, bf16[4,1,16,384]{3,2,1,0:T(8,128)(2,1)S(1)}, u32[]{:S(2)}, u32[]{:S(2)}) collective-permute-start(bf16[4,1,16,384]{3,2,1,0:T(8,128)(2,1)S(1)} %get-tuple-element.128), channel_id=1, source_target_pairs={{0,4},{4,8},{8,12},{12,16},{16,20},{20,24},{24,28},{28,32},{32,36}... | collective-permute-start | bytes 147464 | tf_op jit(solution)/shard_map/ppermute | solution.py:20
  140.6 5.1 %collective-permute-done.4 = bf16[4,1,16,384]{3,2,1,0:T(8,128)(2,1)S(1)} collective-permute-done((bf16[4,1,16,384]{3,2,1,0:T(8,128)(2,1)S(1)}, bf16[4,1,16,384]{3,2,1,0:T(8,128)(2,1)S(1)}, u32[]{:S(2)}, u32[]{:S(2)}) %collective-permute-start.4) | collective-permute-done | bytes 49184 | tf_op jit(solution)/shard_map/ppermute | solution.py:20
  145.8 1.1 broadcast_in_dim.5
  146.9 4.9 %all-to-all-start.2 = ((bf16[4,4,6,16,384]{4,3,2,1,0:T(8,128)(2,1)}), bf16[4,4,6,16,384]{4,3,2,1,0:T(8,128)(2,1)S(1)}, u32[]{:S(2)}, u32[]{:S(2)}) async-start(bf16[4,4,6,16,384]{4,3,2,1,0:T(8,128)(2,1)} %broadcast_in_dim.5), calls=%async_computation.2 | async-start | bytes 2359296 | tf_op jit(solution)/shard_map/all_to_all | solution.py:30
  151.9 1.5 copy.55
  153.7 10.9 %all-to-all-done.2 = bf16[4,4,6,16,384]{4,3,2,1,0:T(8,128)(2,1)S(1)} async-done(((bf16[4,4,6,16,384]{4,3,2,1,0:T(8,128)(2,1)}), bf16[4,4,6,16,384]{4,3,2,1,0:T(8,128)(2,1)S(1)}, u32[]{:S(2)}, u32[]{:S(2)}) %all-to-all-start.2) | async-done | bytes 1179680 | tf_op jit(solution)/shard_map/all_to_all | solution.py:30
  164.8 0.8 pad_slice_fusion.17
  166.0 0.8 pad_slice_fusion.16
  167.0 1.4 copy-done.3
  172.3 0.5 convolution_add_fusion.18
  173.6 0.5 fusion.3
  174.2 0.8 copy.38
  175.0 3.3 %all-to-all-start.3 = ((bf16[2,4,64,96]{3,1,0,2:T(4,128)(2,1)}), bf16[2,4,64,96]{3,1,0,2:T(4,128)(2,1)S(1)}, u32[]{:S(2)}, u32[]{:S(2)}) async-start(bf16[2,4,64,96]{3,1,0,2:T(4,128)(2,1)} %copy.38), calls=%async_computation.3 | async-start | bytes 262144 | tf_op jit(solution)/shard_map/all_to_all | solution.py:129
  178.3 5.9 %all-to-all-done.3 = bf16[2,4,64,96]{3,1,0,2:T(4,128)(2,1)S(1)} async-done(((bf16[2,4,64,96]{3,1,0,2:T(4,128)(2,1)}), bf16[2,4,64,96]{3,1,0,2:T(4,128)(2,1)S(1)}, u32[]{:S(2)}, u32[]{:S(2)}) %all-to-all-start.3) | async-done | bytes 98336 | tf_op jit(solution)/shard_map/all_to_all | solution.py:129
  184.6 0.9 fusion.72
  (126 shorter events, 23.3 us)
Async XLA Ops:
  0.6 20.3 %copy-start = (bf16[3,3,3,96,384]{4,3,2,1,0:T(8,128)(2,1)S(1)}, bf16[3,3,3,96,384]{4,3,2,1,0:T(8,128)(2,1)}, u32[]{:S(2)}) copy-start(bf16[3,3,3,96,384]{4,3,2,1,0:T(8,128)(2,1)} %param.10) | copy-start | bytes 5971972
  0.6 9.8 %collective-permute-start.6 = (bf16[2,4,16,384]{3,2,1,0:T(8,128)(2,1)}, bf16[2,4,16,384]{3,2,1,0:T(8,128)(2,1)S(1)}, u32[]{:S(2)}, u32[]{:S(2)}) collective-permute-start(bf16[2,4,16,384]{3,2,1,0:T(8,128)(2,1)} %param.7), channel_id=1, source_target_pairs={{128,0},{256,128},{384,256},{129,1},{257,129},{385,257},{130,2},{2... | collective-permute-start | bytes 294920 | tf_op jit(solution)/shard_map/ppermute | solution.py:12
  4.1 12.5 %collective-permute-start = (bf16[2,4,16,384]{3,2,1,0:T(8,128)(2,1)S(1)}, bf16[2,4,16,384]{3,2,1,0:T(8,128)(2,1)S(1)}, u32[]{:S(2)}, u32[]{:S(2)}) collective-permute-start(bf16[2,4,16,384]{3,2,1,0:T(8,128)(2,1)S(1)} %fusion.63), channel_id=1, source_target_pairs={{0,128},{128,256},{256,384},{1,129},{129,257},{257,385},{2,130},{1... | collective-permute-start | bytes 294920 | tf_op jit(solution)/shard_map/ppermute | solution.py:12
  12.3 12.7 %all-to-all-start.5 = ((bf16[4,4,4,8,96]{4,3,2,1,0:T(8,128)(2,1)}), bf16[4,4,4,8,96]{4,3,2,1,0:T(8,128)(2,1)S(1)}, u32[]{:S(2)}, u32[]{:S(2)}) async-start(bf16[4,4,4,8,96]{4,3,2,1,0:T(8,128)(2,1)} %copy.42), calls=%async_computation.5 | async-start | bytes 262144 | tf_op jit(solution)/shard_map/all_to_all | solution.py:60
  16.6 13.2 %collective-permute-start.2 = (bf16[4,1,16,384]{3,2,1,0:T(8,128)(2,1)S(1)}, bf16[4,1,16,384]{3,2,1,0:T(8,128)(2,1)S(1)}, u32[]{:S(2)}, u32[]{:S(2)}) collective-permute-start(bf16[4,1,16,384]{3,2,1,0:T(8,128)(2,1)S(1)} %get-tuple-element.131), channel_id=1, source_target_pairs={{4,0},{8,4},{12,8},{16,12},{20,16},{24,20},{28,24},{32,28},{36,32}... | collective-permute-start | bytes 147464 | tf_op jit(solution)/shard_map/ppermute | solution.py:23
  18.5 11.3 %collective-permute-start.1 = (bf16[4,1,16,384]{3,2,1,0:T(8,128)(2,1)S(1)}, bf16[4,1,16,384]{3,2,1,0:T(8,128)(2,1)S(1)}, u32[]{:S(2)}, u32[]{:S(2)}) collective-permute-start(bf16[4,1,16,384]{3,2,1,0:T(8,128)(2,1)S(1)} %get-tuple-element.130), channel_id=1, source_target_pairs={{0,4},{4,8},{8,12},{12,16},{16,20},{20,24},{24,28},{28,32},{32,36}... | collective-permute-start | bytes 147464 | tf_op jit(solution)/shard_map/ppermute | solution.py:20
  22.5 1.8 copy-start.9
  25.0 10.8 %all-to-all-start.4 = ((bf16[4,4,4,8,96]{4,3,2,1,0:T(8,128)(2,1)}), bf16[4,4,4,8,96]{4,3,2,1,0:T(8,128)(2,1)S(1)}, u32[]{:S(2)}, u32[]{:S(2)}) async-start(bf16[4,4,4,8,96]{4,3,2,1,0:T(8,128)(2,1)} %copy.41), calls=%async_computation.4 | async-start | bytes 262144 | tf_op jit(solution)/shard_map/all_to_all | solution.py:60
  36.9 21.7 %all-to-all-start = ((bf16[4,4,6,16,384]{4,3,2,1,0:T(8,128)(2,1)}), bf16[4,4,6,16,384]{4,3,2,1,0:T(8,128)(2,1)S(1)}, u32[]{:S(2)}, u32[]{:S(2)}) async-start(bf16[4,4,6,16,384]{4,3,2,1,0:T(8,128)(2,1)} %broadcast_in_dim.4), calls=%async_computation | async-start | bytes 2359296 | tf_op jit(solution)/shard_map/all_to_all | solution.py:30
  40.6 6.0 %collective-permute-start.8 = (bf16[4,1,64,96]{3,2,1,0:T(8,128)(2,1)S(1)}, bf16[4,1,64,96]{3,2,1,0:T(8,128)(2,1)S(1)}, u32[]{:S(2)}, u32[]{:S(2)}) collective-permute-start(bf16[4,1,64,96]{3,2,1,0:T(8,128)(2,1)S(1)} %get-tuple-element.123), channel_id=1, source_target_pairs={{4,0},{8,4},{12,8},{16,12},{20,16},{24,20},{28,24},{32,28},{36,32}... | collective-permute-start | bytes 147464 | tf_op jit(solution)/shard_map/ppermute | solution.py:23
  44.4 7.7 %collective-permute-start.7 = (bf16[4,1,64,96]{3,2,1,0:T(8,128)(2,1)S(1)}, bf16[4,1,64,96]{3,2,1,0:T(8,128)(2,1)S(1)}, u32[]{:S(2)}, u32[]{:S(2)}) collective-permute-start(bf16[4,1,64,96]{3,2,1,0:T(8,128)(2,1)S(1)} %get-tuple-element.122), channel_id=1, source_target_pairs={{0,4},{4,8},{8,12},{12,16},{16,20},{20,24},{24,28},{28,32},{32,36}... | collective-permute-start | bytes 147464 | tf_op jit(solution)/shard_map/ppermute | solution.py:20
  58.6 14.7 %all-to-all-start.6 = ((bf16[4,2,4,16,384]{4,3,2,1,0:T(8,128)(2,1)}), bf16[4,2,4,16,384]{4,3,2,1,0:T(8,128)(2,1)S(1)}, u32[]{:S(2)}, u32[]{:S(2)}) async-start(bf16[4,2,4,16,384]{4,3,2,1,0:T(8,128)(2,1)} %bitcast.238), calls=%async_computation.6 | async-start | bytes 786432 | tf_op jit(solution)/shard_map/all_to_all | solution.py:66
  65.3 1.6 copy-start.2
  73.4 10.8 %all-to-all-start.1 = ((bf16[2,4,64,96]{3,1,0,2:T(4,128)(2,1)}), bf16[2,4,64,96]{3,1,0,2:T(4,128)(2,1)S(1)}, u32[]{:S(2)}, u32[]{:S(2)}) async-start(bf16[2,4,64,96]{3,1,0,2:T(4,128)(2,1)} %copy.32), calls=%async_computation.1 | async-start | bytes 262144 | tf_op jit(solution)/shard_map/all_to_all | solution.py:129
  85.1 8.3 %collective-permute-start.9 = (bf16[2,4,16,384]{3,2,1,0:T(8,128)(2,1)S(1)}, bf16[2,4,16,384]{3,2,1,0:T(8,128)(2,1)S(1)}, u32[]{:S(2)}, u32[]{:S(2)}) collective-permute-start(bf16[2,4,16,384]{3,2,1,0:T(8,128)(2,1)S(1)} %get-tuple-element.126), channel_id=1, source_target_pairs={{128,0},{256,128},{384,256},{129,1},{257,129},{385,257},{130,2},{2... | collective-permute-start | bytes 294920 | tf_op jit(solution)/shard_map/ppermute | solution.py:12
  94.4 9.7 %all-to-all-start.8 = ((bf16[4,4,4,8,96]{4,3,2,1,0:T(8,128)(2,1)}), bf16[4,4,4,8,96]{4,3,2,1,0:T(8,128)(2,1)S(1)}, u32[]{:S(2)}, u32[]{:S(2)}) async-start(bf16[4,4,4,8,96]{4,3,2,1,0:T(8,128)(2,1)} %copy.48), calls=%async_computation.8 | async-start | bytes 262144 | tf_op jit(solution)/shard_map/all_to_all | solution.py:60
  104.1 11.0 %all-to-all-start.7 = ((bf16[4,4,4,8,96]{4,3,2,1,0:T(8,128)(2,1)}), bf16[4,4,4,8,96]{4,3,2,1,0:T(8,128)(2,1)S(1)}, u32[]{:S(2)}, u32[]{:S(2)}) async-start(bf16[4,4,4,8,96]{4,3,2,1,0:T(8,128)(2,1)} %copy.47), calls=%async_computation.7 | async-start | bytes 262144 | tf_op jit(solution)/shard_map/all_to_all | solution.py:60
  109.2 27.0 %collective-permute-start.3 = (bf16[2,4,16,384]{3,2,1,0:T(8,128)(2,1)S(1)}, bf16[2,4,16,384]{3,2,1,0:T(8,128)(2,1)S(1)}, u32[]{:S(2)}, u32[]{:S(2)}) collective-permute-start(bf16[2,4,16,384]{3,2,1,0:T(8,128)(2,1)S(1)} %get-tuple-element.127), channel_id=1, source_target_pairs={{0,128},{128,256},{256,384},{1,129},{129,257},{257,385},{2,130},{1... | collective-permute-start | bytes 294920 | tf_op jit(solution)/shard_map/ppermute | solution.py:12
  115.2 4.6 %collective-permute-start.11 = (bf16[4,1,64,96]{3,2,1,0:T(8,128)(2,1)S(1)}, bf16[4,1,64,96]{3,2,1,0:T(8,128)(2,1)S(1)}, u32[]{:S(2)}, u32[]{:S(2)}) collective-permute-start(bf16[4,1,64,96]{3,2,1,0:T(8,128)(2,1)S(1)} %get-tuple-element.110), channel_id=1, source_target_pairs={{4,0},{8,4},{12,8},{16,12},{20,16},{24,20},{28,24},{32,28},{36,32}... | collective-permute-start | bytes 147464 | tf_op jit(solution)/shard_map/ppermute | solution.py:23
  117.1 7.7 %collective-permute-start.10 = (bf16[4,1,64,96]{3,2,1,0:T(8,128)(2,1)S(1)}, bf16[4,1,64,96]{3,2,1,0:T(8,128)(2,1)S(1)}, u32[]{:S(2)}, u32[]{:S(2)}) collective-permute-start(bf16[4,1,64,96]{3,2,1,0:T(8,128)(2,1)S(1)} %get-tuple-element.109), channel_id=1, source_target_pairs={{0,4},{4,8},{8,12},{12,16},{16,20},{20,24},{24,28},{28,32},{32,36}... | collective-permute-start | bytes 147464 | tf_op jit(solution)/shard_map/ppermute | solution.py:20
  131.5 14.3 %all-to-all-start.9 = ((bf16[4,2,4,16,384]{4,3,2,1,0:T(8,128)(2,1)}), bf16[4,2,4,16,384]{4,3,2,1,0:T(8,128)(2,1)S(1)}, u32[]{:S(2)}, u32[]{:S(2)}) async-start(bf16[4,2,4,16,384]{4,3,2,1,0:T(8,128)(2,1)} %bitcast.237), calls=%async_computation.9 | async-start | bytes 786432 | tf_op jit(solution)/shard_map/all_to_all | solution.py:66
  136.3 4.3 %collective-permute-start.5 = (bf16[4,1,16,384]{3,2,1,0:T(8,128)(2,1)S(1)}, bf16[4,1,16,384]{3,2,1,0:T(8,128)(2,1)S(1)}, u32[]{:S(2)}, u32[]{:S(2)}) collective-permute-start(bf16[4,1,16,384]{3,2,1,0:T(8,128)(2,1)S(1)} %get-tuple-element.129), channel_id=1, source_target_pairs={{4,0},{8,4},{12,8},{16,12},{20,16},{24,20},{28,24},{32,28},{36,32}... | collective-permute-start | bytes 147464 | tf_op jit(solution)/shard_map/ppermute | solution.py:23
  138.2 7.5 %collective-permute-start.4 = (bf16[4,1,16,384]{3,2,1,0:T(8,128)(2,1)S(1)}, bf16[4,1,16,384]{3,2,1,0:T(8,128)(2,1)S(1)}, u32[]{:S(2)}, u32[]{:S(2)}) collective-permute-start(bf16[4,1,16,384]{3,2,1,0:T(8,128)(2,1)S(1)} %get-tuple-element.128), channel_id=1, source_target_pairs={{0,4},{4,8},{8,12},{12,16},{16,20},{20,24},{24,28},{28,32},{32,36}... | collective-permute-start | bytes 147464 | tf_op jit(solution)/shard_map/ppermute | solution.py:20
  145.8 1.1 copy-start.4
  146.9 4.9 %copy-start.1 = (bf16[3,3,3,96,384]{4,3,2,1,0:T(8,128)(2,1)S(1)}, bf16[3,3,3,96,384]{4,3,2,1,0:T(8,128)(2,1)}, u32[]{:S(2)}) copy-start(bf16[3,3,3,96,384]{4,3,2,1,0:T(8,128)(2,1)} %param.11) | copy-start | bytes 5971972
  146.9 17.7 %all-to-all-start.2 = ((bf16[4,4,6,16,384]{4,3,2,1,0:T(8,128)(2,1)}), bf16[4,4,6,16,384]{4,3,2,1,0:T(8,128)(2,1)S(1)}, u32[]{:S(2)}, u32[]{:S(2)}) async-start(bf16[4,4,6,16,384]{4,3,2,1,0:T(8,128)(2,1)} %broadcast_in_dim.5), calls=%async_computation.2 | async-start | bytes 2359296 | tf_op jit(solution)/shard_map/all_to_all | solution.py:30
  151.8 1.5 copy-start.5
  151.9 1.6 copy-start.6
  151.9 1.6 copy-start.8
  166.8 1.6 copy-start.3
  174.1 10.5 %copy-start.7 = (bf16[2,4,16,384]{3,2,1,0:T(8,128)(2,1)S(1)}, bf16[2,4,16,384]{3,2,1,0:T(8,128)(2,1)}, u32[]{:S(2)}) copy-start(bf16[2,4,16,384]{3,2,1,0:T(8,128)(2,1)} %param.7) | copy-start | bytes 294916
  175.0 9.3 %all-to-all-start.3 = ((bf16[2,4,64,96]{3,1,0,2:T(4,128)(2,1)}), bf16[2,4,64,96]{3,1,0,2:T(4,128)(2,1)S(1)}, u32[]{:S(2)}, u32[]{:S(2)}) async-start(bf16[2,4,64,96]{3,1,0,2:T(4,128)(2,1)} %copy.38), calls=%async_computation.3 | async-start | bytes 262144 | tf_op jit(solution)/shard_map/all_to_all | solution.py:129
where the time goes:
time: 187 us; the launch traced here: 185 us
  starting transfers between devices  74.5 us (40%)
  waiting for transfers between devices  57.8 us (31%)
  local copies, waits for them, and re-layouts  24.4 us (13%)
  matrix products  16.2 us (9%)
  other arithmetic  11 us (6%)
    dot_general x36, matrix products, conv_taps(): jnp.dot(columns, kernel[time_tap, row_tap], preferred_element_type=jnp.fl...  16.2 us
    all_to_all x4, starting transfers between devices, several_exchanges(): lax.all_to_all(section, axis, split_axis=0, concat_axis=0, tiled=True)  15.8 us
    ppermute x4, waiting for transfers between devices, extended_2(): lax.ppermute(lax.slice_in_dim(block, block.shape[dim] - width, None, axis...  15.6 us
    ppermute x4, starting transfers between devices, from_behind(): return lax.ppermute(shard, axis, pairs)  14 us
    all_to_all x2, waiting for transfers between devices, forward_conv(): lax.all_to_all(partial_value.astype(jnp.bfloat16), 'exp', split_axis=2, c...  11.7 us
    all_to_all x4, waiting for transfers between devices, several_exchanges(): lax.all_to_all(section, axis, split_axis=0, concat_axis=0, tiled=True)  11.7 us
    all_to_all x2, waiting for transfers between devices, copy_for_each(): return lax.all_to_all(copies, axis, split_axis=0, concat_axis=0, tiled=True)  10.9 us
    ppermute x4, starting transfers between devices, extended_2(): lax.ppermute(lax.slice_in_dim(block, 0, width, axis=dim), axis, backward)  9.58 us
  transfers between devices with their start and end apart: 22, of which 11 were waited for; matrix products, arithmetic and copies ran while one was open for 19% of the time, Pallas kernels for 0%

commit v1 on v0

v1 whole, which is shorter than its diff:
```python
import functools
import jax
import jax.numpy as jnp
from jax import lax
from jax.experimental import pallas as pl
from jax.experimental.pallas import tpu as pltpu
from jax.sharding import PartitionSpec as P

epsilon = 1e-06
F32 = jnp.float32
BF16 = jnp.bfloat16

T, H, W, C, O, X = 2, 4, 16, 384, 96, 4
WT, WH = T + 2, H + 2
COLS = X * W
LANES = 128
DATA = WT * WH
SENT = DATA + WH
BACK = T * H + T


def vmem(count):
    return [pl.BlockSpec(memory_space=pltpu.VMEM)] * count


def call(kernel, out_shape, *operands, scratch=(), scalars=0, flops=0):
    bytes_accessed = sum(a.size * a.dtype.itemsize for a in operands)
    outs = out_shape if isinstance(out_shape, (list, tuple)) else [out_shape]
    bytes_accessed += sum(a.size * a.dtype.itemsize for a in outs)
    smem = [pl.BlockSpec(memory_space=pltpu.SMEM)] * scalars
    return pl.pallas_call(
        kernel,
        out_shape=out_shape,
        in_specs=smem + vmem(len(operands) - scalars),
        out_specs=vmem(len(outs)) if isinstance(out_shape, (list, tuple)) else vmem(1)[0],
        scratch_shapes=list(scratch),
        compiler_params=pltpu.CompilerParams(vmem_limit_bytes=40 * 1024 * 1024),
        cost_estimate=pl.CostEstimate(
            flops=flops, bytes_accessed=bytes_accessed, transcendentals=0
        ),
    )(*operands)


def sigmoid(values):
    return 1.0 / (1.0 + jnp.exp(-values))


def normalize(values, gain):
    inverse = lax.rsqrt(jnp.mean(values * values, axis=-1, keepdims=True) + epsilon)
    return values * inverse * gain, inverse


def norm_backward(values, inverse, gain, upstream):
    scaled = upstream * gain
    return inverse * scaled - values * inverse**3 * jnp.mean(
        values * scaled, axis=-1, keepdims=True
    )


def silu_slope(normed):
    sigma = sigmoid(normed)
    return sigma * (1.0 + normed * (1.0 - sigma))


def put_data(out, frame, row, block):
    for target in range(X):
        out[target, frame * WH + row] = block


def put_slices(out, row, blocks):
    for target in range(X):
        out[target, DATA + row] = jnp.concatenate(
            [block[:, target * O : (target + 1) * O] for block in blocks], axis=-1
        )


def pack_one_kernel(gain, own, before, lat_row, lat_corner, cot, cot_after, cot_row, cot_corner, out):
    scale = gain[...]

    def active(block):
        normed, _ = normalize(block.astype(F32), scale)
        return (normed * sigmoid(normed)).astype(BF16)

    for frame in range(T):
        for row in range(H):
            put_data(out, frame, row, active(before[frame, row]))
            put_data(out, T + frame, row, active(own[frame, row]))
        for row in range(2):
            put_data(out, frame, H + row, active(lat_corner[frame, row]))
            put_data(out, T + frame, H + row, active(lat_row[frame, row]))
    for row in range(H):
        put_slices(out, row, [cot[0, row], cot[1, row], cot_after[0, row], cot_after[1, row]])
    for row in range(2):
        put_slices(
            out,
            H + row,
            [cot_row[0, row], cot_row[1, row], cot_corner[0, row], cot_corner[1, row]],
        )


def pack_two_kernel(own, before, act_row, act_corner, grad, grad_after, grad_row, grad_corner, out):
    for frame in range(T):
        for row in range(2):
            put_data(out, frame, row, act_corner[frame, row])
            put_data(out, T + frame, row, act_row[frame, row])
        for row in range(H):
            put_data(out, frame, 2 + row, before[frame, row])
            put_data(out, T + frame, 2 + row, own[frame, row])
    for row in range(2):
        put_slices(
            out,
            row,
            [grad_row[0, row], grad_row[1, row], grad_corner[0, row], grad_corner[1, row]],
        )
    for row in range(H):
        put_slices(
            out, 2 + row, [grad[0, row], grad[1, row], grad_after[0, row], grad_after[1, row]]
        )


def shifted_sum(parts):
    size = parts[0].shape[0]
    column = lax.broadcasted_iota(jnp.int32, (size, 1), 0) % COLS
    low = jnp.where(column == 0, 0.0, pltpu.roll(parts[0], 1, 0))
    high = jnp.where(column == COLS - 1, 0.0, pltpu.roll(parts[2], size - 1, 0))
    return low + parts[1] + high


def conv_kernel(flags, got, ahead_weight, back_weight, out, data, grads):
    taps = (
        ((0, 0), (1, None), (2, None), (3, 1)),
        ((1, None), (2, None), (3, None), (4, None)),
        ((2, None), (3, None), (4, 2), (5, 3)),
    )
    zeros = jnp.zeros((W, LANES - O), BF16)
    for tap, reads in enumerate(taps):
        for row, (source, flag) in enumerate(reads):
            for part in range(X):
                place = slice(row * COLS + part * W, row * COLS + (part + 1) * W)
                for frame in range(WT):
                    block = got[part, frame * WH + source]
                    if flag is not None:
                        block = block * flags[flag].astype(BF16)
                    data[frame, place, tap * C : (tap + 1) * C] = block
                block = got[part, DATA + source]
                if flag is not None:
                    block = block * flags[flag].astype(BF16)
                for frame in range(WT):
                    piece = jnp.concatenate([block[:, frame * O : (frame + 1) * O], zeros], axis=-1)
                    grads[frame, place, tap * LANES : (tap + 1) * LANES] = piece
    size = T * H * COLS
    total = jnp.zeros((size, 3 * O), F32)
    for time_tap in range(3):
        total = total + lax.dot_general(
            data[time_tap : time_tap + T].reshape(size, 3 * C),
            jnp.concatenate(
                [ahead_weight[time_tap, tap].reshape(3 * O, C) for tap in range(3)], axis=-1
            ),
            (((1,), (1,)), ((), ())),
            preferred_element_type=F32,
        )
    result = shifted_sum([total[:, tap * O : (tap + 1) * O] for tap in range(3)])
    result = result.astype(BF16)
    for frame in range(T):
        for target in range(X):
            start = [(frame * H + row) * COLS + target * W for row in range(H)]
            out[target, T * H + frame] = jnp.concatenate(
                [result[at : at + W] for at in start], axis=-1
            )
    total = jnp.zeros((size, 3 * C), F32)
    for time_tap in range(3):
        total = total + jnp.dot(
            grads[time_tap : time_tap + T].reshape(size, 3 * LANES),
            back_weight[time_tap],
            preferred_element_type=F32,
        )
    result = shifted_sum([total[:, tap * C : (tap + 1) * C] for tap in range(3)]).astype(BF16)
    for block in range(T * H):
        for target in range(X):
            at = block * COLS + target * W
            out[target, block] = result[at : at + W]


def arrived_grad(got, block):
    total = got[0, block].astype(F32)
    for source in range(1, X):
        total = total + got[source, block].astype(F32)
    return total


def arrived_conv(got, frame, row):
    return jnp.concatenate(
        [got[source, T * H + frame, :, row * O : (row + 1) * O] for source in range(X)], axis=-1
    ).astype(F32)


def middle_kernel(gain, got, active, grad_inner):
    scale = gain[...]
    for frame in range(T):
        for row in range(H):
            inner = arrived_conv(got, frame, row)
            grad_two = arrived_grad(got, frame * H + row)
            normed, inverse = normalize(inner, scale)
            active[frame, row] = (normed * sigmoid(normed)).astype(BF16)
            grad_inner[frame, row] = norm_backward(
                inner, inverse, scale, grad_two * silu_slope(normed)
            ).astype(BF16)


def last_kernel(gain, latent, cotangent, got, block_out, latent_grad):
    scale = gain[...]
    for frame in range(T):
        for row in range(H):
            source = latent[frame, row].astype(F32)
            block_out[frame, row] = (source + arrived_conv(got, frame, row)).astype(BF16)
            normed, inverse = normalize(source, scale)
            grad_one = arrived_grad(got, frame * H + row)
            latent_grad[frame, row] = (
                cotangent[frame, row].astype(F32)
                + norm_backward(source, inverse, scale, grad_one * silu_slope(normed))
            ).astype(BF16)


def shift(values, frames, rows):
    sections, ring = lax.axis_size("section"), lax.axis_size("seq")
    pairs = [
        (s * ring + q, (s + frames) * ring + (q + rows) % ring)
        for s in range(sections)
        for q in range(ring)
        if 0 <= s + frames < sections
    ]
    return lax.ppermute(values, ("section", "seq"), pairs)


def exchange(values):
    return lax.all_to_all(values, "exp", split_axis=0, concat_axis=0, tiled=True)


def back_weight_kernel(weight, out):
    zeros = jnp.zeros((LANES - O, 3 * C), BF16)
    for time_tap in range(3):
        for row_tap in range(3):
            start = row_tap * LANES
            for tap in range(3):
                out[time_tap, start : start + O, tap * C : (tap + 1) * C] = weight[
                    2 - time_tap, 2 - row_tap, 2 - tap
                ]
            out[time_tap, start + O : start + LANES] = zeros


def back_kernel(weight):
    shape = jax.ShapeDtypeStruct((3, 3 * LANES, 3 * C), BF16)
    return call(back_weight_kernel, shape, weight)


def convs(flags, got, ahead_weight, back_weight):
    size = T * H * COLS
    return call(
        conv_kernel,
        jax.ShapeDtypeStruct((X, BACK, W, C), BF16),
        flags,
        got,
        ahead_weight,
        back_weight,
        scratch=(
            pltpu.VMEM((WT, H * COLS, 3 * C), BF16),
            pltpu.VMEM((WT, H * COLS, 3 * LANES), BF16),
        ),
        scalars=1,
        flops=2 * size * 27 * 2 * C * LANES,
    )


def body(latent, cotangent, gain_one, gain_two, kernel_one, kernel_two):
    gain_one, gain_two = gain_one.reshape(1, C), gain_two.reshape(1, C)
    place, last = lax.axis_index("seq"), lax.axis_size("seq") - 1
    one = jnp.ones((), F32)
    not_first, not_last = (place != 0).astype(F32), (place != last).astype(F32)
    flags_one = jnp.stack([one, not_last, not_last, one])
    flags_two = jnp.stack([not_first, one, one, not_last])
    block = jax.ShapeDtypeStruct((T, H, W, C), BF16)
    sent = jax.ShapeDtypeStruct((X, SENT, W, C), BF16)

    before = shift(latent, 1, 0)
    after = shift(cotangent, -1, 0)
    rows = shift(jnp.stack([latent[:, :2], cotangent[:, :2]]), 0, -1)
    lat_corner = shift(latent[:, :2], 1, -1)
    cot_corner = shift(cotangent[:, :2], -1, -1)
    packed = call(
        pack_one_kernel,
        sent,
        gain_one,
        latent,
        before,
        rows[0],
        lat_corner,
        cotangent,
        after,
        rows[1],
        cot_corner,
    )
    got = exchange(packed)
    summed = convs(flags_one, got, kernel_one, back_kernel(kernel_two))
    got = exchange(summed)
    active, grad_inner = call(middle_kernel, [block, block], gain_two, got)

    before = shift(active, 1, 0)
    after = shift(grad_inner, -1, 0)
    rows = shift(jnp.stack([active[:, 2:], grad_inner[:, 2:]]), 0, 1)
    act_corner = shift(active[:, 2:], 1, 1)
    grad_corner = shift(grad_inner[:, 2:], -1, 1)
    packed = call(
        pack_two_kernel,
        sent,
        active,
        before,
        rows[0],
        act_corner,
        grad_inner,
        after,
        rows[1],
        grad_corner,
    )
    got = exchange(packed)
    summed = convs(flags_two, got, kernel_two, back_kernel(kernel_one))
    got = exchange(summed)
    return tuple(call(last_kernel, [block, block], gain_one, latent, cotangent, got))


def solution(mesh):
    in_specs = (
        P("section", "seq", "exp", None),
        P("section", "seq", "exp", None),
        P(),
        P(),
        P(None, None, None, "exp", None),
        P(None, None, None, "exp", None),
    )
    out_specs = (P("section", "seq", "exp", None), P("section", "seq", "exp", None))
    return jax.shard_map(body, mesh=mesh, in_specs=in_specs, out_specs=out_specs, check_vma=False)
```

time: 187 us -> 146 us (0.78)
  the two profiles are of different devices: /device:TPU:256 before, /device:TPU:16 now
where the time goes in v1:
time: 146 us; the launch traced here: 145 us
  waiting for transfers between devices  56.2 us (38%)
  starting transfers between devices  50.3 us (34%)
  Pallas kernels  16.4 us (11%)
  local copies, waits for them, and re-layouts  10.4 us (7%)
  blocking collectives  10.3 us (7%)
    all_to_all x3, waiting for transfers between devices, exchange(): lax.all_to_all(values, 'exp', split_axis=0, concat_axis=0, tiled=True)  42.7 us
    ppermute x10, starting transfers between devices, shift(): return lax.ppermute(values, ('section', 'seq'), pairs)  38.1 us
    pallas_call x8, Pallas kernels, call(): pl.pallas_call(kernel, out_shape=out_shape, in_specs=smem + vmem(len(oper...  16.4 us
    ppermute x10, waiting for transfers between devices, shift(): return lax.ppermute(values, ('section', 'seq'), pairs)  13.5 us
    all_to_all x3, starting transfers between devices, exchange(): lax.all_to_all(values, 'exp', split_axis=0, concat_axis=0, tiled=True)  12.2 us
    all_to_all x1, blocking collectives, exchange(): lax.all_to_all(values, 'exp', split_axis=0, concat_axis=0, tiled=True)  10.3 us
    unnamed x18, local copies, waits for them, and re-layouts  8 us
  transfers between devices with their start and end apart: 13, of which 6 were waited for; matrix products, arithmetic and copies ran while one was open for 1% of the time, Pallas kernels for 0%

profile of v1, /device:TPU:16, one launch (start us, length us, event | category | flops | bytes accessed | tf_op | source)
XLA Modules:
  0.0 144.6 jit_solution(10555531428830274109)
XLA Ops:
  0.6 0.8 fusion.2
  1.4 0.8 fusion.3
  2.3 11.4 %collective-permute-start.1 = (bf16[2,2,2,16,384]{4,3,2,1,0:T(8,128)(2,1)S(1)}, bf16[2,2,2,16,384]{4,3,2,1,0:T(8,128)(2,1)S(1)}, u32[]{:S(2)}, u32[]{:S(2)}) collective-permute-start(bf16[2,2,2,16,384]{4,3,2,1,0:T(8,128)(2,1)S(1)} %pad_maximum_fusion), channel_id=1, source_target_pairs={{0,124},{4,0},{8,4},{12,8},{16,12},{20,16},{24,20},{28,24},{32,28}... | collective-permute-start | bytes 294920 | tf_op jit(solution)/shard_map/ppermute | solution.py:232
  13.7 4.8 %collective-permute-start = (bf16[2,4,16,384]{3,2,1,0:T(8,128)(2,1)}, bf16[2,4,16,384]{3,2,1,0:T(8,128)(2,1)S(1)}, u32[]{:S(2)}, u32[]{:S(2)}) collective-permute-start(bf16[2,4,16,384]{3,2,1,0:T(8,128)(2,1)} %latent.1), channel_id=1, source_target_pairs={{0,128},{4,132},{8,136},{12,140},{16,144},{20,148},{24,152},{28,15... | collective-permute-start | bytes 294920 | tf_op jit(solution)/shard_map/ppermute | solution.py:232
  18.5 1.9 %collective-permute-start.3 = (bf16[2,4,16,384]{3,2,1,0:T(8,128)(2,1)}, bf16[2,4,16,384]{3,2,1,0:T(8,128)(2,1)S(1)}, u32[]{:S(2)}, u32[]{:S(2)}) collective-permute-start(bf16[2,4,16,384]{3,2,1,0:T(8,128)(2,1)} %cotangent.1), channel_id=1, source_target_pairs={{128,0},{132,4},{136,8},{140,12},{144,16},{148,20},{152,24},{156,2... | collective-permute-start | bytes 294920 | tf_op jit(solution)/shard_map/ppermute | solution.py:232
  20.5 5.6 %collective-permute-start.2 = (bf16[2,2,16,384]{3,2,1,0:T(8,128)(2,1)S(1)}, bf16[2,2,16,384]{3,2,1,0:T(8,128)(2,1)S(1)}, u32[]{:S(2)}, u32[]{:S(2)}) collective-permute-start(bf16[2,2,16,384]{3,2,1,0:T(8,128)(2,1)S(1)} %get-tuple-element.16), channel_id=1, source_target_pairs={{0,252},{4,128},{8,132},{12,136},{16,140},{20,144},{24,148},{28,15... | collective-permute-start | bytes 147464 | tf_op jit(solution)/shard_map/ppermute | solution.py:232
  26.0 1.9 %collective-permute-start.4 = (bf16[2,2,16,384]{3,2,1,0:T(8,128)(2,1)S(1)}, bf16[2,2,16,384]{3,2,1,0:T(8,128)(2,1)S(1)}, u32[]{:S(2)}, u32[]{:S(2)}) collective-permute-start(bf16[2,2,16,384]{3,2,1,0:T(8,128)(2,1)S(1)} %get-tuple-element.12), channel_id=1, source_target_pairs={{128,124},{132,0},{136,4},{140,8},{144,12},{148,16},{152,20},{156,... | collective-permute-start | bytes 147464 | tf_op jit(solution)/shard_map/ppermute | solution.py:232
  28.0 0.7 reshape.10.gain
  28.6 0.0 collective-permute-done.1
  28.7 0.0 collective-permute-done.2.lat_corner
  28.7 4.9 %collective-permute-done.4.cot_corner = bf16[2,2,16,384]{3,2,1,0:T(8,128)(2,1)S(1)} collective-permute-done((bf16[2,2,16,384]{3,2,1,0:T(8,128)(2,1)S(1)}, bf16[2,2,16,384]{3,2,1,0:T(8,128)(2,1)S(1)}, u32[]{:S(2)}, u32[]{:S(2)}) %collective-permute-start.4) | collective-permute-done | bytes 49184 | tf_op jit(solution)/shard_map/ppermute | solution.py:232
  33.6 0.0 collective-permute-done.before
  33.6 0.0 collective-permute-done.3.cot_after
  33.6 0.0 copy-start.4
  33.6 0.9 copy-done.4
  34.5 0.0 copy-start.6
  34.5 0.9 copy-done.6
  35.3 1.4 shard_map.77
  36.8 4.3 %all-to-all-start = ((bf16[4,30,16,384]{3,2,1,0:T(8,128)(2,1)}), bf16[4,30,16,384]{3,2,1,0:T(8,128)(2,1)}, u32[]{:S(2)}, u32[]{:S(2)}) async-start(bf16[4,30,16,384]{3,2,1,0:T(8,128)(2,1)} %shard_map.77), calls=%async_computation | async-start | bytes 2949120 | tf_op jit(solution)/shard_map/all_to_all | solution.py:236
  41.1 0.0 copy-start.2
  41.2 1.5 %copy-done.2 = bf16[3,3,3,96,384]{4,3,2,1,0:T(8,128)(2,1)S(1)} copy-done((bf16[3,3,3,96,384]{4,3,2,1,0:T(8,128)(2,1)S(1)}, bf16[3,3,3,96,384]{4,3,2,1,0:T(8,128)(2,1)}, u32[]{:S(2)}) %copy-start.2) | copy-done | bytes 1990680
  42.7 0.2 shard_map.78.back_weight
  42.9 0.1 pad_maximum_fusion.3.flags
  43.0 18.8 %all-to-all-done.got = bf16[4,30,16,384]{3,2,1,0:T(8,128)(2,1)} async-done(((bf16[4,30,16,384]{3,2,1,0:T(8,128)(2,1)}), bf16[4,30,16,384]{3,2,1,0:T(8,128)(2,1)}, u32[]{:S(2)}, u32[]{:S(2)}) %all-to-all-start) | async-done | bytes 1474592 | tf_op jit(solution)/shard_map/all_to_all | solution.py:236
  61.9 0.0 copy-start
  61.9 1.6 %copy-done = bf16[3,3,3,96,384]{4,3,2,1,0:T(8,128)(2,1)S(1)} copy-done((bf16[3,3,3,96,384]{4,3,2,1,0:T(8,128)(2,1)S(1)}, bf16[3,3,3,96,384]{4,3,2,1,0:T(8,128)(2,1)}, u32[]{:S(2)}) %copy-start) | copy-done | bytes 1990680
  63.4 0.0 copy-start.8
  63.4 6.3 %shard_map.79 = bf16[4,10,16,384]{3,2,1,0:T(8,128)(2,1)} custom-call(f32[4]{0:T(128)S(1)} %pad_maximum_fusion.3.flags, bf16[4,30,16,384]{3,2,1,0:T(8,128)(2,1)} %all-to-all-done.got, bf16[3,3,3,96,384]{4,3,2,1,0:T(8,128)(2,1)S(1)} %copy-done, bf16[3,384,1152]{2,1,0:T(8,128)(2,1)S(1)} %shard_map.78.back_weight), custom_call_target="tpu_custom_call" | custom-call | flops 2717908992 | bytes 6610960 | tf_op jit(solution)/shard_map/pallas_call | solution.py:31
  69.7 3.5 %all-to-all-start.1 = ((bf16[4,10,16,384]{3,2,1,0:T(8,128)(2,1)}), bf16[4,10,16,384]{3,2,1,0:T(8,128)(2,1)S(1)}, u32[]{:S(2)}, u32[]{:S(2)}) async-start(bf16[4,10,16,384]{3,2,1,0:T(8,128)(2,1)} %shard_map.79), calls=%async_computation.1 | async-start | bytes 983040 | tf_op jit(solution)/shard_map/all_to_all | solution.py:236
  73.1 0.0 copy-done.8
  73.2 9.8 %all-to-all-done.1.got = bf16[4,10,16,384]{3,2,1,0:T(8,128)(2,1)S(1)} async-done(((bf16[4,10,16,384]{3,2,1,0:T(8,128)(2,1)}), bf16[4,10,16,384]{3,2,1,0:T(8,128)(2,1)S(1)}, u32[]{:S(2)}, u32[]{:S(2)}) %all-to-all-start.1) | async-done | bytes 491552 | tf_op jit(solution)/shard_map/all_to_all | solution.py:236
  82.9 0.4 shard_map.80
  83.4 1.9 %collective-permute-start.6 = (bf16[2,2,2,16,384]{4,3,2,1,0:T(8,128)(2,1)S(1)}, bf16[2,2,2,16,384]{4,3,2,1,0:T(8,128)(2,1)S(1)}, u32[]{:S(2)}, u32[]{:S(2)}) collective-permute-start(bf16[2,2,2,16,384]{4,3,2,1,0:T(8,128)(2,1)S(1)} %pad_maximum_fusion.1), channel_id=1, source_target_pairs={{0,4},{4,8},{8,12},{12,16},{16,20},{20,24},{24,28},{28,32},{32,36}... | collective-permute-start | bytes 294920 | tf_op jit(solution)/shard_map/ppermute | solution.py:232
  85.3 1.9 %collective-permute-start.5 = (bf16[2,4,16,384]{3,2,1,0:T(8,128)(2,1)S(1)}, bf16[2,4,16,384]{3,2,1,0:T(8,128)(2,1)S(1)}, u32[]{:S(2)}, u32[]{:S(2)}) collective-permute-start(bf16[2,4,16,384]{3,2,1,0:T(8,128)(2,1)S(1)} %get-tuple-element.4.own), channel_id=1, source_target_pairs={{0,128},{4,132},{8,136},{12,140},{16,144},{20,148},{24,152},{28,15... | collective-permute-start | bytes 294920 | tf_op jit(solution)/shard_map/ppermute | solution.py:232
  87.2 4.8 %collective-permute-start.8 = (bf16[2,4,16,384]{3,2,1,0:T(8,128)(2,1)S(1)}, bf16[2,4,16,384]{3,2,1,0:T(8,128)(2,1)S(1)}, u32[]{:S(2)}, u32[]{:S(2)}) collective-permute-start(bf16[2,4,16,384]{3,2,1,0:T(8,128)(2,1)S(1)} %get-tuple-element.5.grad), channel_id=1, source_target_pairs={{128,0},{132,4},{136,8},{140,12},{144,16},{148,20},{152,24},{156,2... | collective-permute-start | bytes 294920 | tf_op jit(solution)/shard_map/ppermute | solution.py:232
  92.1 1.9 %collective-permute-start.7 = (bf16[2,2,16,384]{3,2,1,0:T(8,128)(2,1)S(1)}, bf16[2,2,16,384]{3,2,1,0:T(8,128)(2,1)S(1)}, u32[]{:S(2)}, u32[]{:S(2)}) collective-permute-start(bf16[2,2,16,384]{3,2,1,0:T(8,128)(2,1)S(1)} %get-tuple-element.10), channel_id=1, source_target_pairs={{0,132},{4,136},{8,140},{12,144},{16,148},{20,152},{24,156},{28,16... | collective-permute-start | bytes 147464 | tf_op jit(solution)/shard_map/ppermute | solution.py:232
  94.0 1.9 %collective-permute-start.9 = (bf16[2,2,16,384]{3,2,1,0:T(8,128)(2,1)S(1)}, bf16[2,2,16,384]{3,2,1,0:T(8,128)(2,1)S(1)}, u32[]{:S(2)}, u32[]{:S(2)}) collective-permute-start(bf16[2,2,16,384]{3,2,1,0:T(8,128)(2,1)S(1)} %get-tuple-element.6), channel_id=1, source_target_pairs={{128,4},{132,8},{136,12},{140,16},{144,20},{148,24},{152,28},{156,... | collective-permute-start | bytes 147464 | tf_op jit(solution)/shard_map/ppermute | solution.py:232
  95.9 0.0 collective-permute-done.6
  96.0 3.6 %collective-permute-done.7.act_corner = bf16[2,2,16,384]{3,2,1,0:T(8,128)(2,1)S(1)} collective-permute-done((bf16[2,2,16,384]{3,2,1,0:T(8,128)(2,1)S(1)}, bf16[2,2,16,384]{3,2,1,0:T(8,128)(2,1)S(1)}, u32[]{:S(2)}, u32[]{:S(2)}) %collective-permute-start.7) | collective-permute-done | bytes 49184 | tf_op jit(solution)/shard_map/ppermute | solution.py:232
  99.6 5.0 %collective-permute-done.9.grad_corner = bf16[2,2,16,384]{3,2,1,0:T(8,128)(2,1)S(1)} collective-permute-done((bf16[2,2,16,384]{3,2,1,0:T(8,128)(2,1)S(1)}, bf16[2,2,16,384]{3,2,1,0:T(8,128)(2,1)S(1)}, u32[]{:S(2)}, u32[]{:S(2)}) %collective-permute-start.9) | collective-permute-done | bytes 49184 | tf_op jit(solution)/shard_map/ppermute | solution.py:232
  104.5 0.0 collective-permute-done.5.before
  104.5 0.0 collective-permute-done.8.grad_after
  104.5 1.3 shard_map.81
  105.9 4.3 %all-to-all-start.2 = ((bf16[4,30,16,384]{3,2,1,0:T(8,128)(2,1)}), bf16[4,30,16,384]{3,2,1,0:T(8,128)(2,1)}, u32[]{:S(2)}, u32[]{:S(2)}) async-start(bf16[4,30,16,384]{3,2,1,0:T(8,128)(2,1)} %shard_map.81), calls=%async_computation.2 | async-start | bytes 2949120 | tf_op jit(solution)/shard_map/all_to_all | solution.py:236
  110.2 0.0 copy-start.1
  110.2 1.5 %copy-done.1 = bf16[3,3,3,96,384]{4,3,2,1,0:T(8,128)(2,1)S(1)} copy-done((bf16[3,3,3,96,384]{4,3,2,1,0:T(8,128)(2,1)S(1)}, bf16[3,3,3,96,384]{4,3,2,1,0:T(8,128)(2,1)}, u32[]{:S(2)}) %copy-start.1) | copy-done | bytes 1990680
  111.8 0.2 shard_map.82.back_weight
  112.0 0.1 pad_maximum_fusion.2.flags
  112.1 14.1 %all-to-all-done.2.got = bf16[4,30,16,384]{3,2,1,0:T(8,128)(2,1)} async-done(((bf16[4,30,16,384]{3,2,1,0:T(8,128)(2,1)}), bf16[4,30,16,384]{3,2,1,0:T(8,128)(2,1)}, u32[]{:S(2)}, u32[]{:S(2)}) %all-to-all-start.2) | async-done | bytes 1474592 | tf_op jit(solution)/shard_map/all_to_all | solution.py:236
  126.2 0.0 copy-start.3
  126.2 1.6 %copy-done.3 = bf16[3,3,3,96,384]{4,3,2,1,0:T(8,128)(2,1)S(1)} copy-done((bf16[3,3,3,96,384]{4,3,2,1,0:T(8,128)(2,1)S(1)}, bf16[3,3,3,96,384]{4,3,2,1,0:T(8,128)(2,1)}, u32[]{:S(2)}) %copy-start.3) | copy-done | bytes 1990680
  127.8 0.0 copy-start.5
  127.8 0.0 copy-start.7
  127.8 5.5 %shard_map.83 = bf16[4,10,16,384]{3,2,1,0:T(8,128)(2,1)S(1)} custom-call(f32[4]{0:T(128)S(1)} %pad_maximum_fusion.2.flags, bf16[4,30,16,384]{3,2,1,0:T(8,128)(2,1)} %all-to-all-done.2.got, bf16[3,3,3,96,384]{4,3,2,1,0:T(8,128)(2,1)S(1)} %copy-done.3, bf16[3,384,1152]{2,1,0:T(8,128)(2,1)S(1)} %shard_map.82.back_weight), custom_call_target="tpu_custom_call" | custom-call | flops 2717908992 | bytes 6610960 | tf_op jit(solution)/shard_map/pallas_call | solution.py:31
  133.3 10.3 %all_to_all.20.got = bf16[4,10,16,384]{3,2,1,0:T(8,128)(2,1)S(1)} all-to-all(bf16[4,10,16,384]{3,2,1,0:T(8,128)(2,1)S(1)} %shard_map.83), channel_id=1, replica_groups=mesh['section'=4,'seq'=32,'exp'=4] {'exp'}, dimensions={0} | all-to-all | bytes 983040 | tf_op jit(solution)/shard_map/all_to_all | solution.py:236
  143.6 0.0 copy-done.5
  143.6 0.0 copy-done.7
  143.6 1.1 shard_map.84
  (8 shorter events, 0.1 us)
Async XLA Ops:
  2.3 26.4 %collective-permute-start.1 = (bf16[2,2,2,16,384]{4,3,2,1,0:T(8,128)(2,1)S(1)}, bf16[2,2,2,16,384]{4,3,2,1,0:T(8,128)(2,1)S(1)}, u32[]{:S(2)}, u32[]{:S(2)}) collective-permute-start(bf16[2,2,2,16,384]{4,3,2,1,0:T(8,128)(2,1)S(1)} %pad_maximum_fusion), channel_id=1, source_target_pairs={{0,124},{4,0},{8,4},{12,8},{16,12},{20,16},{24,20},{28,24},{32,28}... | collective-permute-start | bytes 294920 | tf_op jit(solution)/shard_map/ppermute | solution.py:232
  13.7 19.9 %collective-permute-start = (bf16[2,4,16,384]{3,2,1,0:T(8,128)(2,1)}, bf16[2,4,16,384]{3,2,1,0:T(8,128)(2,1)S(1)}, u32[]{:S(2)}, u32[]{:S(2)}) collective-permute-start(bf16[2,4,16,384]{3,2,1,0:T(8,128)(2,1)} %latent.1), channel_id=1, source_target_pairs={{0,128},{4,132},{8,136},{12,140},{16,144},{20,148},{24,152},{28,15... | collective-permute-start | bytes 294920 | tf_op jit(solution)/shard_map/ppermute | solution.py:232
  18.5 15.0 %collective-permute-start.3 = (bf16[2,4,16,384]{3,2,1,0:T(8,128)(2,1)}, bf16[2,4,16,384]{3,2,1,0:T(8,128)(2,1)S(1)}, u32[]{:S(2)}, u32[]{:S(2)}) collective-permute-start(bf16[2,4,16,384]{3,2,1,0:T(8,128)(2,1)} %cotangent.1), channel_id=1, source_target_pairs={{128,0},{132,4},{136,8},{140,12},{144,16},{148,20},{152,24},{156,2... | collective-permute-start | bytes 294920 | tf_op jit(solution)/shard_map/ppermute | solution.py:232
  20.5 8.2 %collective-permute-start.2 = (bf16[2,2,16,384]{3,2,1,0:T(8,128)(2,1)S(1)}, bf16[2,2,16,384]{3,2,1,0:T(8,128)(2,1)S(1)}, u32[]{:S(2)}, u32[]{:S(2)}) collective-permute-start(bf16[2,2,16,384]{3,2,1,0:T(8,128)(2,1)S(1)} %get-tuple-element.16), channel_id=1, source_target_pairs={{0,252},{4,128},{8,132},{12,136},{16,140},{20,144},{24,148},{28,15... | collective-permute-start | bytes 147464 | tf_op jit(solution)/shard_map/ppermute | solution.py:232
  26.0 7.5 %collective-permute-start.4 = (bf16[2,2,16,384]{3,2,1,0:T(8,128)(2,1)S(1)}, bf16[2,2,16,384]{3,2,1,0:T(8,128)(2,1)S(1)}, u32[]{:S(2)}, u32[]{:S(2)}) collective-permute-start(bf16[2,2,16,384]{3,2,1,0:T(8,128)(2,1)S(1)} %get-tuple-element.12), channel_id=1, source_target_pairs={{128,124},{132,0},{136,4},{140,8},{144,12},{148,16},{152,20},{156,... | collective-permute-start | bytes 147464 | tf_op jit(solution)/shard_map/ppermute | solution.py:232
  33.6 0.9 copy-start.4
  34.5 0.9 copy-start.6
  36.8 25.1 %all-to-all-start = ((bf16[4,30,16,384]{3,2,1,0:T(8,128)(2,1)}), bf16[4,30,16,384]{3,2,1,0:T(8,128)(2,1)}, u32[]{:S(2)}, u32[]{:S(2)}) async-start(bf16[4,30,16,384]{3,2,1,0:T(8,128)(2,1)} %shard_map.77), calls=%async_computation | async-start | bytes 2949120 | tf_op jit(solution)/shard_map/all_to_all | solution.py:236
  41.1 1.6 %copy-start.2 = (bf16[3,3,3,96,384]{4,3,2,1,0:T(8,128)(2,1)S(1)}, bf16[3,3,3,96,384]{4,3,2,1,0:T(8,128)(2,1)}, u32[]{:S(2)}) copy-start(bf16[3,3,3,96,384]{4,3,2,1,0:T(8,128)(2,1)} %ahead_weight.3) | copy-start | bytes 5971972
  61.9 1.6 %copy-start = (bf16[3,3,3,96,384]{4,3,2,1,0:T(8,128)(2,1)S(1)}, bf16[3,3,3,96,384]{4,3,2,1,0:T(8,128)(2,1)}, u32[]{:S(2)}) copy-start(bf16[3,3,3,96,384]{4,3,2,1,0:T(8,128)(2,1)} %weight.3) | copy-start | bytes 5971972
  63.4 9.7 %copy-start.8 = (f32[384]{0:T(512)S(1)}, f32[384]{0:T(512)}, u32[]{:S(2)}) copy-start(f32[384]{0:T(512)} %param.9) | copy-start | bytes 4612
  69.7 13.3 %all-to-all-start.1 = ((bf16[4,10,16,384]{3,2,1,0:T(8,128)(2,1)}), bf16[4,10,16,384]{3,2,1,0:T(8,128)(2,1)S(1)}, u32[]{:S(2)}, u32[]{:S(2)}) async-start(bf16[4,10,16,384]{3,2,1,0:T(8,128)(2,1)} %shard_map.79), calls=%async_computation.1 | async-start | bytes 983040 | tf_op jit(solution)/shard_map/all_to_all | solution.py:236
  83.4 12.5 %collective-permute-start.6 = (bf16[2,2,2,16,384]{4,3,2,1,0:T(8,128)(2,1)S(1)}, bf16[2,2,2,16,384]{4,3,2,1,0:T(8,128)(2,1)S(1)}, u32[]{:S(2)}, u32[]{:S(2)}) collective-permute-start(bf16[2,2,2,16,384]{4,3,2,1,0:T(8,128)(2,1)S(1)} %pad_maximum_fusion.1), channel_id=1, source_target_pairs={{0,4},{4,8},{8,12},{12,16},{16,20},{20,24},{24,28},{28,32},{32,36}... | collective-permute-start | bytes 294920 | tf_op jit(solution)/shard_map/ppermute | solution.py:232
  85.3 19.2 %collective-permute-start.5 = (bf16[2,4,16,384]{3,2,1,0:T(8,128)(2,1)S(1)}, bf16[2,4,16,384]{3,2,1,0:T(8,128)(2,1)S(1)}, u32[]{:S(2)}, u32[]{:S(2)}) collective-permute-start(bf16[2,4,16,384]{3,2,1,0:T(8,128)(2,1)S(1)} %get-tuple-element.4.own), channel_id=1, source_target_pairs={{0,128},{4,132},{8,136},{12,140},{16,144},{20,148},{24,152},{28,15... | collective-permute-start | bytes 294920 | tf_op jit(solution)/shard_map/ppermute | solution.py:232
  87.2 17.3 %collective-permute-start.8 = (bf16[2,4,16,384]{3,2,1,0:T(8,128)(2,1)S(1)}, bf16[2,4,16,384]{3,2,1,0:T(8,128)(2,1)S(1)}, u32[]{:S(2)}, u32[]{:S(2)}) collective-permute-start(bf16[2,4,16,384]{3,2,1,0:T(8,128)(2,1)S(1)} %get-tuple-element.5.grad), channel_id=1, source_target_pairs={{128,0},{132,4},{136,8},{140,12},{144,16},{148,20},{152,24},{156,2... | collective-permute-start | bytes 294920 | tf_op jit(solution)/shard_map/ppermute | solution.py:232
  92.1 7.5 %collective-permute-start.7 = (bf16[2,2,16,384]{3,2,1,0:T(8,128)(2,1)S(1)}, bf16[2,2,16,384]{3,2,1,0:T(8,128)(2,1)S(1)}, u32[]{:S(2)}, u32[]{:S(2)}) collective-permute-start(bf16[2,2,16,384]{3,2,1,0:T(8,128)(2,1)S(1)} %get-tuple-element.10), channel_id=1, source_target_pairs={{0,132},{4,136},{8,140},{12,144},{16,148},{20,152},{24,156},{28,16... | collective-permute-start | bytes 147464 | tf_op jit(solution)/shard_map/ppermute | solution.py:232
  94.0 10.5 %collective-permute-start.9 = (bf16[2,2,16,384]{3,2,1,0:T(8,128)(2,1)S(1)}, bf16[2,2,16,384]{3,2,1,0:T(8,128)(2,1)S(1)}, u32[]{:S(2)}, u32[]{:S(2)}) collective-permute-start(bf16[2,2,16,384]{3,2,1,0:T(8,128)(2,1)S(1)} %get-tuple-element.6), channel_id=1, source_target_pairs={{128,4},{132,8},{136,12},{140,16},{144,20},{148,24},{152,28},{156,... | collective-permute-start | bytes 147464 | tf_op jit(solution)/shard_map/ppermute | solution.py:232
  105.9 20.3 %all-to-all-start.2 = ((bf16[4,30,16,384]{3,2,1,0:T(8,128)(2,1)}), bf16[4,30,16,384]{3,2,1,0:T(8,128)(2,1)}, u32[]{:S(2)}, u32[]{:S(2)}) async-start(bf16[4,30,16,384]{3,2,1,0:T(8,128)(2,1)} %shard_map.81), calls=%async_computation.2 | async-start | bytes 2949120 | tf_op jit(solution)/shard_map/all_to_all | solution.py:236
  110.2 1.6 %copy-start.1 = (bf16[3,3,3,96,384]{4,3,2,1,0:T(8,128)(2,1)S(1)}, bf16[3,3,3,96,384]{4,3,2,1,0:T(8,128)(2,1)}, u32[]{:S(2)}) copy-start(bf16[3,3,3,96,384]{4,3,2,1,0:T(8,128)(2,1)} %weight.3) | copy-start | bytes 5971972
  126.2 1.6 %copy-start.3 = (bf16[3,3,3,96,384]{4,3,2,1,0:T(8,128)(2,1)S(1)}, bf16[3,3,3,96,384]{4,3,2,1,0:T(8,128)(2,1)}, u32[]{:S(2)}) copy-start(bf16[3,3,3,96,384]{4,3,2,1,0:T(8,128)(2,1)} %ahead_weight.3) | copy-start | bytes 5971972
  127.8 15.8 %copy-start.5 = (bf16[2,4,16,384]{3,2,1,0:T(8,128)(2,1)S(1)}, bf16[2,4,16,384]{3,2,1,0:T(8,128)(2,1)}, u32[]{:S(2)}) copy-start(bf16[2,4,16,384]{3,2,1,0:T(8,128)(2,1)} %latent.1) | copy-start | bytes 294916
  127.8 15.8 %copy-start.7 = (bf16[2,4,16,384]{3,2,1,0:T(8,128)(2,1)S(1)}, bf16[2,4,16,384]{3,2,1,0:T(8,128)(2,1)}, u32[]{:S(2)}) copy-start(bf16[2,4,16,384]{3,2,1,0:T(8,128)(2,1)} %cotangent.1) | copy-start | bytes 294916

commit v2 on v1

v2 whole, which is shorter than its diff:
```python
import jax
import jax.numpy as jnp
from jax import lax
from jax.experimental import pallas as pl
from jax.experimental.pallas import tpu as pltpu
from jax.sharding import PartitionSpec as P

epsilon = 1e-06
F32 = jnp.float32
BF16 = jnp.bfloat16

T, H, W, C, O, X = 2, 4, 16, 384, 96, 4
WT = T + 2
SIZE = T * H * W * X
COLS = X * W
LANES = 128
KINDS = WT + 1
BACK = T * H + T


def vmem(count):
    return [pl.BlockSpec(memory_space=pltpu.VMEM)] * count


def call(kernel, out_shape, *operands, scratch=(), flops=0):
    bytes_accessed = sum(a.size * a.dtype.itemsize for a in operands)
    outs = out_shape if isinstance(out_shape, (list, tuple)) else [out_shape]
    bytes_accessed += sum(a.size * a.dtype.itemsize for a in outs)
    return pl.pallas_call(
        kernel,
        out_shape=out_shape,
        in_specs=vmem(len(operands)),
        out_specs=vmem(len(outs)) if isinstance(out_shape, (list, tuple)) else vmem(1)[0],
        scratch_shapes=list(scratch),
        compiler_params=pltpu.CompilerParams(vmem_limit_bytes=40 * 1024 * 1024),
        cost_estimate=pl.CostEstimate(
            flops=flops, bytes_accessed=bytes_accessed, transcendentals=0
        ),
    )(*operands)


def sigmoid(values):
    return 1.0 / (1.0 + jnp.exp(-values))


def normalize(values, gain):
    inverse = lax.rsqrt(jnp.mean(values * values, axis=-1, keepdims=True) + epsilon)
    return values * inverse * gain, inverse


def norm_backward(values, inverse, gain, upstream):
    scaled = upstream * gain
    return inverse * scaled - values * inverse**3 * jnp.mean(
        values * scaled, axis=-1, keepdims=True
    )


def silu_slope(normed):
    sigma = sigmoid(normed)
    return sigma * (1.0 + normed * (1.0 - sigma))


def put_slices(out, row, blocks):
    for target in range(X):
        out[target, row, WT] = jnp.concatenate(
            [block[:, target * O : (target + 1) * O] for block in blocks], axis=-1
        )


def pack_one_kernel(gain, own, before, cot, after, out):
    scale = gain[...]
    for row in range(H):
        for frame in range(WT):
            block = before[frame, row] if frame < 2 else own[frame - 2, row]
            normed, _ = normalize(block.astype(F32), scale)
            block = (normed * sigmoid(normed)).astype(BF16)
            for target in range(X):
                out[target, row, frame] = block
        put_slices(out, row, [cot[0, row], cot[1, row], after[0, row], after[1, row]])


def pack_two_kernel(own, before, grad, after, out):
    for row in range(H):
        for frame in range(WT):
            block = before[frame, row] if frame < 2 else own[frame - 2, row]
            for target in range(X):
                out[target, row, frame] = block
        put_slices(out, row, [grad[0, row], grad[1, row], after[0, row], after[1, row]])


def shifted_sum(parts):
    size = parts[0].shape[0]
    column = lax.broadcasted_iota(jnp.int32, (size, 1), 0) % COLS
    low = jnp.where(column == 0, 0.0, pltpu.roll(parts[0], 1, 0))
    high = jnp.where(column == COLS - 1, 0.0, pltpu.roll(parts[2], size - 1, 0))
    return low + parts[1] + high


def ahead_dot(values, weight):
    return lax.dot_general(
        values, weight, (((1,), (1,)), ((), ())), preferred_element_type=F32
    )


def padded_slice(block, frame):
    zeros = jnp.zeros((W, LANES - O), BF16)
    return jnp.concatenate([block[:, frame * O : (frame + 1) * O], zeros], axis=-1)


def conv_kernel(got, ahead_weight, back_weight, ahead_out, back_out, data, grads):
    for row in range(H):
        for part in range(X):
            block = got[part, row, WT]
            pieces = [padded_slice(block, frame) for frame in range(WT)]
            for tap in range(3):
                target = row + 1 - tap
                if 0 <= target < H:
                    place = slice(target * COLS + part * W, target * COLS + (part + 1) * W)
                    for frame in range(WT):
                        data[frame, place, tap * C : (tap + 1) * C] = got[part, row, frame]
                        grads[frame, place, tap * LANES : (tap + 1) * LANES] = pieces[frame]
    for tap, row in ((0, 0), (2, H - 1)):
        place = slice(row * COLS, (row + 1) * COLS)
        for frame in range(WT):
            data[frame, place, tap * C : (tap + 1) * C] = jnp.zeros((COLS, C), BF16)
            grads[frame, place, tap * LANES : (tap + 1) * LANES] = jnp.zeros((COLS, LANES), BF16)
    total = jnp.zeros((SIZE, 3 * O), F32)
    for time_tap in range(3):
        total = total + ahead_dot(
            data[time_tap : time_tap + T].reshape(SIZE, 3 * C), ahead_weight[time_tap]
        )
    ahead_out[...] = shifted_sum([total[:, tap * O : (tap + 1) * O] for tap in range(3)])
    total = jnp.zeros((SIZE, 3 * C), F32)
    for time_tap in range(3):
        total = total + jnp.dot(
            grads[time_tap : time_tap + T].reshape(SIZE, 3 * LANES),
            back_weight[time_tap],
            preferred_element_type=F32,
        )
    back_out[...] = shifted_sum([total[:, tap * C : (tap + 1) * C] for tap in range(3)])


def edge_kernel(up, down, ahead_weight, back_weight, ahead, back, out, data, grads):
    ahead_parts, back_parts = [], []
    for side, rows in enumerate((up, down)):
        for part in range(X):
            place = slice(part * W, (part + 1) * W)
            for frame in range(WT):
                data[side, frame, place] = rows[part, frame]
                grads[side, frame, place] = padded_slice(rows[part, WT], frame)
        tap = 2 * side
        ahead_total = jnp.zeros((T * COLS, 3 * O), F32)
        back_total = jnp.zeros((T * COLS, 3 * C), F32)
        for time_tap in range(3):
            ahead_total = ahead_total + ahead_dot(
                data[side, time_tap : time_tap + T].reshape(T * COLS, C),
                ahead_weight[time_tap, :, tap * C : (tap + 1) * C],
            )
            back_total = back_total + jnp.dot(
                grads[side, time_tap : time_tap + T].reshape(T * COLS, LANES),
                back_weight[time_tap, tap * LANES : (tap + 1) * LANES],
                preferred_element_type=F32,
            )
        ahead_parts.append(shifted_sum([ahead_total[:, k * O : (k + 1) * O] for k in range(3)]))
        back_parts.append(shifted_sum([back_total[:, k * C : (k + 1) * C] for k in range(3)]))
    for frame in range(T):
        rows = []
        for row in range(H):
            start = (frame * H + row) * COLS
            ahead_row = ahead[start : start + COLS]
            back_row = back[start : start + COLS]
            if row in (0, H - 1):
                side, at = row // (H - 1), frame * COLS
                ahead_row = ahead_row + ahead_parts[side][at : at + COLS]
                back_row = back_row + back_parts[side][at : at + COLS]
            rows.append(ahead_row.astype(BF16))
            back_row = back_row.astype(BF16)
            for target in range(X):
                out[target, frame * H + row] = back_row[target * W : (target + 1) * W]
        rows = jnp.concatenate(rows, axis=-1)
        for target in range(X):
            out[target, T * H + frame] = rows[target * W : (target + 1) * W]


def arrived_grad(got, block):
    total = got[0, block].astype(F32)
    for source in range(1, X):
        total = total + got[source, block].astype(F32)
    return total


def arrived_conv(got, frame, row):
    return jnp.concatenate(
        [got[source, T * H + frame, :, row * O : (row + 1) * O] for source in range(X)], axis=-1
    ).astype(F32)


def middle_kernel(gain, got, active, grad_inner):
    scale = gain[...]
    for frame in range(T):
        for row in range(H):
            inner = arrived_conv(got, frame, row)
            grad_two = arrived_grad(got, frame * H + row)
            normed, inverse = normalize(inner, scale)
            active[frame, row] = (normed * sigmoid(normed)).astype(BF16)
            grad_inner[frame, row] = norm_backward(
                inner, inverse, scale, grad_two * silu_slope(normed)
            ).astype(BF16)


def last_kernel(gain, latent, cotangent, got, block_out, latent_grad):
    scale = gain[...]
    for frame in range(T):
        for row in range(H):
            source = latent[frame, row].astype(F32)
            block_out[frame, row] = (source + arrived_conv(got, frame, row)).astype(BF16)
            normed, inverse = normalize(source, scale)
            grad_one = arrived_grad(got, frame * H + row)
            latent_grad[frame, row] = (
                cotangent[frame, row].astype(F32)
                + norm_backward(source, inverse, scale, grad_one * silu_slope(normed))
            ).astype(BF16)


def shift(values, axis, by):
    size = lax.axis_size(axis)
    pairs = [(i, i + by) for i in range(size) if 0 <= i + by < size]
    return lax.ppermute(values, axis, pairs)


def exchange(values):
    return lax.all_to_all(values, "exp", split_axis=0, concat_axis=0, tiled=True)


def weights_kernel(ahead, back, ahead_out, back_out):
    zeros = jnp.zeros((LANES - O, 3 * C), BF16)
    for time_tap in range(3):
        for row_tap in range(3):
            start = row_tap * LANES
            for tap in range(3):
                ahead_out[
                    time_tap, tap * O : (tap + 1) * O, row_tap * C : (row_tap + 1) * C
                ] = ahead[time_tap, row_tap, tap]
                back_out[time_tap, start : start + O, tap * C : (tap + 1) * C] = back[
                    2 - time_tap, 2 - row_tap, 2 - tap
                ]
            back_out[time_tap, start + O : start + LANES] = zeros


def weights(ahead, back):
    shapes = [
        jax.ShapeDtypeStruct((3, 3 * O, 3 * C), BF16),
        jax.ShapeDtypeStruct((3, 3 * LANES, 3 * C), BF16),
    ]
    return call(weights_kernel, shapes, ahead, back)


def convs(packed, ahead, back):
    got = exchange(packed)
    ahead_weight, back_weight = weights(ahead, back)
    up = shift(got[:, H - 1], "seq", 1)
    down = shift(got[:, 0], "seq", -1)
    sums = call(
        conv_kernel,
        [jax.ShapeDtypeStruct((SIZE, O), F32), jax.ShapeDtypeStruct((SIZE, C), F32)],
        got,
        ahead_weight,
        back_weight,
        scratch=(
            pltpu.VMEM((WT, H * COLS, 3 * C), BF16),
            pltpu.VMEM((WT, H * COLS, 3 * LANES), BF16),
        ),
        flops=2 * SIZE * 27 * 2 * C * LANES,
    )
    summed = call(
        edge_kernel,
        jax.ShapeDtypeStruct((X, BACK, W, C), BF16),
        up,
        down,
        ahead_weight,
        back_weight,
        *sums,
        scratch=(
            pltpu.VMEM((2, WT, COLS, C), BF16),
            pltpu.VMEM((2, WT, COLS, LANES), BF16),
        ),
        flops=SIZE * 9 * 2 * C * LANES,
    )
    return exchange(summed)


def body(latent, cotangent, gain_one, gain_two, kernel_one, kernel_two):
    gain_one, gain_two = gain_one.reshape(1, C), gain_two.reshape(1, C)
    block = jax.ShapeDtypeStruct((T, H, W, C), BF16)
    sent = jax.ShapeDtypeStruct((X, H, KINDS, W, C), BF16)

    before = shift(latent, "section", 1)
    after = shift(cotangent, "section", -1)
    packed = call(pack_one_kernel, sent, gain_one, latent, before, cotangent, after)
    got = convs(packed, kernel_one, kernel_two)
    active, grad_inner = call(middle_kernel, [block, block], gain_two, got)

    before = shift(active, "section", 1)
    after = shift(grad_inner, "section", -1)
    packed = call(pack_two_kernel, sent, active, before, grad_inner, after)
    got = convs(packed, kernel_two, kernel_one)
    return tuple(call(last_kernel, [block, block], gain_one, latent, cotangent, got))


def solution(mesh):
    in_specs = (
        P("section", "seq", "exp", None),
        P("section", "seq", "exp", None),
        P(),
        P(),
        P(None, None, None, "exp", None),
        P(None, None, None, "exp", None),
    )
    out_specs = (P("section", "seq", "exp", None), P("section", "seq", "exp", None))
    return jax.shard_map(body, mesh=mesh, in_specs=in_specs, out_specs=out_specs, check_vma=False)
```

time: 146 us -> 125 us (0.86)
  the two profiles are of different devices: /device:TPU:16 before, /device:TPU:1 now
where the time goes in v2:
time: 125 us; the launch traced here: 124 us
  waiting for transfers between devices  44.4 us (36%)
  starting transfers between devices  32.8 us (26%)
  local copies, waits for them, and re-layouts  18 us (14%)
  Pallas kernels  16.1 us (13%)
  blocking collectives  11.8 us (9%)
    all_to_all x3, waiting for transfers between devices, exchange(): lax.all_to_all(values, 'exp', split_axis=0, concat_axis=0, tiled=True)  27.3 us
    ppermute x8, starting transfers between devices, shift(): return lax.ppermute(values, axis, pairs)  21.7 us
    unnamed x32, local copies, waits for them, and re-layouts  17.2 us
    ppermute x8, waiting for transfers between devices, shift(): return lax.ppermute(values, axis, pairs)  17.1 us
    pallas_call x10, Pallas kernels, call(): pl.pallas_call(kernel, out_shape=out_shape, in_specs=vmem(len(operands)),...  16.1 us
    all_to_all x1, blocking collectives, exchange(): lax.all_to_all(values, 'exp', split_axis=0, concat_axis=0, tiled=True)  11.8 us
    all_to_all x3, starting transfers between devices, exchange(): lax.all_to_all(values, 'exp', split_axis=0, concat_axis=0, tiled=True)  11.1 us
  transfers between devices with their start and end apart: 11, of which 6 were waited for; matrix products, arithmetic and copies ran while one was open for 1% of the time, Pallas kernels for 7%

profile of v2, /device:TPU:1, one launch (start us, length us, event | category | flops | bytes accessed | tf_op | source)
XLA Modules:
  0.0 123.8 jit_solution(16031636648331015844)
XLA Ops:
  0.6 0.0 copy-start
  0.6 5.2 %collective-permute-start = (bf16[2,4,16,384]{3,2,1,0:T(8,128)(2,1)}, bf16[2,4,16,384]{3,2,1,0:T(8,128)(2,1)S(1)}, u32[]{:S(2)}, u32[]{:S(2)}) collective-permute-start(bf16[2,4,16,384]{3,2,1,0:T(8,128)(2,1)} %latent.1), channel_id=1, source_target_pairs={{0,128},{128,256},{256,384},{1,129},{129,257},{257,385},{2,130},{1... | collective-permute-start | bytes 294920 | tf_op jit(solution)/shard_map/ppermute | solution.py:228
  5.8 1.3 %collective-permute-start.1 = (bf16[2,4,16,384]{3,2,1,0:T(8,128)(2,1)}, bf16[2,4,16,384]{3,2,1,0:T(8,128)(2,1)S(1)}, u32[]{:S(2)}, u32[]{:S(2)}) collective-permute-start(bf16[2,4,16,384]{3,2,1,0:T(8,128)(2,1)} %cotangent.1), channel_id=1, source_target_pairs={{128,0},{256,128},{384,256},{129,1},{257,129},{385,257},{130,2},{2... | collective-permute-start | bytes 294920 | tf_op jit(solution)/shard_map/ppermute | solution.py:228
  7.1 0.7 reshape.10.gain
  7.8 0.0 collective-permute-done.before
  7.8 8.8 %collective-permute-done.1.after = bf16[2,4,16,384]{3,2,1,0:T(8,128)(2,1)S(1)} collective-permute-done((bf16[2,4,16,384]{3,2,1,0:T(8,128)(2,1)}, bf16[2,4,16,384]{3,2,1,0:T(8,128)(2,1)S(1)}, u32[]{:S(2)}, u32[]{:S(2)}) %collective-permute-start.1) | collective-permute-done | bytes 98336 | tf_op jit(solution)/shard_map/ppermute | solution.py:228
  16.6 0.0 copy-start.11
  16.6 0.9 copy-done.11
  17.5 0.0 copy-start.13
  17.5 0.9 copy-done.13
  18.4 1.3 %shard_map.77 = bf16[4,4,5,16,384]{4,3,2,1,0:T(8,128)(2,1)} custom-call(f32[1,384]{1,0:T(1,128)S(1)} %reshape.10.gain, bf16[2,4,16,384]{3,2,1,0:T(8,128)(2,1)S(1)} %copy-done.11, bf16[2,4,16,384]{3,2,1,0:T(8,128)(2,1)S(1)} %collective-permute-done.before, bf16[2,4,16,384]{3,2,1,0:T(8,128)(2,1)S(1)} %copy-done.13, ...), custom_call_target="tpu_custom_call" | custom-call | bytes 1377792 | tf_op jit(solution)/shard_map/pallas_call | solution.py:29
  19.7 4.1 %all-to-all-start = ((bf16[4,4,5,16,384]{4,3,2,1,0:T(8,128)(2,1)}), bf16[4,4,5,16,384]{4,3,2,1,0:T(8,128)(2,1)S(1)}, u32[]{:S(2)}, u32[]{:S(2)}) async-start(bf16[4,4,5,16,384]{4,3,2,1,0:T(8,128)(2,1)} %shard_map.77), calls=%async_computation | async-start | bytes 1966080 | tf_op jit(solution)/shard_map/all_to_all | solution.py:232
  23.8 0.0 copy-done
  23.8 1.6 %copy-done.1 = bf16[3,3,3,96,384]{4,3,2,1,0:T(8,128)(2,1)S(1)} copy-done((bf16[3,3,3,96,384]{4,3,2,1,0:T(8,128)(2,1)S(1)}, bf16[3,3,3,96,384]{4,3,2,1,0:T(8,128)(2,1)}, u32[]{:S(2)}) %copy-start.1) | copy-done | bytes 1990680
  25.3 0.4 shard_map.78
  25.7 0.0 copy-start.3
  25.7 1.5 %copy-done.3 = bf16[3,384,1152]{2,1,0:T(8,128)(2,1)} copy-done((bf16[3,384,1152]{2,1,0:T(8,128)(2,1)}, bf16[3,384,1152]{2,1,0:T(8,128)(2,1)S(1)}, u32[]{:S(2)}) %copy-start.3) | copy-done | bytes 2654232
  27.2 0.0 copy-start.7
  27.2 1.3 %copy-done.7 = bf16[3,288,1152]{2,1,0:T(8,128)(2,1)} copy-done((bf16[3,288,1152]{2,1,0:T(8,128)(2,1)}, bf16[3,288,1152]{2,1,0:T(8,128)(2,1)S(1)}, u32[]{:S(2)}) %copy-start.7) | copy-done | bytes 1990680
  28.6 8.8 %all-to-all-done.got = bf16[4,4,5,16,384]{4,3,2,1,0:T(8,128)(2,1)S(1)} async-done(((bf16[4,4,5,16,384]{4,3,2,1,0:T(8,128)(2,1)}), bf16[4,4,5,16,384]{4,3,2,1,0:T(8,128)(2,1)S(1)}, u32[]{:S(2)}, u32[]{:S(2)}) %all-to-all-start) | async-done | bytes 983072 | tf_op jit(solution)/shard_map/all_to_all | solution.py:232
  37.3 0.1 slice_bitcast_fusion.2
  37.4 1.9 %collective-permute-start.2 = (bf16[4,5,16,384]{3,2,1,0:T(8,128)(2,1)S(1)}, bf16[4,5,16,384]{3,2,1,0:T(8,128)(2,1)S(1)}, u32[]{:S(2)}, u32[]{:S(2)}) collective-permute-start(bf16[4,5,16,384]{3,2,1,0:T(8,128)(2,1)S(1)} %get-tuple-element.25), channel_id=1, source_target_pairs={{0,4},{4,8},{8,12},{12,16},{16,20},{20,24},{24,28},{28,32},{32,36}... | collective-permute-start | bytes 737288 | tf_op jit(solution)/shard_map/ppermute | solution.py:228
  39.3 3.1 %collective-permute-start.3 = (bf16[4,5,16,384]{3,2,1,0:T(8,128)(2,1)S(1)}, bf16[4,5,16,384]{3,2,1,0:T(8,128)(2,1)S(1)}, u32[]{:S(2)}, u32[]{:S(2)}) collective-permute-start(bf16[4,5,16,384]{3,2,1,0:T(8,128)(2,1)S(1)} %get-tuple-element.24), channel_id=1, source_target_pairs={{4,0},{8,4},{12,8},{16,12},{20,16},{24,20},{28,24},{32,28},{36,32}... | collective-permute-start | bytes 737288 | tf_op jit(solution)/shard_map/ppermute | solution.py:228
  42.4 0.0 copy-start.4
  42.4 1.7 %copy-done.4 = bf16[3,384,1152]{2,1,0:T(8,128)(2,1)S(1)} copy-done((bf16[3,384,1152]{2,1,0:T(8,128)(2,1)S(1)}, bf16[3,384,1152]{2,1,0:T(8,128)(2,1)}, u32[]{:S(2)}) %copy-start.4) | copy-done | bytes 2654232
  44.2 1.6 %copy-done.8 = bf16[3,288,1152]{2,1,0:T(8,128)(2,1)S(1)} copy-done((bf16[3,288,1152]{2,1,0:T(8,128)(2,1)S(1)}, bf16[3,288,1152]{2,1,0:T(8,128)(2,1)}, u32[]{:S(2)}) %copy-start.8) | copy-done | bytes 1990680
  45.7 4.1 %shard_map.79 = (f32[512,96]{1,0:T(8,128)S(1)}, f32[512,384]{1,0:T(8,128)S(1)}) custom-call(bf16[4,4,5,16,384]{4,3,2,1,0:T(8,128)(2,1)S(1)} %all-to-all-done.got, bf16[3,288,1152]{2,1,0:T(8,128)(2,1)S(1)} %copy-done.8, bf16[3,384,1152]{2,1,0:T(8,128)(2,1)S(1)} %copy-done.4), custom_call_target="tpu_custom_call" | custom-call | flops 2717908992 | bytes 6610944 | tf_op jit(solution)/shard_map/pallas_call | solution.py:29
  49.8 0.0 collective-permute-done.2.up
  49.8 0.0 collective-permute-done.3.down
  49.8 0.0 copy-start.15
  49.8 2.1 %shard_map.80 = bf16[4,10,16,384]{3,2,1,0:T(8,128)(2,1)} custom-call(bf16[4,5,16,384]{3,2,1,0:T(8,128)(2,1)S(1)} %collective-permute-done.2.up, bf16[4,5,16,384]{3,2,1,0:T(8,128)(2,1)S(1)} %collective-permute-done.3.down, bf16[3,288,1152]{2,1,0:T(8,128)(2,1)S(1)} %copy-done.8, bf16[3,384,1152]{2,1,0:T(8,128)(2,1)S(1)} %copy-done.4, ...), custom_call_target="tpu_custom_call" | custom-call | flops 452984832 | bytes 6610944 | tf_op jit(solution)/shard_map/pallas_call | solution.py:29
  51.9 3.5 %all-to-all-start.1 = ((bf16[4,10,16,384]{3,2,1,0:T(8,128)(2,1)}), bf16[4,10,16,384]{3,2,1,0:T(8,128)(2,1)S(1)}, u32[]{:S(2)}, u32[]{:S(2)}) async-start(bf16[4,10,16,384]{3,2,1,0:T(8,128)(2,1)} %shard_map.80), calls=%async_computation.1 | async-start | bytes 983040 | tf_op jit(solution)/shard_map/all_to_all | solution.py:232
  55.4 0.0 copy-done.15
  55.4 9.3 %all-to-all-done.1.got = bf16[4,10,16,384]{3,2,1,0:T(8,128)(2,1)S(1)} async-done(((bf16[4,10,16,384]{3,2,1,0:T(8,128)(2,1)}), bf16[4,10,16,384]{3,2,1,0:T(8,128)(2,1)S(1)}, u32[]{:S(2)}, u32[]{:S(2)}) %all-to-all-start.1) | async-done | bytes 491552 | tf_op jit(solution)/shard_map/all_to_all | solution.py:232
  64.7 0.4 shard_map.81
  65.1 4.4 %collective-permute-start.4 = (bf16[2,4,16,384]{3,2,1,0:T(8,128)(2,1)S(1)}, bf16[2,4,16,384]{3,2,1,0:T(8,128)(2,1)S(1)}, u32[]{:S(2)}, u32[]{:S(2)}) collective-permute-start(bf16[2,4,16,384]{3,2,1,0:T(8,128)(2,1)S(1)} %get-tuple-element.16.own), channel_id=1, source_target_pairs={{0,128},{128,256},{256,384},{1,129},{129,257},{257,385},{2,130},{1... | collective-permute-start | bytes 294920 | tf_op jit(solution)/shard_map/ppermute | solution.py:228
  69.5 1.3 %collective-permute-start.5 = (bf16[2,4,16,384]{3,2,1,0:T(8,128)(2,1)S(1)}, bf16[2,4,16,384]{3,2,1,0:T(8,128)(2,1)S(1)}, u32[]{:S(2)}, u32[]{:S(2)}) collective-permute-start(bf16[2,4,16,384]{3,2,1,0:T(8,128)(2,1)S(1)} %get-tuple-element.17.grad), channel_id=1, source_target_pairs={{128,0},{256,128},{384,256},{129,1},{257,129},{385,257},{130,2},{2... | collective-permute-start | bytes 294920 | tf_op jit(solution)/shard_map/ppermute | solution.py:228
  70.8 0.3 collective-permute-done.4.before
  71.1 8.0 %collective-permute-done.5.after = bf16[2,4,16,384]{3,2,1,0:T(8,128)(2,1)S(1)} collective-permute-done((bf16[2,4,16,384]{3,2,1,0:T(8,128)(2,1)S(1)}, bf16[2,4,16,384]{3,2,1,0:T(8,128)(2,1)S(1)}, u32[]{:S(2)}, u32[]{:S(2)}) %collective-permute-start.5) | collective-permute-done | bytes 98336 | tf_op jit(solution)/shard_map/ppermute | solution.py:228
  79.1 1.1 shard_map.82
  80.2 3.5 %all-to-all-start.2 = ((bf16[4,4,5,16,384]{4,3,2,1,0:T(8,128)(2,1)}), bf16[4,4,5,16,384]{4,3,2,1,0:T(8,128)(2,1)S(1)}, u32[]{:S(2)}, u32[]{:S(2)}) async-start(bf16[4,4,5,16,384]{4,3,2,1,0:T(8,128)(2,1)} %shard_map.82), calls=%async_computation.2 | async-start | bytes 1966080 | tf_op jit(solution)/shard_map/all_to_all | solution.py:232
  83.7 0.0 copy-start.2
  83.7 1.5 %copy-done.2 = bf16[3,3,3,96,384]{4,3,2,1,0:T(8,128)(2,1)S(1)} copy-done((bf16[3,3,3,96,384]{4,3,2,1,0:T(8,128)(2,1)S(1)}, bf16[3,3,3,96,384]{4,3,2,1,0:T(8,128)(2,1)}, u32[]{:S(2)}) %copy-start.2) | copy-done | bytes 1990680
  85.3 0.4 shard_map.83
  85.7 0.0 copy-start.5
  85.7 1.5 %copy-done.5 = bf16[3,384,1152]{2,1,0:T(8,128)(2,1)} copy-done((bf16[3,384,1152]{2,1,0:T(8,128)(2,1)}, bf16[3,384,1152]{2,1,0:T(8,128)(2,1)S(1)}, u32[]{:S(2)}) %copy-start.5) | copy-done | bytes 2654232
  87.2 1.3 %copy-done.9 = bf16[3,288,1152]{2,1,0:T(8,128)(2,1)} copy-done((bf16[3,288,1152]{2,1,0:T(8,128)(2,1)}, bf16[3,288,1152]{2,1,0:T(8,128)(2,1)S(1)}, u32[]{:S(2)}) %copy-start.9) | copy-done | bytes 1990680
  88.5 9.2 %all-to-all-done.2.got = bf16[4,4,5,16,384]{4,3,2,1,0:T(8,128)(2,1)S(1)} async-done(((bf16[4,4,5,16,384]{4,3,2,1,0:T(8,128)(2,1)}), bf16[4,4,5,16,384]{4,3,2,1,0:T(8,128)(2,1)S(1)}, u32[]{:S(2)}, u32[]{:S(2)}) %all-to-all-start.2) | async-done | bytes 983072 | tf_op jit(solution)/shard_map/all_to_all | solution.py:232
  97.7 0.1 slice_bitcast_fusion
  97.8 1.9 %collective-permute-start.6 = (bf16[4,5,16,384]{3,2,1,0:T(8,128)(2,1)S(1)}, bf16[4,5,16,384]{3,2,1,0:T(8,128)(2,1)S(1)}, u32[]{:S(2)}, u32[]{:S(2)}) collective-permute-start(bf16[4,5,16,384]{3,2,1,0:T(8,128)(2,1)S(1)} %get-tuple-element.23), channel_id=1, source_target_pairs={{0,4},{4,8},{8,12},{12,16},{16,20},{20,24},{24,28},{28,32},{32,36}... | collective-permute-start | bytes 737288 | tf_op jit(solution)/shard_map/ppermute | solution.py:228
  99.7 2.6 %collective-permute-start.7 = (bf16[4,5,16,384]{3,2,1,0:T(8,128)(2,1)S(1)}, bf16[4,5,16,384]{3,2,1,0:T(8,128)(2,1)S(1)}, u32[]{:S(2)}, u32[]{:S(2)}) collective-permute-start(bf16[4,5,16,384]{3,2,1,0:T(8,128)(2,1)S(1)} %get-tuple-element.22), channel_id=1, source_target_pairs={{4,0},{8,4},{12,8},{16,12},{20,16},{24,20},{28,24},{32,28},{36,32}... | collective-permute-start | bytes 737288 | tf_op jit(solution)/shard_map/ppermute | solution.py:228
  102.3 0.0 copy-start.6
  102.3 1.7 %copy-done.6 = bf16[3,384,1152]{2,1,0:T(8,128)(2,1)S(1)} copy-done((bf16[3,384,1152]{2,1,0:T(8,128)(2,1)S(1)}, bf16[3,384,1152]{2,1,0:T(8,128)(2,1)}, u32[]{:S(2)}) %copy-start.6) | copy-done | bytes 2654232
  104.1 1.6 %copy-done.10 = bf16[3,288,1152]{2,1,0:T(8,128)(2,1)S(1)} copy-done((bf16[3,288,1152]{2,1,0:T(8,128)(2,1)S(1)}, bf16[3,288,1152]{2,1,0:T(8,128)(2,1)}, u32[]{:S(2)}) %copy-start.10) | copy-done | bytes 1990680
  105.6 4.1 %shard_map.84 = (f32[512,96]{1,0:T(8,128)S(1)}, f32[512,384]{1,0:T(8,128)S(1)}) custom-call(bf16[4,4,5,16,384]{4,3,2,1,0:T(8,128)(2,1)S(1)} %all-to-all-done.2.got, bf16[3,288,1152]{2,1,0:T(8,128)(2,1)S(1)} %copy-done.10, bf16[3,384,1152]{2,1,0:T(8,128)(2,1)S(1)} %copy-done.6), custom_call_target="tpu_custom_call" | custom-call | flops 2717908992 | bytes 6610944 | tf_op jit(solution)/shard_map/pallas_call | solution.py:29
  109.7 0.0 collective-permute-done.6.up
  109.7 0.0 collective-permute-done.7.down
  109.7 0.0 copy-start.12
  109.8 0.0 copy-start.14
  109.8 1.3 %shard_map.85 = bf16[4,10,16,384]{3,2,1,0:T(8,128)(2,1)S(1)} custom-call(bf16[4,5,16,384]{3,2,1,0:T(8,128)(2,1)S(1)} %collective-permute-done.6.up, bf16[4,5,16,384]{3,2,1,0:T(8,128)(2,1)S(1)} %collective-permute-done.7.down, bf16[3,288,1152]{2,1,0:T(8,128)(2,1)S(1)} %copy-done.10, bf16[3,384,1152]{2,1,0:T(8,128)(2,1)S(1)} %copy-done.6, ...), custom_call_target="tpu_custom_call" | custom-call | flops 452984832 | bytes 6610944 | tf_op jit(solution)/shard_map/pallas_call | solution.py:29
  111.0 11.8 %all_to_all.20.got = bf16[4,10,16,384]{3,2,1,0:T(8,128)(2,1)S(1)} all-to-all(bf16[4,10,16,384]{3,2,1,0:T(8,128)(2,1)S(1)} %shard_map.85), channel_id=1, replica_groups=mesh['section'=4,'seq'=32,'exp'=4] {'exp'}, dimensions={0} | all-to-all | bytes 983040 | tf_op jit(solution)/shard_map/all_to_all | solution.py:232
  122.8 0.0 copy-done.12
  122.8 0.0 copy-done.14
  122.8 1.1 shard_map.86
  (5 shorter events, 0.0 us)
Async XLA Ops:
  0.6 23.1 %copy-start = (bf16[3,3,3,96,384]{4,3,2,1,0:T(8,128)(2,1)S(1)}, bf16[3,3,3,96,384]{4,3,2,1,0:T(8,128)(2,1)}, u32[]{:S(2)}) copy-start(bf16[3,3,3,96,384]{4,3,2,1,0:T(8,128)(2,1)} %back.3) | copy-start | bytes 5971972
  0.6 7.2 %collective-permute-start = (bf16[2,4,16,384]{3,2,1,0:T(8,128)(2,1)}, bf16[2,4,16,384]{3,2,1,0:T(8,128)(2,1)S(1)}, u32[]{:S(2)}, u32[]{:S(2)}) collective-permute-start(bf16[2,4,16,384]{3,2,1,0:T(8,128)(2,1)} %latent.1), channel_id=1, source_target_pairs={{0,128},{128,256},{256,384},{1,129},{129,257},{257,385},{2,130},{1... | collective-permute-start | bytes 294920 | tf_op jit(solution)/shard_map/ppermute | solution.py:228
  5.8 10.8 %collective-permute-start.1 = (bf16[2,4,16,384]{3,2,1,0:T(8,128)(2,1)}, bf16[2,4,16,384]{3,2,1,0:T(8,128)(2,1)S(1)}, u32[]{:S(2)}, u32[]{:S(2)}) collective-permute-start(bf16[2,4,16,384]{3,2,1,0:T(8,128)(2,1)} %cotangent.1), channel_id=1, source_target_pairs={{128,0},{256,128},{384,256},{129,1},{257,129},{385,257},{130,2},{2... | collective-permute-start | bytes 294920 | tf_op jit(solution)/shard_map/ppermute | solution.py:228
  16.6 0.9 copy-start.11
  17.5 0.9 copy-start.13
  19.7 17.7 %all-to-all-start = ((bf16[4,4,5,16,384]{4,3,2,1,0:T(8,128)(2,1)}), bf16[4,4,5,16,384]{4,3,2,1,0:T(8,128)(2,1)S(1)}, u32[]{:S(2)}, u32[]{:S(2)}) async-start(bf16[4,4,5,16,384]{4,3,2,1,0:T(8,128)(2,1)} %shard_map.77), calls=%async_computation | async-start | bytes 1966080 | tf_op jit(solution)/shard_map/all_to_all | solution.py:232
  23.8 1.6 %copy-start.1 = (bf16[3,3,3,96,384]{4,3,2,1,0:T(8,128)(2,1)S(1)}, bf16[3,3,3,96,384]{4,3,2,1,0:T(8,128)(2,1)}, u32[]{:S(2)}) copy-start(bf16[3,3,3,96,384]{4,3,2,1,0:T(8,128)(2,1)} %ahead.3) | copy-start | bytes 5971972
  25.7 1.5 %copy-start.3 = (bf16[3,384,1152]{2,1,0:T(8,128)(2,1)}, bf16[3,384,1152]{2,1,0:T(8,128)(2,1)S(1)}, u32[]{:S(2)}) copy-start(bf16[3,384,1152]{2,1,0:T(8,128)(2,1)S(1)} %get-tuple-element.13.back_weight) | copy-start | bytes 7962628
  27.2 1.3 %copy-start.7 = (bf16[3,288,1152]{2,1,0:T(8,128)(2,1)}, bf16[3,288,1152]{2,1,0:T(8,128)(2,1)S(1)}, u32[]{:S(2)}) copy-start(bf16[3,288,1152]{2,1,0:T(8,128)(2,1)S(1)} %get-tuple-element.12.ahead_weight) | copy-start | bytes 5971972
  37.4 12.4 %collective-permute-start.2 = (bf16[4,5,16,384]{3,2,1,0:T(8,128)(2,1)S(1)}, bf16[4,5,16,384]{3,2,1,0:T(8,128)(2,1)S(1)}, u32[]{:S(2)}, u32[]{:S(2)}) collective-permute-start(bf16[4,5,16,384]{3,2,1,0:T(8,128)(2,1)S(1)} %get-tuple-element.25), channel_id=1, source_target_pairs={{0,4},{4,8},{8,12},{12,16},{16,20},{20,24},{24,28},{28,32},{32,36}... | collective-permute-start | bytes 737288 | tf_op jit(solution)/shard_map/ppermute | solution.py:228
  39.3 10.5 %collective-permute-start.3 = (bf16[4,5,16,384]{3,2,1,0:T(8,128)(2,1)S(1)}, bf16[4,5,16,384]{3,2,1,0:T(8,128)(2,1)S(1)}, u32[]{:S(2)}, u32[]{:S(2)}) collective-permute-start(bf16[4,5,16,384]{3,2,1,0:T(8,128)(2,1)S(1)} %get-tuple-element.24), channel_id=1, source_target_pairs={{4,0},{8,4},{12,8},{16,12},{20,16},{24,20},{28,24},{32,28},{36,32}... | collective-permute-start | bytes 737288 | tf_op jit(solution)/shard_map/ppermute | solution.py:228
  42.4 1.8 %copy-start.4 = (bf16[3,384,1152]{2,1,0:T(8,128)(2,1)S(1)}, bf16[3,384,1152]{2,1,0:T(8,128)(2,1)}, u32[]{:S(2)}) copy-start(bf16[3,384,1152]{2,1,0:T(8,128)(2,1)} %copy-done.3) | copy-start | bytes 7962628
  44.2 1.6 %copy-start.8 = (bf16[3,288,1152]{2,1,0:T(8,128)(2,1)S(1)}, bf16[3,288,1152]{2,1,0:T(8,128)(2,1)}, u32[]{:S(2)}) copy-start(bf16[3,288,1152]{2,1,0:T(8,128)(2,1)} %copy-done.7) | copy-start | bytes 5971972
  49.8 5.5 %copy-start.15 = (f32[384]{0:T(512)S(1)}, f32[384]{0:T(512)}, u32[]{:S(2)}) copy-start(f32[384]{0:T(512)} %param.9) | copy-start | bytes 4612
  51.9 12.8 %all-to-all-start.1 = ((bf16[4,10,16,384]{3,2,1,0:T(8,128)(2,1)}), bf16[4,10,16,384]{3,2,1,0:T(8,128)(2,1)S(1)}, u32[]{:S(2)}, u32[]{:S(2)}) async-start(bf16[4,10,16,384]{3,2,1,0:T(8,128)(2,1)} %shard_map.80), calls=%async_computation.1 | async-start | bytes 983040 | tf_op jit(solution)/shard_map/all_to_all | solution.py:232
  65.1 6.0 %collective-permute-start.4 = (bf16[2,4,16,384]{3,2,1,0:T(8,128)(2,1)S(1)}, bf16[2,4,16,384]{3,2,1,0:T(8,128)(2,1)S(1)}, u32[]{:S(2)}, u32[]{:S(2)}) collective-permute-start(bf16[2,4,16,384]{3,2,1,0:T(8,128)(2,1)S(1)} %get-tuple-element.16.own), channel_id=1, source_target_pairs={{0,128},{128,256},{256,384},{1,129},{129,257},{257,385},{2,130},{1... | collective-permute-start | bytes 294920 | tf_op jit(solution)/shard_map/ppermute | solution.py:228
  69.5 9.6 %collective-permute-start.5 = (bf16[2,4,16,384]{3,2,1,0:T(8,128)(2,1)S(1)}, bf16[2,4,16,384]{3,2,1,0:T(8,128)(2,1)S(1)}, u32[]{:S(2)}, u32[]{:S(2)}) collective-permute-start(bf16[2,4,16,384]{3,2,1,0:T(8,128)(2,1)S(1)} %get-tuple-element.17.grad), channel_id=1, source_target_pairs={{128,0},{256,128},{384,256},{129,1},{257,129},{385,257},{130,2},{2... | collective-permute-start | bytes 294920 | tf_op jit(solution)/shard_map/ppermute | solution.py:228
  80.2 17.5 %all-to-all-start.2 = ((bf16[4,4,5,16,384]{4,3,2,1,0:T(8,128)(2,1)}), bf16[4,4,5,16,384]{4,3,2,1,0:T(8,128)(2,1)S(1)}, u32[]{:S(2)}, u32[]{:S(2)}) async-start(bf16[4,4,5,16,384]{4,3,2,1,0:T(8,128)(2,1)} %shard_map.82), calls=%async_computation.2 | async-start | bytes 1966080 | tf_op jit(solution)/shard_map/all_to_all | solution.py:232
  83.7 1.6 %copy-start.2 = (bf16[3,3,3,96,384]{4,3,2,1,0:T(8,128)(2,1)S(1)}, bf16[3,3,3,96,384]{4,3,2,1,0:T(8,128)(2,1)}, u32[]{:S(2)}) copy-start(bf16[3,3,3,96,384]{4,3,2,1,0:T(8,128)(2,1)} %ahead.3) | copy-start | bytes 5971972
  85.7 1.5 %copy-start.5 = (bf16[3,384,1152]{2,1,0:T(8,128)(2,1)}, bf16[3,384,1152]{2,1,0:T(8,128)(2,1)S(1)}, u32[]{:S(2)}) copy-start(bf16[3,384,1152]{2,1,0:T(8,128)(2,1)S(1)} %get-tuple-element.19.back_weight) | copy-start | bytes 7962628
  87.2 1.3 %copy-start.9 = (bf16[3,288,1152]{2,1,0:T(8,128)(2,1)}, bf16[3,288,1152]{2,1,0:T(8,128)(2,1)S(1)}, u32[]{:S(2)}) copy-start(bf16[3,288,1152]{2,1,0:T(8,128)(2,1)S(1)} %get-tuple-element.18.ahead_weight) | copy-start | bytes 5971972
  97.8 12.0 %collective-permute-start.6 = (bf16[4,5,16,384]{3,2,1,0:T(8,128)(2,1)S(1)}, bf16[4,5,16,384]{3,2,1,0:T(8,128)(2,1)S(1)}, u32[]{:S(2)}, u32[]{:S(2)}) collective-permute-start(bf16[4,5,16,384]{3,2,1,0:T(8,128)(2,1)S(1)} %get-tuple-element.23), channel_id=1, source_target_pairs={{0,4},{4,8},{8,12},{12,16},{16,20},{20,24},{24,28},{28,32},{32,36}... | collective-permute-start | bytes 737288 | tf_op jit(solution)/shard_map/ppermute | solution.py:228
  99.7 10.1 %collective-permute-start.7 = (bf16[4,5,16,384]{3,2,1,0:T(8,128)(2,1)S(1)}, bf16[4,5,16,384]{3,2,1,0:T(8,128)(2,1)S(1)}, u32[]{:S(2)}, u32[]{:S(2)}) collective-permute-start(bf16[4,5,16,384]{3,2,1,0:T(8,128)(2,1)S(1)} %get-tuple-element.22), channel_id=1, source_target_pairs={{4,0},{8,4},{12,8},{16,12},{20,16},{24,20},{28,24},{32,28},{36,32}... | collective-permute-start | bytes 737288 | tf_op jit(solution)/shard_map/ppermute | solution.py:228
  102.3 1.8 %copy-start.6 = (bf16[3,384,1152]{2,1,0:T(8,128)(2,1)S(1)}, bf16[3,384,1152]{2,1,0:T(8,128)(2,1)}, u32[]{:S(2)}) copy-start(bf16[3,384,1152]{2,1,0:T(8,128)(2,1)} %copy-done.5) | copy-start | bytes 7962628
  104.1 1.6 %copy-start.10 = (bf16[3,288,1152]{2,1,0:T(8,128)(2,1)S(1)}, bf16[3,288,1152]{2,1,0:T(8,128)(2,1)}, u32[]{:S(2)}) copy-start(bf16[3,288,1152]{2,1,0:T(8,128)(2,1)} %copy-done.9) | copy-start | bytes 5971972
  109.7 13.0 %copy-start.12 = (bf16[2,4,16,384]{3,2,1,0:T(8,128)(2,1)S(1)}, bf16[2,4,16,384]{3,2,1,0:T(8,128)(2,1)}, u32[]{:S(2)}) copy-start(bf16[2,4,16,384]{3,2,1,0:T(8,128)(2,1)} %latent.1) | copy-start | bytes 294916
  109.8 13.0 %copy-start.14 = (bf16[2,4,16,384]{3,2,1,0:T(8,128)(2,1)S(1)}, bf16[2,4,16,384]{3,2,1,0:T(8,128)(2,1)}, u32[]{:S(2)}) copy-start(bf16[2,4,16,384]{3,2,1,0:T(8,128)(2,1)} %cotangent.1) | copy-start | bytes 294916

commit v3 on v2

--- a/solution.py
+++ b/solution.py
@@ -18,25 +18,27 @@
 BACK = T * H + T
 
 
-def vmem(count):
-    return [pl.BlockSpec(memory_space=pltpu.VMEM)] * count
-
-
-def call(kernel, out_shape, *operands, scratch=(), flops=0):
+def places(count, space):
+    return [pl.BlockSpec(memory_space=space)] * count
+
+
+def call(kernel, out_shape, *operands, scratch=(), flops=0, far=0):
     bytes_accessed = sum(a.size * a.dtype.itemsize for a in operands)
     outs = out_shape if isinstance(out_shape, (list, tuple)) else [out_shape]
     bytes_accessed += sum(a.size * a.dtype.itemsize for a in outs)
+    near = len(operands) - far
+    pinned = [pltpu.with_memory_space_constraint(a, pltpu.HBM) for a in operands[near:]]
     return pl.pallas_call(
         kernel,
         out_shape=out_shape,
-        in_specs=vmem(len(operands)),
-        out_specs=vmem(len(outs)) if isinstance(out_shape, (list, tuple)) else vmem(1)[0],
+        in_specs=places(near, pltpu.VMEM) + places(far, pltpu.HBM),
+        out_specs=places(len(outs), pltpu.VMEM) if outs is out_shape else places(1, pltpu.VMEM)[0],
         scratch_shapes=list(scratch),
         compiler_params=pltpu.CompilerParams(vmem_limit_bytes=40 * 1024 * 1024),
         cost_estimate=pl.CostEstimate(
             flops=flops, bytes_accessed=bytes_accessed, transcendentals=0
         ),
-    )(*operands)
+    )(*operands[:near], *pinned)
 
 
 def sigmoid(values):
@@ -67,15 +69,30 @@
         )
 
 
-def pack_one_kernel(gain, own, before, cot, after, out):
+def put_active(out, row, frame, block, scale):
+    normed, _ = normalize(block.astype(F32), scale)
+    block = (normed * sigmoid(normed)).astype(BF16)
+    for target in range(X):
+        out[target, row, frame] = block
+
+
+def pack_one_kernel(gain, before, after, own_far, cot_far, out, own, cot, sems):
     scale = gain[...]
-    for row in range(H):
-        for frame in range(WT):
-            block = before[frame, row] if frame < 2 else own[frame - 2, row]
-            normed, _ = normalize(block.astype(F32), scale)
-            block = (normed * sigmoid(normed)).astype(BF16)
-            for target in range(X):
-                out[target, row, frame] = block
+    copies = [
+        pltpu.make_async_copy(own_far, own, sems.at[0]),
+        pltpu.make_async_copy(cot_far, cot, sems.at[1]),
+    ]
+    for copy in copies:
+        copy.start()
+    for row in range(H):
+        for frame in range(T):
+            put_active(out, row, frame, before[frame, row], scale)
+    copies[0].wait()
+    for row in range(H):
+        for frame in range(T):
+            put_active(out, row, T + frame, own[frame, row], scale)
+    copies[1].wait()
+    for row in range(H):
         put_slices(out, row, [cot[0, row], cot[1, row], after[0, row], after[1, row]])
 
 
@@ -107,37 +124,55 @@
     return jnp.concatenate([block[:, frame * O : (frame + 1) * O], zeros], axis=-1)
 
 
-def conv_kernel(got, ahead_weight, back_weight, ahead_out, back_out, data, grads):
+def own_taps():
+    return [
+        (tap, row, row + 1 - tap) for tap in range(3) for row in range(H) if 0 <= row + 1 - tap < H
+    ]
+
+
+def clear_borders(operand, width):
+    for tap, row in ((0, 0), (2, H - 1)):
+        place = slice(row * COLS, (row + 1) * COLS)
+        for frame in range(WT):
+            operand[frame, place, tap * width : (tap + 1) * width] = jnp.zeros((COLS, width), BF16)
+
+
+def ahead_kernel(got, weight, out, data):
+    for tap, row, target in own_taps():
+        for part in range(X):
+            place = slice(target * COLS + part * W, target * COLS + (part + 1) * W)
+            for frame in range(WT):
+                data[frame, place, tap * C : (tap + 1) * C] = got[part, row, frame]
+    clear_borders(data, C)
+    total = jnp.zeros((3 * O, SIZE), F32)
+    for time_tap in range(3):
+        total = total + ahead_dot(
+            weight[time_tap], data[time_tap : time_tap + T].reshape(SIZE, 3 * C)
+        )
+    column = lax.broadcasted_iota(jnp.int32, (1, SIZE), 1) % COLS
+    low = jnp.where(column == 0, 0.0, pltpu.roll(total[:O], 1, 1))
+    high = jnp.where(column == COLS - 1, 0.0, pltpu.roll(total[2 * O :], SIZE - 1, 1))
+    out[...] = (low + total[O : 2 * O] + high).T
+
+
+def back_kernel(got, weight, out, grads):
     for row in range(H):
         for part in range(X):
             block = got[part, row, WT]
             pieces = [padded_slice(block, frame) for frame in range(WT)]
-            for tap in range(3):
-                target = row + 1 - tap
-                if 0 <= target < H:
+            for tap, source, target in own_taps():
+                if source == row:
                     place = slice(target * COLS + part * W, target * COLS + (part + 1) * W)
                     for frame in range(WT):
-                        data[frame, place, tap * C : (tap + 1) * C] = got[part, row, frame]
                         grads[frame, place, tap * LANES : (tap + 1) * LANES] = pieces[frame]
-    for tap, row in ((0, 0), (2, H - 1)):
-        place = slice(row * COLS, (row + 1) * COLS)
-        for frame in range(WT):
-            data[frame, place, tap * C : (tap + 1) * C] = jnp.zeros((COLS, C), BF16)
-            grads[frame, place, tap * LANES : (tap + 1) * LANES] = jnp.zeros((COLS, LANES), BF16)
-    total = jnp.zeros((SIZE, 3 * O), F32)
-    for time_tap in range(3):
-        total = total + ahead_dot(
-            data[time_tap : time_tap + T].reshape(SIZE, 3 * C), ahead_weight[time_tap]
-        )
-    ahead_out[...] = shifted_sum([total[:, tap * O : (tap + 1) * O] for tap in range(3)])
-    total = jnp.zeros((SIZE, 3 * C), F32)
-    for time_tap in range(3):
-        total = total + jnp.dot(
-            grads[time_tap : time_tap + T].reshape(SIZE, 3 * LANES),
-            back_weight[time_tap],
-            preferred_element_type=F32,
-        )
-    back_out[...] = shifted_sum([total[:, tap * C : (tap + 1) * C] for tap in range(3)])
+    clear_borders(grads, LANES)
+    operand = jnp.concatenate(
+        [grads[tap : tap + T].reshape(SIZE, 3 * LANES) for tap in range(3)], axis=-1
+    )
+    total = jnp.dot(
+        operand, weight[...].reshape(9 * LANES, 3 * C), preferred_element_type=F32
+    )
+    out[...] = shifted_sum([total[:, tap * C : (tap + 1) * C] for tap in range(3)])
 
 
 def edge_kernel(up, down, ahead_weight, back_weight, ahead, back, out, data, grads):
@@ -247,30 +282,32 @@
             back_out[time_tap, start + O : start + LANES] = zeros
 
 
-def weights(ahead, back):
-    shapes = [
-        jax.ShapeDtypeStruct((3, 3 * O, 3 * C), BF16),
-        jax.ShapeDtypeStruct((3, 3 * LANES, 3 * C), BF16),
-    ]
-    return call(weights_kernel, shapes, ahead, back)
+WEIGHTS = [
+    jax.ShapeDtypeStruct((3, 3 * O, 3 * C), BF16),
+    jax.ShapeDtypeStruct((3, 3 * LANES, 3 * C), BF16),
+]
 
 
 def convs(packed, ahead, back):
     got = exchange(packed)
-    ahead_weight, back_weight = weights(ahead, back)
+    ahead_weight, back_weight = call(weights_kernel, WEIGHTS, ahead, back)
     up = shift(got[:, H - 1], "seq", 1)
     down = shift(got[:, 0], "seq", -1)
-    sums = call(
-        conv_kernel,
-        [jax.ShapeDtypeStruct((SIZE, O), F32), jax.ShapeDtypeStruct((SIZE, C), F32)],
+    own_ahead = call(
+        ahead_kernel,
+        jax.ShapeDtypeStruct((SIZE, O), F32),
         got,
         ahead_weight,
+        scratch=(pltpu.VMEM((WT, H * COLS, 3 * C), BF16),),
+        flops=2 * SIZE * 27 * C * LANES,
+    )
+    own_back = call(
+        back_kernel,
+        jax.ShapeDtypeStruct((SIZE, C), F32),
+        got,
         back_weight,
-        scratch=(
-            pltpu.VMEM((WT, H * COLS, 3 * C), BF16),
-            pltpu.VMEM((WT, H * COLS, 3 * LANES), BF16),
-        ),
-        flops=2 * SIZE * 27 * 2 * C * LANES,
+        scratch=(pltpu.VMEM((WT, H * COLS, 3 * LANES), BF16),),
+        flops=2 * SIZE * 27 * C * LANES,
     )
     summed = call(
         edge_kernel,
@@ -279,7 +316,8 @@
         down,
         ahead_weight,
         back_weight,
-        *sums,
+        own_ahead,
+        own_back,
         scratch=(
             pltpu.VMEM((2, WT, COLS, C), BF16),
             pltpu.VMEM((2, WT, COLS, LANES), BF16),
@@ -296,7 +334,21 @@
 
     before = shift(latent, "section", 1)
     after = shift(cotangent, "section", -1)
-    packed = call(pack_one_kernel, sent, gain_one, latent, before, cotangent, after)
+    packed = call(
+        pack_one_kernel,
+        sent,
+        gain_one,
+        before,
+        after,
+        latent,
+        cotangent,
+        scratch=(
+            pltpu.VMEM((T, H, W, C), BF16),
+            pltpu.VMEM((T, H, W, C), BF16),
+            pltpu.SemaphoreType.DMA((2,)),
+        ),
+        far=2,
+    )
     got = convs(packed, kernel_one, kernel_two)
     active, grad_inner = call(middle_kernel, [block, block], gain_two, got)
 

time: 125 us -> 120 us (0.960)
  local copies, waits for them, and re-layouts: 18 us -> 13.1 us
    unnamed x32, local copies, waits for them, and re-layouts: 17.2 us -> 12.4 us
    pallas_call x10 -> x12, Pallas kernels: 16.1 us -> 15.7 us  [call(): pl.pallas_call(kernel, out_shape=out_shape, in_specs=places(near, pltpu.V...]
  transfers between devices with their start and end apart: 11 -> 11, of which waited for: 6 -> 7; matrix products, arithmetic and copies ran while one was open for 1% -> 1% of each run, Pallas kernels for 7% -> 6%
where the time goes in v3:
time: 120 us; the launch traced here: 119 us
  waiting for transfers between devices  44.3 us (37%)
  starting transfers between devices  32.9 us (27%)
  Pallas kernels  15.7 us (13%)
  local copies, waits for them, and re-layouts  13.1 us (11%)
  blocking collectives  11.8 us (10%)
    all_to_all x3, waiting for transfers between devices, exchange(): lax.all_to_all(values, 'exp', split_axis=0, concat_axis=0, tiled=True)  26.4 us
    ppermute x8, starting transfers between devices, shift(): return lax.ppermute(values, axis, pairs)  21.8 us
    ppermute x8, waiting for transfers between devices, shift(): return lax.ppermute(values, axis, pairs)  17.9 us
    pallas_call x12, Pallas kernels, call(): pl.pallas_call(kernel, out_shape=out_shape, in_specs=places(near, pltpu.V...  15.7 us
    unnamed x32, local copies, waits for them, and re-layouts  12.4 us
    all_to_all x1, blocking collectives, exchange(): lax.all_to_all(values, 'exp', split_axis=0, concat_axis=0, tiled=True)  11.8 us
    all_to_all x3, starting transfers between devices, exchange(): lax.all_to_all(values, 'exp', split_axis=0, concat_axis=0, tiled=True)  11.1 us
  transfers between devices with their start and end apart: 11, of which 7 were waited for; matrix products, arithmetic and copies ran while one was open for 1% of the time, Pallas kernels for 6%

profile of v3, /device:TPU:1, one launch (start us, length us, event | category | flops | bytes accessed | tf_op | source)
XLA Modules:
  0.0 118.7 jit_solution(6514859287559457652)
XLA Ops:
  0.6 0.0 copy-start
  0.6 5.2 %collective-permute-start = (bf16[2,4,16,384]{3,2,1,0:T(8,128)(2,1)}, bf16[2,4,16,384]{3,2,1,0:T(8,128)(2,1)S(1)}, u32[]{:S(2)}, u32[]{:S(2)}) collective-permute-start(bf16[2,4,16,384]{3,2,1,0:T(8,128)(2,1)} %latent.1), channel_id=1, source_target_pairs={{0,128},{128,256},{256,384},{1,129},{129,257},{257,385},{2,130},{1... | collective-permute-start | bytes 294920 | tf_op jit(solution)/shard_map/ppermute | solution.py:263
  5.8 1.3 %collective-permute-start.1 = (bf16[2,4,16,384]{3,2,1,0:T(8,128)(2,1)}, bf16[2,4,16,384]{3,2,1,0:T(8,128)(2,1)S(1)}, u32[]{:S(2)}, u32[]{:S(2)}) collective-permute-start(bf16[2,4,16,384]{3,2,1,0:T(8,128)(2,1)} %cotangent.1), channel_id=1, source_target_pairs={{128,0},{256,128},{384,256},{129,1},{257,129},{385,257},{130,2},{2... | collective-permute-start | bytes 294920 | tf_op jit(solution)/shard_map/ppermute | solution.py:263
  7.1 0.7 reshape.10.gain
  7.8 0.0 collective-permute-done.before
  7.8 8.8 %collective-permute-done.1.after = bf16[2,4,16,384]{3,2,1,0:T(8,128)(2,1)S(1)} collective-permute-done((bf16[2,4,16,384]{3,2,1,0:T(8,128)(2,1)}, bf16[2,4,16,384]{3,2,1,0:T(8,128)(2,1)S(1)}, u32[]{:S(2)}, u32[]{:S(2)}) %collective-permute-start.1) | collective-permute-done | bytes 98336 | tf_op jit(solution)/shard_map/ppermute | solution.py:263
  16.6 2.2 %shard_map.77 = bf16[4,4,5,16,384]{4,3,2,1,0:T(8,128)(2,1)} custom-call(f32[1,384]{1,0:T(1,128)S(1)} %reshape.10.gain, bf16[2,4,16,384]{3,2,1,0:T(8,128)(2,1)S(1)} %collective-permute-done.before, bf16[2,4,16,384]{3,2,1,0:T(8,128)(2,1)S(1)} %collective-permute-done.1.after, bf16[2,4,16,384]{3,2,1,0:T(8,128)(2,1)} %latent.1, bf16[2,4,16,384]{3,2,1,0:T(8,128)(2,1)} %cotangent.1), custom_call_target="tpu_custom_call" | custom-call | bytes 1377792 | tf_op jit(solution)/shard_map/pallas_call | solution.py:31
  18.8 4.1 %all-to-all-start = ((bf16[4,4,5,16,384]{4,3,2,1,0:T(8,128)(2,1)}), bf16[4,4,5,16,384]{4,3,2,1,0:T(8,128)(2,1)S(1)}, u32[]{:S(2)}, u32[]{:S(2)}) async-start(bf16[4,4,5,16,384]{4,3,2,1,0:T(8,128)(2,1)} %shard_map.77), calls=%async_computation | async-start | bytes 1966080 | tf_op jit(solution)/shard_map/all_to_all | solution.py:267
  22.9 0.0 copy-done
  22.9 1.6 %copy-done.1 = bf16[3,3,3,96,384]{4,3,2,1,0:T(8,128)(2,1)S(1)} copy-done((bf16[3,3,3,96,384]{4,3,2,1,0:T(8,128)(2,1)S(1)}, bf16[3,3,3,96,384]{4,3,2,1,0:T(8,128)(2,1)}, u32[]{:S(2)}) %copy-start.1) | copy-done | bytes 1990680
  24.5 0.4 shard_map.78
  24.9 0.0 copy-start.3
  24.9 1.5 %copy-done.3 = bf16[3,384,1152]{2,1,0:T(8,128)(2,1)} copy-done((bf16[3,384,1152]{2,1,0:T(8,128)(2,1)}, bf16[3,384,1152]{2,1,0:T(8,128)(2,1)S(1)}, u32[]{:S(2)}) %copy-start.3) | copy-done | bytes 2654232
  26.4 1.3 %copy-done.9 = bf16[3,288,1152]{2,1,0:T(8,128)(2,1)} copy-done((bf16[3,288,1152]{2,1,0:T(8,128)(2,1)}, bf16[3,288,1152]{2,1,0:T(8,128)(2,1)S(1)}, u32[]{:S(2)}) %copy-start.9) | copy-done | bytes 1990680
  27.7 8.8 %all-to-all-done.got = bf16[4,4,5,16,384]{4,3,2,1,0:T(8,128)(2,1)S(1)} async-done(((bf16[4,4,5,16,384]{4,3,2,1,0:T(8,128)(2,1)}), bf16[4,4,5,16,384]{4,3,2,1,0:T(8,128)(2,1)S(1)}, u32[]{:S(2)}, u32[]{:S(2)}) %all-to-all-start) | async-done | bytes 983072 | tf_op jit(solution)/shard_map/all_to_all | solution.py:267
  36.5 0.1 slice_bitcast_fusion.2
  36.5 1.9 %collective-permute-start.2 = (bf16[4,5,16,384]{3,2,1,0:T(8,128)(2,1)S(1)}, bf16[4,5,16,384]{3,2,1,0:T(8,128)(2,1)S(1)}, u32[]{:S(2)}, u32[]{:S(2)}) collective-permute-start(bf16[4,5,16,384]{3,2,1,0:T(8,128)(2,1)S(1)} %get-tuple-element.17), channel_id=1, source_target_pairs={{0,4},{4,8},{8,12},{12,16},{16,20},{20,24},{24,28},{28,32},{32,36}... | collective-permute-start | bytes 737288 | tf_op jit(solution)/shard_map/ppermute | solution.py:263
  38.5 3.1 %collective-permute-start.3 = (bf16[4,5,16,384]{3,2,1,0:T(8,128)(2,1)S(1)}, bf16[4,5,16,384]{3,2,1,0:T(8,128)(2,1)S(1)}, u32[]{:S(2)}, u32[]{:S(2)}) collective-permute-start(bf16[4,5,16,384]{3,2,1,0:T(8,128)(2,1)S(1)} %get-tuple-element.16), channel_id=1, source_target_pairs={{4,0},{8,4},{12,8},{16,12},{20,16},{24,20},{28,24},{32,28},{36,32}... | collective-permute-start | bytes 737288 | tf_op jit(solution)/shard_map/ppermute | solution.py:263
  41.6 0.0 copy-start.4
  41.6 1.7 %copy-done.4 = bf16[3,384,1152]{2,1,0:T(8,128)(2,1)S(1)} copy-done((bf16[3,384,1152]{2,1,0:T(8,128)(2,1)S(1)}, bf16[3,384,1152]{2,1,0:T(8,128)(2,1)}, u32[]{:S(2)}) %copy-start.4) | copy-done | bytes 2654232
  43.3 1.9 %shard_map.80.back = f32[512,384]{1,0:T(8,128)S(1)} custom-call(bf16[4,4,5,16,384]{4,3,2,1,0:T(8,128)(2,1)S(1)} %all-to-all-done.got, bf16[3,384,1152]{2,1,0:T(8,128)(2,1)S(1)} %copy-done.4), custom_call_target="tpu_custom_call" | custom-call | flops 1358954496 | bytes 4423680 | tf_op jit(solution)/shard_map/pallas_call | solution.py:31
  45.2 0.0 copy-done.10
  45.2 0.0 copy-start.5
  45.2 1.6 %shard_map.79.ahead = f32[512,96]{1,0:T(8,128)S(1)} custom-call(bf16[4,4,5,16,384]{4,3,2,1,0:T(8,128)(2,1)S(1)} %all-to-all-done.got, bf16[3,288,1152]{2,1,0:T(8,128)(2,1)S(1)} %copy-done.10), custom_call_target="tpu_custom_call" | custom-call | flops 1358954496 | bytes 3170304 | tf_op jit(solution)/shard_map/pallas_call | solution.py:31
  46.8 0.0 copy-start.15
  46.8 0.0 collective-permute-done.2.up
  46.8 0.8 collective-permute-done.3.down
  47.7 0.0 copy-done.5
  47.7 2.0 %shard_map.81 = bf16[4,10,16,384]{3,2,1,0:T(8,128)(2,1)} custom-call(bf16[4,5,16,384]{3,2,1,0:T(8,128)(2,1)S(1)} %collective-permute-done.2.up, bf16[4,5,16,384]{3,2,1,0:T(8,128)(2,1)S(1)} %collective-permute-done.3.down, bf16[3,288,1152]{2,1,0:T(8,128)(2,1)S(1)} %copy-done.10, bf16[3,384,1152]{2,1,0:T(8,128)(2,1)S(1)} %copy-done.5, ...), custom_call_target="tpu_custom_call" | custom-call | flops 452984832 | bytes 6610944 | tf_op jit(solution)/shard_map/pallas_call | solution.py:31
  49.7 3.5 %all-to-all-start.1 = ((bf16[4,10,16,384]{3,2,1,0:T(8,128)(2,1)}), bf16[4,10,16,384]{3,2,1,0:T(8,128)(2,1)S(1)}, u32[]{:S(2)}, u32[]{:S(2)}) async-start(bf16[4,10,16,384]{3,2,1,0:T(8,128)(2,1)} %shard_map.81), calls=%async_computation.1 | async-start | bytes 983040 | tf_op jit(solution)/shard_map/all_to_all | solution.py:267
  53.2 0.0 copy-done.15
  53.2 8.5 %all-to-all-done.1.got = bf16[4,10,16,384]{3,2,1,0:T(8,128)(2,1)S(1)} async-done(((bf16[4,10,16,384]{3,2,1,0:T(8,128)(2,1)}), bf16[4,10,16,384]{3,2,1,0:T(8,128)(2,1)S(1)}, u32[]{:S(2)}, u32[]{:S(2)}) %all-to-all-start.1) | async-done | bytes 491552 | tf_op jit(solution)/shard_map/all_to_all | solution.py:267
  61.7 0.4 shard_map.82
  62.1 4.4 %collective-permute-start.4 = (bf16[2,4,16,384]{3,2,1,0:T(8,128)(2,1)S(1)}, bf16[2,4,16,384]{3,2,1,0:T(8,128)(2,1)S(1)}, u32[]{:S(2)}, u32[]{:S(2)}) collective-permute-start(bf16[2,4,16,384]{3,2,1,0:T(8,128)(2,1)S(1)} %get-tuple-element.10.own), channel_id=1, source_target_pairs={{0,128},{128,256},{256,384},{1,129},{129,257},{257,385},{2,130},{1... | collective-permute-start | bytes 294920 | tf_op jit(solution)/shard_map/ppermute | solution.py:263
  66.4 1.3 %collective-permute-start.5 = (bf16[2,4,16,384]{3,2,1,0:T(8,128)(2,1)S(1)}, bf16[2,4,16,384]{3,2,1,0:T(8,128)(2,1)S(1)}, u32[]{:S(2)}, u32[]{:S(2)}) collective-permute-start(bf16[2,4,16,384]{3,2,1,0:T(8,128)(2,1)S(1)} %get-tuple-element.11.grad), channel_id=1, source_target_pairs={{128,0},{256,128},{384,256},{129,1},{257,129},{385,257},{130,2},{2... | collective-permute-start | bytes 294920 | tf_op jit(solution)/shard_map/ppermute | solution.py:263
  67.7 1.3 %collective-permute-done.4.before = bf16[2,4,16,384]{3,2,1,0:T(8,128)(2,1)S(1)} collective-permute-done((bf16[2,4,16,384]{3,2,1,0:T(8,128)(2,1)S(1)}, bf16[2,4,16,384]{3,2,1,0:T(8,128)(2,1)S(1)}, u32[]{:S(2)}, u32[]{:S(2)}) %collective-permute-start.4) | collective-permute-done | bytes 98336 | tf_op jit(solution)/shard_map/ppermute | solution.py:263
  69.1 6.9 %collective-permute-done.5.after = bf16[2,4,16,384]{3,2,1,0:T(8,128)(2,1)S(1)} collective-permute-done((bf16[2,4,16,384]{3,2,1,0:T(8,128)(2,1)S(1)}, bf16[2,4,16,384]{3,2,1,0:T(8,128)(2,1)S(1)}, u32[]{:S(2)}, u32[]{:S(2)}) %collective-permute-start.5) | collective-permute-done | bytes 98336 | tf_op jit(solution)/shard_map/ppermute | solution.py:263
  76.0 1.1 shard_map.83
  77.1 3.5 %all-to-all-start.2 = ((bf16[4,4,5,16,384]{4,3,2,1,0:T(8,128)(2,1)}), bf16[4,4,5,16,384]{4,3,2,1,0:T(8,128)(2,1)S(1)}, u32[]{:S(2)}, u32[]{:S(2)}) async-start(bf16[4,4,5,16,384]{4,3,2,1,0:T(8,128)(2,1)} %shard_map.83), calls=%async_computation.2 | async-start | bytes 1966080 | tf_op jit(solution)/shard_map/all_to_all | solution.py:267
  80.6 0.0 copy-start.2
  80.6 1.5 %copy-done.2 = bf16[3,3,3,96,384]{4,3,2,1,0:T(8,128)(2,1)S(1)} copy-done((bf16[3,3,3,96,384]{4,3,2,1,0:T(8,128)(2,1)S(1)}, bf16[3,3,3,96,384]{4,3,2,1,0:T(8,128)(2,1)}, u32[]{:S(2)}) %copy-start.2) | copy-done | bytes 1990680
  82.2 0.4 shard_map.84
  82.6 0.0 copy-start.6
  82.6 1.5 %copy-done.6 = bf16[3,384,1152]{2,1,0:T(8,128)(2,1)} copy-done((bf16[3,384,1152]{2,1,0:T(8,128)(2,1)}, bf16[3,384,1152]{2,1,0:T(8,128)(2,1)S(1)}, u32[]{:S(2)}) %copy-start.6) | copy-done | bytes 2654232
  84.1 1.3 %copy-done.11 = bf16[3,288,1152]{2,1,0:T(8,128)(2,1)} copy-done((bf16[3,288,1152]{2,1,0:T(8,128)(2,1)}, bf16[3,288,1152]{2,1,0:T(8,128)(2,1)S(1)}, u32[]{:S(2)}) %copy-start.11) | copy-done | bytes 1990680
  85.4 9.1 %all-to-all-done.2.got = bf16[4,4,5,16,384]{4,3,2,1,0:T(8,128)(2,1)S(1)} async-done(((bf16[4,4,5,16,384]{4,3,2,1,0:T(8,128)(2,1)}), bf16[4,4,5,16,384]{4,3,2,1,0:T(8,128)(2,1)S(1)}, u32[]{:S(2)}, u32[]{:S(2)}) %all-to-all-start.2) | async-done | bytes 983072 | tf_op jit(solution)/shard_map/all_to_all | solution.py:267
  94.5 0.1 slice_bitcast_fusion
  94.6 1.9 %collective-permute-start.6 = (bf16[4,5,16,384]{3,2,1,0:T(8,128)(2,1)S(1)}, bf16[4,5,16,384]{3,2,1,0:T(8,128)(2,1)S(1)}, u32[]{:S(2)}, u32[]{:S(2)}) collective-permute-start(bf16[4,5,16,384]{3,2,1,0:T(8,128)(2,1)S(1)} %get-tuple-element.15), channel_id=1, source_target_pairs={{0,4},{4,8},{8,12},{12,16},{16,20},{20,24},{24,28},{28,32},{32,36}... | collective-permute-start | bytes 737288 | tf_op jit(solution)/shard_map/ppermute | solution.py:263
  96.5 2.7 %collective-permute-start.7 = (bf16[4,5,16,384]{3,2,1,0:T(8,128)(2,1)S(1)}, bf16[4,5,16,384]{3,2,1,0:T(8,128)(2,1)S(1)}, u32[]{:S(2)}, u32[]{:S(2)}) collective-permute-start(bf16[4,5,16,384]{3,2,1,0:T(8,128)(2,1)S(1)} %get-tuple-element.14), channel_id=1, source_target_pairs={{4,0},{8,4},{12,8},{16,12},{20,16},{24,20},{28,24},{32,28},{36,32}... | collective-permute-start | bytes 737288 | tf_op jit(solution)/shard_map/ppermute | solution.py:263
  99.2 0.0 copy-start.7
  99.2 1.7 %copy-done.7 = bf16[3,384,1152]{2,1,0:T(8,128)(2,1)S(1)} copy-done((bf16[3,384,1152]{2,1,0:T(8,128)(2,1)S(1)}, bf16[3,384,1152]{2,1,0:T(8,128)(2,1)}, u32[]{:S(2)}) %copy-start.7) | copy-done | bytes 2654232
  101.0 1.9 %shard_map.86.back = f32[512,384]{1,0:T(8,128)S(1)} custom-call(bf16[4,4,5,16,384]{4,3,2,1,0:T(8,128)(2,1)S(1)} %all-to-all-done.2.got, bf16[3,384,1152]{2,1,0:T(8,128)(2,1)S(1)} %copy-done.7), custom_call_target="tpu_custom_call" | custom-call | flops 1358954496 | bytes 4423680 | tf_op jit(solution)/shard_map/pallas_call | solution.py:31
  102.9 0.0 copy-done.12
  102.9 0.0 copy-start.8
  102.9 1.6 %shard_map.85.ahead = f32[512,96]{1,0:T(8,128)S(1)} custom-call(bf16[4,4,5,16,384]{4,3,2,1,0:T(8,128)(2,1)S(1)} %all-to-all-done.2.got, bf16[3,288,1152]{2,1,0:T(8,128)(2,1)S(1)} %copy-done.12), custom_call_target="tpu_custom_call" | custom-call | flops 1358954496 | bytes 3170304 | tf_op jit(solution)/shard_map/pallas_call | solution.py:31
  104.4 0.0 copy-start.13
  104.5 0.0 copy-start.14
  104.5 0.0 collective-permute-done.6.up
  104.5 0.0 collective-permute-done.7.down
  104.5 0.1 copy-done.8
  104.6 1.3 %shard_map.87 = bf16[4,10,16,384]{3,2,1,0:T(8,128)(2,1)S(1)} custom-call(bf16[4,5,16,384]{3,2,1,0:T(8,128)(2,1)S(1)} %collective-permute-done.6.up, bf16[4,5,16,384]{3,2,1,0:T(8,128)(2,1)S(1)} %collective-permute-done.7.down, bf16[3,288,1152]{2,1,0:T(8,128)(2,1)S(1)} %copy-done.12, bf16[3,384,1152]{2,1,0:T(8,128)(2,1)S(1)} %copy-done.8, ...), custom_call_target="tpu_custom_call" | custom-call | flops 452984832 | bytes 6610944 | tf_op jit(solution)/shard_map/pallas_call | solution.py:31
  105.9 11.8 %all_to_all.20.got = bf16[4,10,16,384]{3,2,1,0:T(8,128)(2,1)S(1)} all-to-all(bf16[4,10,16,384]{3,2,1,0:T(8,128)(2,1)S(1)} %shard_map.87), channel_id=1, replica_groups=mesh['section'=4,'seq'=32,'exp'=4] {'exp'}, dimensions={0} | all-to-all | bytes 983040 | tf_op jit(solution)/shard_map/all_to_all | solution.py:267
  117.6 0.0 copy-done.13
  117.6 1.0 shard_map.88
  (7 shorter events, 0.0 us)
Async XLA Ops:
  0.6 22.3 %copy-start = (bf16[3,3,3,96,384]{4,3,2,1,0:T(8,128)(2,1)S(1)}, bf16[3,3,3,96,384]{4,3,2,1,0:T(8,128)(2,1)}, u32[]{:S(2)}) copy-start(bf16[3,3,3,96,384]{4,3,2,1,0:T(8,128)(2,1)} %back.3) | copy-start | bytes 5971972
  0.6 7.2 %collective-permute-start = (bf16[2,4,16,384]{3,2,1,0:T(8,128)(2,1)}, bf16[2,4,16,384]{3,2,1,0:T(8,128)(2,1)S(1)}, u32[]{:S(2)}, u32[]{:S(2)}) collective-permute-start(bf16[2,4,16,384]{3,2,1,0:T(8,128)(2,1)} %latent.1), channel_id=1, source_target_pairs={{0,128},{128,256},{256,384},{1,129},{129,257},{257,385},{2,130},{1... | collective-permute-start | bytes 294920 | tf_op jit(solution)/shard_map/ppermute | solution.py:263
  5.8 10.8 %collective-permute-start.1 = (bf16[2,4,16,384]{3,2,1,0:T(8,128)(2,1)}, bf16[2,4,16,384]{3,2,1,0:T(8,128)(2,1)S(1)}, u32[]{:S(2)}, u32[]{:S(2)}) collective-permute-start(bf16[2,4,16,384]{3,2,1,0:T(8,128)(2,1)} %cotangent.1), channel_id=1, source_target_pairs={{128,0},{256,128},{384,256},{129,1},{257,129},{385,257},{130,2},{2... | collective-permute-start | bytes 294920 | tf_op jit(solution)/shard_map/ppermute | solution.py:263
  18.8 17.7 %all-to-all-start = ((bf16[4,4,5,16,384]{4,3,2,1,0:T(8,128)(2,1)}), bf16[4,4,5,16,384]{4,3,2,1,0:T(8,128)(2,1)S(1)}, u32[]{:S(2)}, u32[]{:S(2)}) async-start(bf16[4,4,5,16,384]{4,3,2,1,0:T(8,128)(2,1)} %shard_map.77), calls=%async_computation | async-start | bytes 1966080 | tf_op jit(solution)/shard_map/all_to_all | solution.py:267
  22.9 1.6 %copy-start.1 = (bf16[3,3,3,96,384]{4,3,2,1,0:T(8,128)(2,1)S(1)}, bf16[3,3,3,96,384]{4,3,2,1,0:T(8,128)(2,1)}, u32[]{:S(2)}) copy-start(bf16[3,3,3,96,384]{4,3,2,1,0:T(8,128)(2,1)} %ahead.3) | copy-start | bytes 5971972
  24.9 1.5 %copy-start.3 = (bf16[3,384,1152]{2,1,0:T(8,128)(2,1)}, bf16[3,384,1152]{2,1,0:T(8,128)(2,1)S(1)}, u32[]{:S(2)}) copy-start(bf16[3,384,1152]{2,1,0:T(8,128)(2,1)S(1)} %get-tuple-element.9.weight.back_weight) | copy-start | bytes 7962628
  26.4 1.3 %copy-start.9 = (bf16[3,288,1152]{2,1,0:T(8,128)(2,1)}, bf16[3,288,1152]{2,1,0:T(8,128)(2,1)S(1)}, u32[]{:S(2)}) copy-start(bf16[3,288,1152]{2,1,0:T(8,128)(2,1)S(1)} %get-tuple-element.8.weight.ahead_weight) | copy-start | bytes 5971972
  36.5 10.3 %collective-permute-start.2 = (bf16[4,5,16,384]{3,2,1,0:T(8,128)(2,1)S(1)}, bf16[4,5,16,384]{3,2,1,0:T(8,128)(2,1)S(1)}, u32[]{:S(2)}, u32[]{:S(2)}) collective-permute-start(bf16[4,5,16,384]{3,2,1,0:T(8,128)(2,1)S(1)} %get-tuple-element.17), channel_id=1, source_target_pairs={{0,4},{4,8},{8,12},{12,16},{16,20},{20,24},{24,28},{28,32},{32,36}... | collective-permute-start | bytes 737288 | tf_op jit(solution)/shard_map/ppermute | solution.py:263
  38.5 9.2 %collective-permute-start.3 = (bf16[4,5,16,384]{3,2,1,0:T(8,128)(2,1)S(1)}, bf16[4,5,16,384]{3,2,1,0:T(8,128)(2,1)S(1)}, u32[]{:S(2)}, u32[]{:S(2)}) collective-permute-start(bf16[4,5,16,384]{3,2,1,0:T(8,128)(2,1)S(1)} %get-tuple-element.16), channel_id=1, source_target_pairs={{4,0},{8,4},{12,8},{16,12},{20,16},{24,20},{28,24},{32,28},{36,32}... | collective-permute-start | bytes 737288 | tf_op jit(solution)/shard_map/ppermute | solution.py:263
  41.6 1.8 %copy-start.4 = (bf16[3,384,1152]{2,1,0:T(8,128)(2,1)S(1)}, bf16[3,384,1152]{2,1,0:T(8,128)(2,1)}, u32[]{:S(2)}) copy-start(bf16[3,384,1152]{2,1,0:T(8,128)(2,1)} %copy-done.3) | copy-start | bytes 7962628
  43.3 1.9 %copy-start.10 = (bf16[3,288,1152]{2,1,0:T(8,128)(2,1)S(1)}, bf16[3,288,1152]{2,1,0:T(8,128)(2,1)}, u32[]{:S(2)}) copy-start(bf16[3,288,1152]{2,1,0:T(8,128)(2,1)} %copy-done.9) | copy-start | bytes 5971972
  45.2 2.4 %copy-start.5 = (bf16[3,384,1152]{2,1,0:T(8,128)(2,1)S(1)}, bf16[3,384,1152]{2,1,0:T(8,128)(2,1)}, u32[]{:S(2)}) copy-start(bf16[3,384,1152]{2,1,0:T(8,128)(2,1)} %copy-done.3) | copy-start | bytes 7962628
  46.8 6.4 %copy-start.15 = (f32[384]{0:T(512)S(1)}, f32[384]{0:T(512)}, u32[]{:S(2)}) copy-start(f32[384]{0:T(512)} %param.9) | copy-start | bytes 4612
  49.7 12.0 %all-to-all-start.1 = ((bf16[4,10,16,384]{3,2,1,0:T(8,128)(2,1)}), bf16[4,10,16,384]{3,2,1,0:T(8,128)(2,1)S(1)}, u32[]{:S(2)}, u32[]{:S(2)}) async-start(bf16[4,10,16,384]{3,2,1,0:T(8,128)(2,1)} %shard_map.81), calls=%async_computation.1 | async-start | bytes 983040 | tf_op jit(solution)/shard_map/all_to_all | solution.py:267
  62.1 7.0 %collective-permute-start.4 = (bf16[2,4,16,384]{3,2,1,0:T(8,128)(2,1)S(1)}, bf16[2,4,16,384]{3,2,1,0:T(8,128)(2,1)S(1)}, u32[]{:S(2)}, u32[]{:S(2)}) collective-permute-start(bf16[2,4,16,384]{3,2,1,0:T(8,128)(2,1)S(1)} %get-tuple-element.10.own), channel_id=1, source_target_pairs={{0,128},{128,256},{256,384},{1,129},{129,257},{257,385},{2,130},{1... | collective-permute-start | bytes 294920 | tf_op jit(solution)/shard_map/ppermute | solution.py:263
  66.4 9.6 %collective-permute-start.5 = (bf16[2,4,16,384]{3,2,1,0:T(8,128)(2,1)S(1)}, bf16[2,4,16,384]{3,2,1,0:T(8,128)(2,1)S(1)}, u32[]{:S(2)}, u32[]{:S(2)}) collective-permute-start(bf16[2,4,16,384]{3,2,1,0:T(8,128)(2,1)S(1)} %get-tuple-element.11.grad), channel_id=1, source_target_pairs={{128,0},{256,128},{384,256},{129,1},{257,129},{385,257},{130,2},{2... | collective-permute-start | bytes 294920 | tf_op jit(solution)/shard_map/ppermute | solution.py:263
  77.1 17.4 %all-to-all-start.2 = ((bf16[4,4,5,16,384]{4,3,2,1,0:T(8,128)(2,1)}), bf16[4,4,5,16,384]{4,3,2,1,0:T(8,128)(2,1)S(1)}, u32[]{:S(2)}, u32[]{:S(2)}) async-start(bf16[4,4,5,16,384]{4,3,2,1,0:T(8,128)(2,1)} %shard_map.83), calls=%async_computation.2 | async-start | bytes 1966080 | tf_op jit(solution)/shard_map/all_to_all | solution.py:267
  80.6 1.6 %copy-start.2 = (bf16[3,3,3,96,384]{4,3,2,1,0:T(8,128)(2,1)S(1)}, bf16[3,3,3,96,384]{4,3,2,1,0:T(8,128)(2,1)}, u32[]{:S(2)}) copy-start(bf16[3,3,3,96,384]{4,3,2,1,0:T(8,128)(2,1)} %ahead.3) | copy-start | bytes 5971972
  82.6 1.5 %copy-start.6 = (bf16[3,384,1152]{2,1,0:T(8,128)(2,1)}, bf16[3,384,1152]{2,1,0:T(8,128)(2,1)S(1)}, u32[]{:S(2)}) copy-start(bf16[3,384,1152]{2,1,0:T(8,128)(2,1)S(1)} %get-tuple-element.13.weight.back_weight) | copy-start | bytes 7962628
  84.1 1.3 %copy-start.11 = (bf16[3,288,1152]{2,1,0:T(8,128)(2,1)}, bf16[3,288,1152]{2,1,0:T(8,128)(2,1)S(1)}, u32[]{:S(2)}) copy-start(bf16[3,288,1152]{2,1,0:T(8,128)(2,1)S(1)} %get-tuple-element.12.weight.ahead_weight) | copy-start | bytes 5971972
  94.6 9.9 %collective-permute-start.6 = (bf16[4,5,16,384]{3,2,1,0:T(8,128)(2,1)S(1)}, bf16[4,5,16,384]{3,2,1,0:T(8,128)(2,1)S(1)}, u32[]{:S(2)}, u32[]{:S(2)}) collective-permute-start(bf16[4,5,16,384]{3,2,1,0:T(8,128)(2,1)S(1)} %get-tuple-element.15), channel_id=1, source_target_pairs={{0,4},{4,8},{8,12},{12,16},{16,20},{20,24},{24,28},{28,32},{32,36}... | collective-permute-start | bytes 737288 | tf_op jit(solution)/shard_map/ppermute | solution.py:263
  96.5 8.0 %collective-permute-start.7 = (bf16[4,5,16,384]{3,2,1,0:T(8,128)(2,1)S(1)}, bf16[4,5,16,384]{3,2,1,0:T(8,128)(2,1)S(1)}, u32[]{:S(2)}, u32[]{:S(2)}) collective-permute-start(bf16[4,5,16,384]{3,2,1,0:T(8,128)(2,1)S(1)} %get-tuple-element.14), channel_id=1, source_target_pairs={{4,0},{8,4},{12,8},{16,12},{20,16},{24,20},{28,24},{32,28},{36,32}... | collective-permute-start | bytes 737288 | tf_op jit(solution)/shard_map/ppermute | solution.py:263
  99.2 1.8 %copy-start.7 = (bf16[3,384,1152]{2,1,0:T(8,128)(2,1)S(1)}, bf16[3,384,1152]{2,1,0:T(8,128)(2,1)}, u32[]{:S(2)}) copy-start(bf16[3,384,1152]{2,1,0:T(8,128)(2,1)} %copy-done.6) | copy-start | bytes 7962628
  101.0 1.9 %copy-start.12 = (bf16[3,288,1152]{2,1,0:T(8,128)(2,1)S(1)}, bf16[3,288,1152]{2,1,0:T(8,128)(2,1)}, u32[]{:S(2)}) copy-start(bf16[3,288,1152]{2,1,0:T(8,128)(2,1)} %copy-done.11) | copy-start | bytes 5971972
  102.9 1.8 %copy-start.8 = (bf16[3,384,1152]{2,1,0:T(8,128)(2,1)S(1)}, bf16[3,384,1152]{2,1,0:T(8,128)(2,1)}, u32[]{:S(2)}) copy-start(bf16[3,384,1152]{2,1,0:T(8,128)(2,1)} %copy-done.6) | copy-start | bytes 7962628
  104.4 13.2 %copy-start.13 = (bf16[2,4,16,384]{3,2,1,0:T(8,128)(2,1)S(1)}, bf16[2,4,16,384]{3,2,1,0:T(8,128)(2,1)}, u32[]{:S(2)}) copy-start(bf16[2,4,16,384]{3,2,1,0:T(8,128)(2,1)} %latent.1) | copy-start | bytes 294916
  104.5 13.2 %copy-start.14 = (bf16[2,4,16,384]{3,2,1,0:T(8,128)(2,1)S(1)}, bf16[2,4,16,384]{3,2,1,0:T(8,128)(2,1)}, u32[]{:S(2)}) copy-start(bf16[2,4,16,384]{3,2,1,0:T(8,128)(2,1)} %cotangent.1) | copy-start | bytes 294916

commit v4 on v3

--- a/solution.py
+++ b/solution.py
@@ -1,3 +1,4 @@
+import functools
 import jax
 import jax.numpy as jnp
 from jax import lax
@@ -22,17 +23,21 @@
     return [pl.BlockSpec(memory_space=space)] * count
 
 
-def call(kernel, out_shape, *operands, scratch=(), flops=0, far=0):
+def call(kernel, out_shape, *operands, scratch=(), flops=0, far=0, far_out=False):
     bytes_accessed = sum(a.size * a.dtype.itemsize for a in operands)
     outs = out_shape if isinstance(out_shape, (list, tuple)) else [out_shape]
     bytes_accessed += sum(a.size * a.dtype.itemsize for a in outs)
     near = len(operands) - far
+    out_specs = places(len(outs), pltpu.VMEM) if outs is out_shape else places(1, pltpu.VMEM)[0]
+    if far_out:
+        out_shape = pltpu.HBM(out_shape.shape, out_shape.dtype)
+        out_specs = pl.BlockSpec(memory_space=pltpu.HBM)
     pinned = [pltpu.with_memory_space_constraint(a, pltpu.HBM) for a in operands[near:]]
     return pl.pallas_call(
         kernel,
         out_shape=out_shape,
         in_specs=places(near, pltpu.VMEM) + places(far, pltpu.HBM),
-        out_specs=places(len(outs), pltpu.VMEM) if outs is out_shape else places(1, pltpu.VMEM)[0],
+        out_specs=out_specs,
         scratch_shapes=list(scratch),
         compiler_params=pltpu.CompilerParams(vmem_limit_bytes=40 * 1024 * 1024),
         cost_estimate=pl.CostEstimate(
@@ -69,40 +74,49 @@
         )
 
 
-def put_active(out, row, frame, block, scale):
+def activated(block, scale):
     normed, _ = normalize(block.astype(F32), scale)
-    block = (normed * sigmoid(normed)).astype(BF16)
+    return (normed * sigmoid(normed)).astype(BF16)
+
+
+def put_block(out, row, frame, block):
     for target in range(X):
         out[target, row, frame] = block
 
 
-def pack_one_kernel(gain, before, after, own_far, cot_far, out, own, cot, sems):
-    scale = gain[...]
+def own_kernel(gains, own_far, cot_far, active, cot, own, sems):
     copies = [
         pltpu.make_async_copy(own_far, own, sems.at[0]),
         pltpu.make_async_copy(cot_far, cot, sems.at[1]),
     ]
     for copy in copies:
         copy.start()
+    copies[0].wait()
+    scale = gains[0:1]
     for row in range(H):
         for frame in range(T):
-            put_active(out, row, frame, before[frame, row], scale)
-    copies[0].wait()
+            active[frame, row] = activated(own[frame, row], scale)
+    copies[1].wait()
+
+
+def pack_kernel(gains, before, own, cot, after, out_far, out, sems):
+    copies = []
     for row in range(H):
         for frame in range(T):
-            put_active(out, row, T + frame, own[frame, row], scale)
-    copies[1].wait()
-    for row in range(H):
+            block = before[frame, row]
+            put_block(out, row, frame, block if gains is None else activated(block, gains[0:1]))
+            put_block(out, row, T + frame, own[frame, row])
         put_slices(out, row, [cot[0, row], cot[1, row], after[0, row], after[1, row]])
-
-
-def pack_two_kernel(own, before, grad, after, out):
-    for row in range(H):
-        for frame in range(WT):
-            block = before[frame, row] if frame < 2 else own[frame - 2, row]
-            for target in range(X):
-                out[target, row, frame] = block
-        put_slices(out, row, [grad[0, row], grad[1, row], after[0, row], after[1, row]])
+        copies.append(pltpu.make_async_copy(out.at[:, row], out_far.at[:, row], sems.at[row]))
+        copies[row].start()
+    for copy in copies:
+        copy.wait()
+
+
+def pack(kernel, *operands):
+    sent = jax.ShapeDtypeStruct((X, H, KINDS, W, C), BF16)
+    scratch = (pltpu.VMEM(sent.shape, BF16), pltpu.SemaphoreType.DMA((H,)))
+    return call(kernel, sent, *operands, scratch=scratch, far_out=True)
 
 
 def shifted_sum(parts):
@@ -175,7 +189,23 @@
     out[...] = shifted_sum([total[:, tap * C : (tap + 1) * C] for tap in range(3)])
 
 
+INNER_ROWS = [(frame, row) for frame in range(T) for row in range(1, H - 1)]
+OUTER_ROWS = [(frame, row) for frame in range(T) for row in (0, H - 1)]
+BLOCKS = {place: block for block, place in enumerate(INNER_ROWS + OUTER_ROWS)}
+
+
 def edge_kernel(up, down, ahead_weight, back_weight, ahead, back, out, data, grads):
+    def put_back(frame, row, values):
+        values = values.astype(BF16)
+        for target in range(X):
+            out[target, BLOCKS[frame, row]] = values[target * W : (target + 1) * W]
+
+    def rows_of(values, frame, row):
+        start = (frame * H + row) * COLS
+        return values[start : start + COLS]
+
+    for frame, row in INNER_ROWS:
+        put_back(frame, row, rows_of(back, frame, row))
     ahead_parts, back_parts = [], []
     for side, rows in enumerate((up, down)):
         for part in range(X):
@@ -184,35 +214,34 @@
                 data[side, frame, place] = rows[part, frame]
                 grads[side, frame, place] = padded_slice(rows[part, WT], frame)
         tap = 2 * side
-        ahead_total = jnp.zeros((T * COLS, 3 * O), F32)
-        back_total = jnp.zeros((T * COLS, 3 * C), F32)
-        for time_tap in range(3):
-            ahead_total = ahead_total + ahead_dot(
-                data[side, time_tap : time_tap + T].reshape(T * COLS, C),
-                ahead_weight[time_tap, :, tap * C : (tap + 1) * C],
-            )
-            back_total = back_total + jnp.dot(
-                grads[side, time_tap : time_tap + T].reshape(T * COLS, LANES),
-                back_weight[time_tap, tap * LANES : (tap + 1) * LANES],
-                preferred_element_type=F32,
-            )
+        ahead_total = ahead_dot(
+            jnp.concatenate(
+                [data[side, time : time + T].reshape(T * COLS, C) for time in range(3)], axis=-1
+            ),
+            jnp.concatenate(
+                [ahead_weight[time, :, tap * C : (tap + 1) * C] for time in range(3)], axis=-1
+            ),
+        )
+        back_total = jnp.dot(
+            jnp.concatenate(
+                [grads[side, time : time + T].reshape(T * COLS, LANES) for time in range(3)],
+                axis=-1,
+            ),
+            jnp.concatenate(
+                [back_weight[time, tap * LANES : (tap + 1) * LANES] for time in range(3)], axis=0
+            ),
+            preferred_element_type=F32,
+        )
         ahead_parts.append(shifted_sum([ahead_total[:, k * O : (k + 1) * O] for k in range(3)]))
         back_parts.append(shifted_sum([back_total[:, k * C : (k + 1) * C] for k in range(3)]))
+    for frame, row in OUTER_ROWS:
+        part = back_parts[row // (H - 1)][frame * COLS : (frame + 1) * COLS]
+        put_back(frame, row, rows_of(back, frame, row) + part)
     for frame in range(T):
-        rows = []
-        for row in range(H):
-            start = (frame * H + row) * COLS
-            ahead_row = ahead[start : start + COLS]
-            back_row = back[start : start + COLS]
-            if row in (0, H - 1):
-                side, at = row // (H - 1), frame * COLS
-                ahead_row = ahead_row + ahead_parts[side][at : at + COLS]
-                back_row = back_row + back_parts[side][at : at + COLS]
-            rows.append(ahead_row.astype(BF16))
-            back_row = back_row.astype(BF16)
-            for target in range(X):
-                out[target, frame * H + row] = back_row[target * W : (target + 1) * W]
-        rows = jnp.concatenate(rows, axis=-1)
+        rows = [rows_of(ahead, frame, row) for row in range(H)]
+        for side, row in enumerate((0, H - 1)):
+            rows[row] = rows[row] + ahead_parts[side][frame * COLS : (frame + 1) * COLS]
+        rows = jnp.concatenate([row.astype(BF16) for row in rows], axis=-1)
         for target in range(X):
             out[target, T * H + frame] = rows[target * W : (target + 1) * W]
 
@@ -230,12 +259,12 @@
     ).astype(F32)
 
 
-def middle_kernel(gain, got, active, grad_inner):
-    scale = gain[...]
+def middle_kernel(gains, got, active, grad_inner):
+    scale = gains[1:2]
     for frame in range(T):
         for row in range(H):
             inner = arrived_conv(got, frame, row)
-            grad_two = arrived_grad(got, frame * H + row)
+            grad_two = arrived_grad(got, BLOCKS[frame, row])
             normed, inverse = normalize(inner, scale)
             active[frame, row] = (normed * sigmoid(normed)).astype(BF16)
             grad_inner[frame, row] = norm_backward(
@@ -243,14 +272,14 @@
             ).astype(BF16)
 
 
-def last_kernel(gain, latent, cotangent, got, block_out, latent_grad):
-    scale = gain[...]
+def last_kernel(gains, latent, cotangent, got, block_out, latent_grad):
+    scale = gains[0:1]
     for frame in range(T):
         for row in range(H):
             source = latent[frame, row].astype(F32)
             block_out[frame, row] = (source + arrived_conv(got, frame, row)).astype(BF16)
             normed, inverse = normalize(source, scale)
-            grad_one = arrived_grad(got, frame * H + row)
+            grad_one = arrived_grad(got, BLOCKS[frame, row])
             latent_grad[frame, row] = (
                 cotangent[frame, row].astype(F32)
                 + norm_backward(source, inverse, scale, grad_one * silu_slope(normed))
@@ -309,54 +338,47 @@
         scratch=(pltpu.VMEM((WT, H * COLS, 3 * LANES), BF16),),
         flops=2 * SIZE * 27 * C * LANES,
     )
+    summed = jax.ShapeDtypeStruct((X, BACK, W, C), BF16)
+    scratch = (pltpu.VMEM((2, WT, COLS, C), BF16), pltpu.VMEM((2, WT, COLS, LANES), BF16))
     summed = call(
         edge_kernel,
-        jax.ShapeDtypeStruct((X, BACK, W, C), BF16),
+        summed,
         up,
         down,
         ahead_weight,
         back_weight,
         own_ahead,
         own_back,
-        scratch=(
-            pltpu.VMEM((2, WT, COLS, C), BF16),
-            pltpu.VMEM((2, WT, COLS, LANES), BF16),
-        ),
+        scratch=scratch,
         flops=SIZE * 9 * 2 * C * LANES,
     )
     return exchange(summed)
 
 
 def body(latent, cotangent, gain_one, gain_two, kernel_one, kernel_two):
-    gain_one, gain_two = gain_one.reshape(1, C), gain_two.reshape(1, C)
+    gains = jnp.stack([gain_one, gain_two])
     block = jax.ShapeDtypeStruct((T, H, W, C), BF16)
-    sent = jax.ShapeDtypeStruct((X, H, KINDS, W, C), BF16)
 
     before = shift(latent, "section", 1)
     after = shift(cotangent, "section", -1)
-    packed = call(
-        pack_one_kernel,
-        sent,
-        gain_one,
-        before,
-        after,
+    active, cot = call(
+        own_kernel,
+        [block, block],
+        gains,
         latent,
         cotangent,
-        scratch=(
-            pltpu.VMEM((T, H, W, C), BF16),
-            pltpu.VMEM((T, H, W, C), BF16),
-            pltpu.SemaphoreType.DMA((2,)),
-        ),
+        scratch=(pltpu.VMEM((T, H, W, C), BF16), pltpu.SemaphoreType.DMA((2,))),
         far=2,
     )
+    packed = pack(pack_kernel, gains, before, active, cot, after)
     got = convs(packed, kernel_one, kernel_two)
-    active, grad_inner = call(middle_kernel, [block, block], gain_two, got)
+    active, grad_inner = call(middle_kernel, [block, block], gains, got)
 
     before = shift(active, "section", 1)
     after = shift(grad_inner, "section", -1)
-    packed = call(pack_two_kernel, sent, active, before, grad_inner, after)
+    packed = pack(functools.partial(pack_kernel, None), before, active, grad_inner, after)
     got = convs(packed, kernel_two, kernel_one)
-    return tuple(call(last_kernel, [block, block], gain_one, latent, cotangent, got))
+    return tuple(call(last_kernel, [block, block], gains, latent, cotangent, got))
 
 
 def solution(mesh):

time: 120 us -> 117 us (0.975)
  blocking collectives: 11.8 us -> 22.2 us
  waiting for transfers between devices: 44.3 us -> 34.6 us
  starting transfers between devices: 32.9 us -> 29.2 us
    all_to_all x1 -> x2, blocking collectives: 11.8 us -> 22.2 us  [exchange(): lax.all_to_all(values, 'exp', split_axis=0, concat_axis=0, tiled=True)]
    all_to_all x3 -> x2, waiting for transfers between devices: 26.4 us -> 18.1 us  [exchange(): lax.all_to_all(values, 'exp', split_axis=0, concat_axis=0, tiled=True)]
    all_to_all x3 -> x2, starting transfers between devices: 11.1 us -> 7.65 us  [exchange(): lax.all_to_all(values, 'exp', split_axis=0, concat_axis=0, tiled=True)]
    ppermute x8, waiting for transfers between devices: 17.9 us -> 16.5 us  [shift(): return lax.ppermute(values, axis, pairs)]
    another operation x0 -> x2, local copies, waits for them, and re-layouts: none -> 1.37 us  [body(): gains = jnp.stack([gain_one, gain_two])]
    pallas_call x12 -> x13, Pallas kernels: 15.7 us -> 14.5 us  [call(): pl.pallas_call(kernel, out_shape=out_shape, in_specs=places(near, pltpu.V...]
    unnamed x32 -> x26, local copies, waits for them, and re-layouts: 12.4 us -> 12.3 us
  transfers between devices with their start and end apart: 11 -> 10, of which waited for: 7 -> 7; matrix products, arithmetic and copies ran while one was open for 1% -> 1% of each run, Pallas kernels for 6% -> 8%
where the time goes in v4:
time: 117 us; the launch traced here: 115 us
  waiting for transfers between devices  34.6 us (30%)
  starting transfers between devices  29.2 us (25%)
  blocking collectives  22.2 us (19%)
  Pallas kernels  14.5 us (12%)
  local copies, waits for them, and re-layouts  13.7 us (12%)
    all_to_all x2, blocking collectives, exchange(): lax.all_to_all(values, 'exp', split_axis=0, concat_axis=0, tiled=True)  22.2 us
    ppermute x8, starting transfers between devices, shift(): return lax.ppermute(values, axis, pairs)  21.6 us
    all_to_all x2, waiting for transfers between devices, exchange(): lax.all_to_all(values, 'exp', split_axis=0, concat_axis=0, tiled=True)  18.1 us
    ppermute x8, waiting for transfers between devices, shift(): return lax.ppermute(values, axis, pairs)  16.5 us
    pallas_call x13, Pallas kernels, call(): pl.pallas_call(kernel, out_shape=out_shape, in_specs=places(near, pltpu.V...  14.5 us
    unnamed x26, local copies, waits for them, and re-layouts  12.3 us
    all_to_all x2, starting transfers between devices, exchange(): lax.all_to_all(values, 'exp', split_axis=0, concat_axis=0, tiled=True)  7.65 us
  transfers between devices with their start and end apart: 10, of which 7 were waited for; matrix products, arithmetic and copies ran while one was open for 1% of the time, Pallas kernels for 8%

profile of v4, /device:TPU:1, one launch (start us, length us, event | category | flops | bytes accessed | tf_op | source)
XLA Modules:
  0.0 115.1 jit_solution(13317545467289761719)
XLA Ops:
  0.6 0.0 copy-start
  0.6 5.2 %collective-permute-start = (bf16[2,4,16,384]{3,2,1,0:T(8,128)(2,1)}, bf16[2,4,16,384]{3,2,1,0:T(8,128)(2,1)S(1)}, u32[]{:S(2)}, u32[]{:S(2)}) collective-permute-start(bf16[2,4,16,384]{3,2,1,0:T(8,128)(2,1)} %latent.1), channel_id=1, source_target_pairs={{0,128},{128,256},{256,384},{1,129},{129,257},{257,385},{2,130},{1... | collective-permute-start | bytes 294920 | tf_op jit(solution)/shard_map/ppermute | solution.py:292
  5.8 1.3 %collective-permute-start.1 = (bf16[2,4,16,384]{3,2,1,0:T(8,128)(2,1)}, bf16[2,4,16,384]{3,2,1,0:T(8,128)(2,1)S(1)}, u32[]{:S(2)}, u32[]{:S(2)}) collective-permute-start(bf16[2,4,16,384]{3,2,1,0:T(8,128)(2,1)} %cotangent.1), channel_id=1, source_target_pairs={{128,0},{256,128},{384,256},{129,1},{257,129},{385,257},{130,2},{2... | collective-permute-start | bytes 294920 | tf_op jit(solution)/shard_map/ppermute | solution.py:292
  7.1 0.7 stack.10
  7.8 0.7 stack.9
  8.5 1.1 shard_map.77
  9.6 0.0 collective-permute-done.before
  9.6 7.0 %collective-permute-done.1.after = bf16[2,4,16,384]{3,2,1,0:T(8,128)(2,1)S(1)} collective-permute-done((bf16[2,4,16,384]{3,2,1,0:T(8,128)(2,1)}, bf16[2,4,16,384]{3,2,1,0:T(8,128)(2,1)S(1)}, u32[]{:S(2)}, u32[]{:S(2)}) %collective-permute-start.1) | collective-permute-done | bytes 98336 | tf_op jit(solution)/shard_map/ppermute | solution.py:292
  16.6 1.1 shard_map.78
  17.7 4.1 %all-to-all-start = ((bf16[4,4,5,16,384]{4,3,2,1,0:T(8,128)(2,1)}), bf16[4,4,5,16,384]{4,3,2,1,0:T(8,128)(2,1)S(1)}, u32[]{:S(2)}, u32[]{:S(2)}) async-start(bf16[4,4,5,16,384]{4,3,2,1,0:T(8,128)(2,1)} %shard_map.78), calls=%async_computation | async-start | bytes 1966080 | tf_op jit(solution)/shard_map/all_to_all | solution.py:296
  21.8 0.0 copy-done
  21.8 0.0 copy-start.1
  21.8 1.6 %copy-done.1 = bf16[3,3,3,96,384]{4,3,2,1,0:T(8,128)(2,1)S(1)} copy-done((bf16[3,3,3,96,384]{4,3,2,1,0:T(8,128)(2,1)S(1)}, bf16[3,3,3,96,384]{4,3,2,1,0:T(8,128)(2,1)}, u32[]{:S(2)}) %copy-start.1) | copy-done | bytes 1990680
  23.4 0.4 shard_map.79
  23.8 0.0 copy-start.3
  23.8 1.5 %copy-done.3 = bf16[3,384,1152]{2,1,0:T(8,128)(2,1)} copy-done((bf16[3,384,1152]{2,1,0:T(8,128)(2,1)}, bf16[3,384,1152]{2,1,0:T(8,128)(2,1)S(1)}, u32[]{:S(2)}) %copy-start.3) | copy-done | bytes 2654232
  25.3 0.0 copy-start.7
  25.3 1.3 %copy-done.7 = bf16[3,288,1152]{2,1,0:T(8,128)(2,1)} copy-done((bf16[3,288,1152]{2,1,0:T(8,128)(2,1)}, bf16[3,288,1152]{2,1,0:T(8,128)(2,1)S(1)}, u32[]{:S(2)}) %copy-start.7) | copy-done | bytes 1990680
  26.6 8.8 %all-to-all-done.got = bf16[4,4,5,16,384]{4,3,2,1,0:T(8,128)(2,1)S(1)} async-done(((bf16[4,4,5,16,384]{4,3,2,1,0:T(8,128)(2,1)}), bf16[4,4,5,16,384]{4,3,2,1,0:T(8,128)(2,1)S(1)}, u32[]{:S(2)}, u32[]{:S(2)}) %all-to-all-start) | async-done | bytes 983072 | tf_op jit(solution)/shard_map/all_to_all | solution.py:296
  35.4 0.1 slice_bitcast_fusion.2
  35.5 1.9 %collective-permute-start.2 = (bf16[4,5,16,384]{3,2,1,0:T(8,128)(2,1)S(1)}, bf16[4,5,16,384]{3,2,1,0:T(8,128)(2,1)S(1)}, u32[]{:S(2)}, u32[]{:S(2)}) collective-permute-start(bf16[4,5,16,384]{3,2,1,0:T(8,128)(2,1)S(1)} %get-tuple-element.21), channel_id=1, source_target_pairs={{0,4},{4,8},{8,12},{12,16},{16,20},{20,24},{24,28},{28,32},{32,36}... | collective-permute-start | bytes 737288 | tf_op jit(solution)/shard_map/ppermute | solution.py:292
  37.4 3.1 %collective-permute-start.3 = (bf16[4,5,16,384]{3,2,1,0:T(8,128)(2,1)S(1)}, bf16[4,5,16,384]{3,2,1,0:T(8,128)(2,1)S(1)}, u32[]{:S(2)}, u32[]{:S(2)}) collective-permute-start(bf16[4,5,16,384]{3,2,1,0:T(8,128)(2,1)S(1)} %get-tuple-element.20), channel_id=1, source_target_pairs={{4,0},{8,4},{12,8},{16,12},{20,16},{24,20},{28,24},{32,28},{36,32}... | collective-permute-start | bytes 737288 | tf_op jit(solution)/shard_map/ppermute | solution.py:292
  40.5 0.0 copy-start.8
  40.5 1.5 %copy-done.8 = bf16[3,288,1152]{2,1,0:T(8,128)(2,1)S(1)} copy-done((bf16[3,288,1152]{2,1,0:T(8,128)(2,1)S(1)}, bf16[3,288,1152]{2,1,0:T(8,128)(2,1)}, u32[]{:S(2)}) %copy-start.8) | copy-done | bytes 1990680
  42.0 0.0 copy-start.4
  42.0 1.5 %shard_map.80.ahead = f32[512,96]{1,0:T(8,128)S(1)} custom-call(bf16[4,4,5,16,384]{4,3,2,1,0:T(8,128)(2,1)S(1)} %all-to-all-done.got, bf16[3,288,1152]{2,1,0:T(8,128)(2,1)S(1)} %copy-done.8), custom_call_target="tpu_custom_call" | custom-call | flops 1358954496 | bytes 3170304 | tf_op jit(solution)/shard_map/pallas_call | solution.py:36
  43.6 0.2 copy-done.4
  43.8 1.9 %shard_map.81.back = f32[512,384]{1,0:T(8,128)S(1)} custom-call(bf16[4,4,5,16,384]{4,3,2,1,0:T(8,128)(2,1)S(1)} %all-to-all-done.got, bf16[3,384,1152]{2,1,0:T(8,128)(2,1)S(1)} %copy-done.4), custom_call_target="tpu_custom_call" | custom-call | flops 1358954496 | bytes 4423680 | tf_op jit(solution)/shard_map/pallas_call | solution.py:36
  45.7 0.0 collective-permute-done.2.up
  45.7 0.9 collective-permute-done.3.down
  46.6 1.1 shard_map.82
  47.6 10.8 %all_to_all.20.got = bf16[4,10,16,384]{3,2,1,0:T(8,128)(2,1)S(1)} all-to-all(bf16[4,10,16,384]{3,2,1,0:T(8,128)(2,1)S(1)} %shard_map.82), channel_id=1, replica_groups=mesh['section'=4,'seq'=32,'exp'=4] {'exp'}, dimensions={0} | all-to-all | bytes 983040 | tf_op jit(solution)/shard_map/all_to_all | solution.py:296
  58.4 0.4 shard_map.83
  58.8 4.4 %collective-permute-start.4 = (bf16[2,4,16,384]{3,2,1,0:T(8,128)(2,1)S(1)}, bf16[2,4,16,384]{3,2,1,0:T(8,128)(2,1)S(1)}, u32[]{:S(2)}, u32[]{:S(2)}) collective-permute-start(bf16[2,4,16,384]{3,2,1,0:T(8,128)(2,1)S(1)} %get-tuple-element.14.own), channel_id=1, source_target_pairs={{0,128},{128,256},{256,384},{1,129},{129,257},{257,385},{2,130},{1... | collective-permute-start | bytes 294920 | tf_op jit(solution)/shard_map/ppermute | solution.py:292
  63.2 1.3 %collective-permute-start.5 = (bf16[2,4,16,384]{3,2,1,0:T(8,128)(2,1)S(1)}, bf16[2,4,16,384]{3,2,1,0:T(8,128)(2,1)S(1)}, u32[]{:S(2)}, u32[]{:S(2)}) collective-permute-start(bf16[2,4,16,384]{3,2,1,0:T(8,128)(2,1)S(1)} %get-tuple-element.15.cot), channel_id=1, source_target_pairs={{128,0},{256,128},{384,256},{129,1},{257,129},{385,257},{130,2},{2... | collective-permute-start | bytes 294920 | tf_op jit(solution)/shard_map/ppermute | solution.py:292
  64.5 1.1 collective-permute-done.4.before
  65.6 7.3 %collective-permute-done.5.after = bf16[2,4,16,384]{3,2,1,0:T(8,128)(2,1)S(1)} collective-permute-done((bf16[2,4,16,384]{3,2,1,0:T(8,128)(2,1)S(1)}, bf16[2,4,16,384]{3,2,1,0:T(8,128)(2,1)S(1)}, u32[]{:S(2)}, u32[]{:S(2)}) %collective-permute-start.5) | collective-permute-done | bytes 98336 | tf_op jit(solution)/shard_map/ppermute | solution.py:292
  72.9 1.1 shard_map.84
  74.0 3.5 %all-to-all-start.2 = ((bf16[4,4,5,16,384]{4,3,2,1,0:T(8,128)(2,1)}), bf16[4,4,5,16,384]{4,3,2,1,0:T(8,128)(2,1)S(1)}, u32[]{:S(2)}, u32[]{:S(2)}) async-start(bf16[4,4,5,16,384]{4,3,2,1,0:T(8,128)(2,1)} %shard_map.84), calls=%async_computation.2 | async-start | bytes 1966080 | tf_op jit(solution)/shard_map/all_to_all | solution.py:296
  77.5 0.0 copy-start.2
  77.5 1.5 %copy-done.2 = bf16[3,3,3,96,384]{4,3,2,1,0:T(8,128)(2,1)S(1)} copy-done((bf16[3,3,3,96,384]{4,3,2,1,0:T(8,128)(2,1)S(1)}, bf16[3,3,3,96,384]{4,3,2,1,0:T(8,128)(2,1)}, u32[]{:S(2)}) %copy-start.2) | copy-done | bytes 1990680
  79.1 0.4 shard_map.85
  79.4 0.0 copy-start.5
  79.5 1.5 %copy-done.5 = bf16[3,384,1152]{2,1,0:T(8,128)(2,1)} copy-done((bf16[3,384,1152]{2,1,0:T(8,128)(2,1)}, bf16[3,384,1152]{2,1,0:T(8,128)(2,1)S(1)}, u32[]{:S(2)}) %copy-start.5) | copy-done | bytes 2654232
  81.0 0.0 copy-start.9
  81.0 1.3 %copy-done.9 = bf16[3,288,1152]{2,1,0:T(8,128)(2,1)} copy-done((bf16[3,288,1152]{2,1,0:T(8,128)(2,1)}, bf16[3,288,1152]{2,1,0:T(8,128)(2,1)S(1)}, u32[]{:S(2)}) %copy-start.9) | copy-done | bytes 1990680
  82.3 9.3 %all-to-all-done.2.got = bf16[4,4,5,16,384]{4,3,2,1,0:T(8,128)(2,1)S(1)} async-done(((bf16[4,4,5,16,384]{4,3,2,1,0:T(8,128)(2,1)}), bf16[4,4,5,16,384]{4,3,2,1,0:T(8,128)(2,1)S(1)}, u32[]{:S(2)}, u32[]{:S(2)}) %all-to-all-start.2) | async-done | bytes 983072 | tf_op jit(solution)/shard_map/all_to_all | solution.py:296
  91.6 0.1 slice_bitcast_fusion
  91.6 2.4 %collective-permute-start.6 = (bf16[4,5,16,384]{3,2,1,0:T(8,128)(2,1)S(1)}, bf16[4,5,16,384]{3,2,1,0:T(8,128)(2,1)S(1)}, u32[]{:S(2)}, u32[]{:S(2)}) collective-permute-start(bf16[4,5,16,384]{3,2,1,0:T(8,128)(2,1)S(1)} %get-tuple-element.19), channel_id=1, source_target_pairs={{0,4},{4,8},{8,12},{12,16},{16,20},{20,24},{24,28},{28,32},{32,36}... | collective-permute-start | bytes 737288 | tf_op jit(solution)/shard_map/ppermute | solution.py:292
  94.1 2.0 %collective-permute-start.7 = (bf16[4,5,16,384]{3,2,1,0:T(8,128)(2,1)S(1)}, bf16[4,5,16,384]{3,2,1,0:T(8,128)(2,1)S(1)}, u32[]{:S(2)}, u32[]{:S(2)}) collective-permute-start(bf16[4,5,16,384]{3,2,1,0:T(8,128)(2,1)S(1)} %get-tuple-element.18), channel_id=1, source_target_pairs={{4,0},{8,4},{12,8},{16,12},{20,16},{24,20},{28,24},{32,28},{36,32}... | collective-permute-start | bytes 737288 | tf_op jit(solution)/shard_map/ppermute | solution.py:292
  96.1 0.0 copy-start.10
  96.1 1.5 %copy-done.10 = bf16[3,288,1152]{2,1,0:T(8,128)(2,1)S(1)} copy-done((bf16[3,288,1152]{2,1,0:T(8,128)(2,1)S(1)}, bf16[3,288,1152]{2,1,0:T(8,128)(2,1)}, u32[]{:S(2)}) %copy-start.10) | copy-done | bytes 1990680
  97.6 1.5 %shard_map.86.ahead = f32[512,96]{1,0:T(8,128)S(1)} custom-call(bf16[4,4,5,16,384]{4,3,2,1,0:T(8,128)(2,1)S(1)} %all-to-all-done.2.got, bf16[3,288,1152]{2,1,0:T(8,128)(2,1)S(1)} %copy-done.10), custom_call_target="tpu_custom_call" | custom-call | flops 1358954496 | bytes 3170304 | tf_op jit(solution)/shard_map/pallas_call | solution.py:36
  99.2 0.2 copy-done.6
  99.4 1.9 %shard_map.87.back = f32[512,384]{1,0:T(8,128)S(1)} custom-call(bf16[4,4,5,16,384]{4,3,2,1,0:T(8,128)(2,1)S(1)} %all-to-all-done.2.got, bf16[3,384,1152]{2,1,0:T(8,128)(2,1)S(1)} %copy-done.6), custom_call_target="tpu_custom_call" | custom-call | flops 1358954496 | bytes 4423680 | tf_op jit(solution)/shard_map/pallas_call | solution.py:36
  101.3 0.0 copy-start.11
  101.3 0.0 copy-start.12
  101.3 0.0 collective-permute-done.6.up
  101.3 0.2 collective-permute-done.7.down
  101.6 1.1 shard_map.88
  102.7 11.4 %all_to_all.21.got = bf16[4,10,16,384]{3,2,1,0:T(8,128)(2,1)S(1)} all-to-all(bf16[4,10,16,384]{3,2,1,0:T(8,128)(2,1)S(1)} %shard_map.88), channel_id=1, replica_groups=mesh['section'=4,'seq'=32,'exp'=4] {'exp'}, dimensions={0} | all-to-all | bytes 983040 | tf_op jit(solution)/shard_map/all_to_all | solution.py:296
  114.1 0.0 copy-done.11
  114.1 0.0 copy-done.12
  114.1 1.0 shard_map.89
  (2 shorter events, 0.0 us)
Async XLA Ops:
  0.6 21.2 %copy-start = (bf16[3,3,3,96,384]{4,3,2,1,0:T(8,128)(2,1)S(1)}, bf16[3,3,3,96,384]{4,3,2,1,0:T(8,128)(2,1)}, u32[]{:S(2)}) copy-start(bf16[3,3,3,96,384]{4,3,2,1,0:T(8,128)(2,1)} %back.3) | copy-start | bytes 5971972
  0.6 9.0 %collective-permute-start = (bf16[2,4,16,384]{3,2,1,0:T(8,128)(2,1)}, bf16[2,4,16,384]{3,2,1,0:T(8,128)(2,1)S(1)}, u32[]{:S(2)}, u32[]{:S(2)}) collective-permute-start(bf16[2,4,16,384]{3,2,1,0:T(8,128)(2,1)} %latent.1), channel_id=1, source_target_pairs={{0,128},{128,256},{256,384},{1,129},{129,257},{257,385},{2,130},{1... | collective-permute-start | bytes 294920 | tf_op jit(solution)/shard_map/ppermute | solution.py:292
  5.8 10.8 %collective-permute-start.1 = (bf16[2,4,16,384]{3,2,1,0:T(8,128)(2,1)}, bf16[2,4,16,384]{3,2,1,0:T(8,128)(2,1)S(1)}, u32[]{:S(2)}, u32[]{:S(2)}) collective-permute-start(bf16[2,4,16,384]{3,2,1,0:T(8,128)(2,1)} %cotangent.1), channel_id=1, source_target_pairs={{128,0},{256,128},{384,256},{129,1},{257,129},{385,257},{130,2},{2... | collective-permute-start | bytes 294920 | tf_op jit(solution)/shard_map/ppermute | solution.py:292
  17.7 17.7 %all-to-all-start = ((bf16[4,4,5,16,384]{4,3,2,1,0:T(8,128)(2,1)}), bf16[4,4,5,16,384]{4,3,2,1,0:T(8,128)(2,1)S(1)}, u32[]{:S(2)}, u32[]{:S(2)}) async-start(bf16[4,4,5,16,384]{4,3,2,1,0:T(8,128)(2,1)} %shard_map.78), calls=%async_computation | async-start | bytes 1966080 | tf_op jit(solution)/shard_map/all_to_all | solution.py:296
  21.8 1.6 %copy-start.1 = (bf16[3,3,3,96,384]{4,3,2,1,0:T(8,128)(2,1)S(1)}, bf16[3,3,3,96,384]{4,3,2,1,0:T(8,128)(2,1)}, u32[]{:S(2)}) copy-start(bf16[3,3,3,96,384]{4,3,2,1,0:T(8,128)(2,1)} %ahead.3) | copy-start | bytes 5971972
  23.8 1.5 %copy-start.3 = (bf16[3,384,1152]{2,1,0:T(8,128)(2,1)}, bf16[3,384,1152]{2,1,0:T(8,128)(2,1)S(1)}, u32[]{:S(2)}) copy-start(bf16[3,384,1152]{2,1,0:T(8,128)(2,1)S(1)} %get-tuple-element.13.weight.back_weight) | copy-start | bytes 7962628
  25.3 1.3 %copy-start.7 = (bf16[3,288,1152]{2,1,0:T(8,128)(2,1)}, bf16[3,288,1152]{2,1,0:T(8,128)(2,1)S(1)}, u32[]{:S(2)}) copy-start(bf16[3,288,1152]{2,1,0:T(8,128)(2,1)S(1)} %get-tuple-element.12.weight.ahead_weight) | copy-start | bytes 5971972
  35.5 10.2 %collective-permute-start.2 = (bf16[4,5,16,384]{3,2,1,0:T(8,128)(2,1)S(1)}, bf16[4,5,16,384]{3,2,1,0:T(8,128)(2,1)S(1)}, u32[]{:S(2)}, u32[]{:S(2)}) collective-permute-start(bf16[4,5,16,384]{3,2,1,0:T(8,128)(2,1)S(1)} %get-tuple-element.21), channel_id=1, source_target_pairs={{0,4},{4,8},{8,12},{12,16},{16,20},{20,24},{24,28},{28,32},{32,36}... | collective-permute-start | bytes 737288 | tf_op jit(solution)/shard_map/ppermute | solution.py:292
  37.4 9.2 %collective-permute-start.3 = (bf16[4,5,16,384]{3,2,1,0:T(8,128)(2,1)S(1)}, bf16[4,5,16,384]{3,2,1,0:T(8,128)(2,1)S(1)}, u32[]{:S(2)}, u32[]{:S(2)}) collective-permute-start(bf16[4,5,16,384]{3,2,1,0:T(8,128)(2,1)S(1)} %get-tuple-element.20), channel_id=1, source_target_pairs={{4,0},{8,4},{12,8},{16,12},{20,16},{24,20},{28,24},{32,28},{36,32}... | collective-permute-start | bytes 737288 | tf_op jit(solution)/shard_map/ppermute | solution.py:292
  40.5 1.6 %copy-start.8 = (bf16[3,288,1152]{2,1,0:T(8,128)(2,1)S(1)}, bf16[3,288,1152]{2,1,0:T(8,128)(2,1)}, u32[]{:S(2)}) copy-start(bf16[3,288,1152]{2,1,0:T(8,128)(2,1)} %copy-done.7) | copy-start | bytes 5971972
  42.0 1.7 %copy-start.4 = (bf16[3,384,1152]{2,1,0:T(8,128)(2,1)S(1)}, bf16[3,384,1152]{2,1,0:T(8,128)(2,1)}, u32[]{:S(2)}) copy-start(bf16[3,384,1152]{2,1,0:T(8,128)(2,1)} %copy-done.3) | copy-start | bytes 7962628
  58.8 6.7 %collective-permute-start.4 = (bf16[2,4,16,384]{3,2,1,0:T(8,128)(2,1)S(1)}, bf16[2,4,16,384]{3,2,1,0:T(8,128)(2,1)S(1)}, u32[]{:S(2)}, u32[]{:S(2)}) collective-permute-start(bf16[2,4,16,384]{3,2,1,0:T(8,128)(2,1)S(1)} %get-tuple-element.14.own), channel_id=1, source_target_pairs={{0,128},{128,256},{256,384},{1,129},{129,257},{257,385},{2,130},{1... | collective-permute-start | bytes 294920 | tf_op jit(solution)/shard_map/ppermute | solution.py:292
  63.2 9.7 %collective-permute-start.5 = (bf16[2,4,16,384]{3,2,1,0:T(8,128)(2,1)S(1)}, bf16[2,4,16,384]{3,2,1,0:T(8,128)(2,1)S(1)}, u32[]{:S(2)}, u32[]{:S(2)}) collective-permute-start(bf16[2,4,16,384]{3,2,1,0:T(8,128)(2,1)S(1)} %get-tuple-element.15.cot), channel_id=1, source_target_pairs={{128,0},{256,128},{384,256},{129,1},{257,129},{385,257},{130,2},{2... | collective-permute-start | bytes 294920 | tf_op jit(solution)/shard_map/ppermute | solution.py:292
  74.0 17.6 %all-to-all-start.2 = ((bf16[4,4,5,16,384]{4,3,2,1,0:T(8,128)(2,1)}), bf16[4,4,5,16,384]{4,3,2,1,0:T(8,128)(2,1)S(1)}, u32[]{:S(2)}, u32[]{:S(2)}) async-start(bf16[4,4,5,16,384]{4,3,2,1,0:T(8,128)(2,1)} %shard_map.84), calls=%async_computation.2 | async-start | bytes 1966080 | tf_op jit(solution)/shard_map/all_to_all | solution.py:296
  77.5 1.6 %copy-start.2 = (bf16[3,3,3,96,384]{4,3,2,1,0:T(8,128)(2,1)S(1)}, bf16[3,3,3,96,384]{4,3,2,1,0:T(8,128)(2,1)}, u32[]{:S(2)}) copy-start(bf16[3,3,3,96,384]{4,3,2,1,0:T(8,128)(2,1)} %ahead.3) | copy-start | bytes 5971972
  79.4 1.5 %copy-start.5 = (bf16[3,384,1152]{2,1,0:T(8,128)(2,1)}, bf16[3,384,1152]{2,1,0:T(8,128)(2,1)S(1)}, u32[]{:S(2)}) copy-start(bf16[3,384,1152]{2,1,0:T(8,128)(2,1)S(1)} %get-tuple-element.17.weight.back_weight) | copy-start | bytes 7962628
  81.0 1.3 %copy-start.9 = (bf16[3,288,1152]{2,1,0:T(8,128)(2,1)}, bf16[3,288,1152]{2,1,0:T(8,128)(2,1)S(1)}, u32[]{:S(2)}) copy-start(bf16[3,288,1152]{2,1,0:T(8,128)(2,1)S(1)} %get-tuple-element.16.weight.ahead_weight) | copy-start | bytes 5971972
  91.6 9.7 %collective-permute-start.6 = (bf16[4,5,16,384]{3,2,1,0:T(8,128)(2,1)S(1)}, bf16[4,5,16,384]{3,2,1,0:T(8,128)(2,1)S(1)}, u32[]{:S(2)}, u32[]{:S(2)}) collective-permute-start(bf16[4,5,16,384]{3,2,1,0:T(8,128)(2,1)S(1)} %get-tuple-element.19), channel_id=1, source_target_pairs={{0,4},{4,8},{8,12},{12,16},{16,20},{20,24},{24,28},{28,32},{32,36}... | collective-permute-start | bytes 737288 | tf_op jit(solution)/shard_map/ppermute | solution.py:292
  94.1 7.5 %collective-permute-start.7 = (bf16[4,5,16,384]{3,2,1,0:T(8,128)(2,1)S(1)}, bf16[4,5,16,384]{3,2,1,0:T(8,128)(2,1)S(1)}, u32[]{:S(2)}, u32[]{:S(2)}) collective-permute-start(bf16[4,5,16,384]{3,2,1,0:T(8,128)(2,1)S(1)} %get-tuple-element.18), channel_id=1, source_target_pairs={{4,0},{8,4},{12,8},{16,12},{20,16},{24,20},{28,24},{32,28},{36,32}... | collective-permute-start | bytes 737288 | tf_op jit(solution)/shard_map/ppermute | solution.py:292
  96.1 1.6 %copy-start.10 = (bf16[3,288,1152]{2,1,0:T(8,128)(2,1)S(1)}, bf16[3,288,1152]{2,1,0:T(8,128)(2,1)}, u32[]{:S(2)}) copy-start(bf16[3,288,1152]{2,1,0:T(8,128)(2,1)} %copy-done.9) | copy-start | bytes 5971972
  97.6 1.7 %copy-start.6 = (bf16[3,384,1152]{2,1,0:T(8,128)(2,1)S(1)}, bf16[3,384,1152]{2,1,0:T(8,128)(2,1)}, u32[]{:S(2)}) copy-start(bf16[3,384,1152]{2,1,0:T(8,128)(2,1)} %copy-done.5) | copy-start | bytes 7962628
  101.3 12.8 %copy-start.11 = (bf16[2,4,16,384]{3,2,1,0:T(8,128)(2,1)S(1)}, bf16[2,4,16,384]{3,2,1,0:T(8,128)(2,1)}, u32[]{:S(2)}) copy-start(bf16[2,4,16,384]{3,2,1,0:T(8,128)(2,1)} %latent.1) | copy-start | bytes 294916
  101.3 12.8 %copy-start.12 = (bf16[2,4,16,384]{3,2,1,0:T(8,128)(2,1)S(1)}, bf16[2,4,16,384]{3,2,1,0:T(8,128)(2,1)}, u32[]{:S(2)}) copy-start(bf16[2,4,16,384]{3,2,1,0:T(8,128)(2,1)} %cotangent.1) | copy-start | bytes 294916

commit v5 on v4

--- a/solution.py
+++ b/solution.py
@@ -138,26 +138,47 @@
     return jnp.concatenate([block[:, frame * O : (frame + 1) * O], zeros], axis=-1)
 
 
-def own_taps():
-    return [
-        (tap, row, row + 1 - tap) for tap in range(3) for row in range(H) if 0 <= row + 1 - tap < H
-    ]
-
-
-def clear_borders(operand, width):
-    for tap, row in ((0, 0), (2, H - 1)):
-        place = slice(row * COLS, (row + 1) * COLS)
-        for frame in range(WT):
-            operand[frame, place, tap * width : (tap + 1) * width] = jnp.zeros((COLS, width), BF16)
-
-
-def ahead_kernel(got, weight, out, data):
-    for tap, row, target in own_taps():
+OWN = {1: range(0, H), 2: range(2, H + 2)}
+FLAGS = {1: {(0, 3): 0, (2, 4): 0}, 2: {(0, 0): 1, (2, 5): 0}}
+
+
+def taps(phase, own):
+    found = []
+    for tap in range(3):
+        for row in range(H + 2):
+            target = row - tap
+            if 0 <= target < H and (row in OWN[phase]) == own:
+                flag = FLAGS[phase].get((tap, row)) if target in (0, 2, 3) else None
+                found.append((tap, row, target, flag))
+    return found
+
+
+def masked(block, flags, flag):
+    if flag is None:
+        return block
+    return block * flags[flag : flag + 1, : block.shape[1]].astype(BF16)
+
+
+def clear_borders(operand, width, phase):
+    given = [(tap, target) for tap, _, target, _ in taps(phase, True)]
+    for tap in range(3):
+        for row in range(H):
+            if (tap, row) not in given:
+                place = slice(row * COLS, (row + 1) * COLS)
+                for frame in range(WT):
+                    operand[frame, place, tap * width : (tap + 1) * width] = jnp.zeros(
+                        (COLS, width), BF16
+                    )
+
+
+def ahead_kernel(phase, flags, got, weight, out, data):
+    for tap, row, target, flag in taps(phase, True):
         for part in range(X):
             place = slice(target * COLS + part * W, target * COLS + (part + 1) * W)
             for frame in range(WT):
-                data[frame, place, tap * C : (tap + 1) * C] = got[part, row, frame]
-    clear_borders(data, C)
+                block = masked(got[part, row - OWN[phase][0], frame], flags, flag)
+                data[frame, place, tap * C : (tap + 1) * C] = block
+    clear_borders(data, C, phase)
     total = jnp.zeros((3 * O, SIZE), F32)
     for time_tap in range(3):
         total = total + ahead_dot(
@@ -169,17 +190,18 @@
     out[...] = (low + total[O : 2 * O] + high).T
 
 
-def back_kernel(got, weight, out, grads):
-    for row in range(H):
+def back_kernel(phase, flags, got, weight, out, grads):
+    for row in OWN[phase]:
         for part in range(X):
-            block = got[part, row, WT]
+            block = got[part, row - OWN[phase][0], WT]
             pieces = [padded_slice(block, frame) for frame in range(WT)]
-            for tap, source, target in own_taps():
+            for tap, source, target, flag in taps(phase, True):
                 if source == row:
                     place = slice(target * COLS + part * W, target * COLS + (part + 1) * W)
                     for frame in range(WT):
-                        grads[frame, place, tap * LANES : (tap + 1) * LANES] = pieces[frame]
-    clear_borders(grads, LANES)
+                        piece = masked(pieces[frame], flags, flag)
+                        grads[frame, place, tap * LANES : (tap + 1) * LANES] = piece
+    clear_borders(grads, LANES, phase)
     operand = jnp.concatenate(
         [grads[tap : tap + T].reshape(SIZE, 3 * LANES) for tap in range(3)], axis=-1
     )
@@ -189,61 +211,63 @@
     out[...] = shifted_sum([total[:, tap * C : (tap + 1) * C] for tap in range(3)])
 
 
-INNER_ROWS = [(frame, row) for frame in range(T) for row in range(1, H - 1)]
-OUTER_ROWS = [(frame, row) for frame in range(T) for row in (0, H - 1)]
-BLOCKS = {place: block for block, place in enumerate(INNER_ROWS + OUTER_ROWS)}
-
-
-def edge_kernel(up, down, ahead_weight, back_weight, ahead, back, out, data, grads):
-    def put_back(frame, row, values):
-        values = values.astype(BF16)
-        for target in range(X):
-            out[target, BLOCKS[frame, row]] = values[target * W : (target + 1) * W]
-
-    def rows_of(values, frame, row):
-        start = (frame * H + row) * COLS
-        return values[start : start + COLS]
-
-    for frame, row in INNER_ROWS:
-        put_back(frame, row, rows_of(back, frame, row))
-    ahead_parts, back_parts = [], []
-    for side, rows in enumerate((up, down)):
+def edge_kernel(
+    phase, flags, rows, ahead_weight, back_weight, ahead, back, out, data, grads
+):
+    pairs = taps(phase, False)
+    for number, (_, row, _, flag) in enumerate(pairs):
+        near = row - (H if phase == 1 else 0)
         for part in range(X):
             place = slice(part * W, (part + 1) * W)
             for frame in range(WT):
-                data[side, frame, place] = rows[part, frame]
-                grads[side, frame, place] = padded_slice(rows[part, WT], frame)
-        tap = 2 * side
-        ahead_total = ahead_dot(
+                data[number, frame, place] = masked(rows[part, near, frame], flags, flag)
+                piece = padded_slice(rows[part, near, WT], frame)
+                grads[number, frame, place] = masked(piece, flags, flag)
+    ahead_parts, back_parts = {}, {}
+    for target in sorted({pair[2] for pair in pairs}):
+        terms = [
+            (number, pair[0], time)
+            for number, pair in enumerate(pairs)
+            if pair[2] == target
+            for time in range(3)
+        ]
+        size = T * COLS
+        total = ahead_dot(
             jnp.concatenate(
-                [data[side, time : time + T].reshape(T * COLS, C) for time in range(3)], axis=-1
+                [data[n, time : time + T].reshape(size, C) for n, _, time in terms], axis=-1
             ),
             jnp.concatenate(
-                [ahead_weight[time, :, tap * C : (tap + 1) * C] for time in range(3)], axis=-1
+                [ahead_weight[time, :, tap * C : (tap + 1) * C] for _, tap, time in terms], axis=-1
             ),
         )
-        back_total = jnp.dot(
+        ahead_parts[target] = shifted_sum([total[:, k * O : (k + 1) * O] for k in range(3)])
+        total = jnp.dot(
             jnp.concatenate(
-                [grads[side, time : time + T].reshape(T * COLS, LANES) for time in range(3)],
-                axis=-1,
+                [grads[n, time : time + T].reshape(size, LANES) for n, _, time in terms], axis=-1
             ),
             jnp.concatenate(
-                [back_weight[time, tap * LANES : (tap + 1) * LANES] for time in range(3)], axis=0
+                [back_weight[time, tap * LANES : (tap + 1) * LANES] for _, tap, time in terms],
+                axis=0,
             ),
             preferred_element_type=F32,
         )
-        ahead_parts.append(shifted_sum([ahead_total[:, k * O : (k + 1) * O] for k in range(3)]))
-        back_parts.append(shifted_sum([back_total[:, k * C : (k + 1) * C] for k in range(3)]))
-    for frame, row in OUTER_ROWS:
-        part = back_parts[row // (H - 1)][frame * COLS : (frame + 1) * COLS]
-        put_back(frame, row, rows_of(back, frame, row) + part)
+        back_parts[target] = shifted_sum([total[:, k * C : (k + 1) * C] for k in range(3)])
     for frame in range(T):
-        rows = [rows_of(ahead, frame, row) for row in range(H)]
-        for side, row in enumerate((0, H - 1)):
-            rows[row] = rows[row] + ahead_parts[side][frame * COLS : (frame + 1) * COLS]
-        rows = jnp.concatenate([row.astype(BF16) for row in rows], axis=-1)
+        packed = []
+        for row in range(H):
+            start = (frame * H + row) * COLS
+            ahead_row, back_row = ahead[start : start + COLS], back[start : start + COLS]
+            if row in ahead_parts:
+                at = frame * COLS
+                ahead_row = ahead_row + ahead_parts[row][at : at + COLS]
+                back_row = back_row + back_parts[row][at : at + COLS]
+            packed.append(ahead_row.astype(BF16))
+            back_row = back_row.astype(BF16)
+            for target in range(X):
+                out[target, frame * H + row] = back_row[target * W : (target + 1) * W]
+        packed = jnp.concatenate(packed, axis=-1)
         for target in range(X):
-            out[target, T * H + frame] = rows[target * W : (target + 1) * W]
+            out[target, T * H + frame] = packed[target * W : (target + 1) * W]
 
 
 def arrived_grad(got, block):
@@ -264,7 +288,7 @@
     for frame in range(T):
         for row in range(H):
             inner = arrived_conv(got, frame, row)
-            grad_two = arrived_grad(got, BLOCKS[frame, row])
+            grad_two = arrived_grad(got, frame * H + row)
             normed, inverse = normalize(inner, scale)
             active[frame, row] = (normed * sigmoid(normed)).astype(BF16)
             grad_inner[frame, row] = norm_backward(
@@ -279,16 +303,16 @@
             source = latent[frame, row].astype(F32)
             block_out[frame, row] = (source + arrived_conv(got, frame, row)).astype(BF16)
             normed, inverse = normalize(source, scale)
-            grad_one = arrived_grad(got, BLOCKS[frame, row])
+            grad_one = arrived_grad(got, frame * H + row)
             latent_grad[frame, row] = (
                 cotangent[frame, row].astype(F32)
                 + norm_backward(source, inverse, scale, grad_one * silu_slope(normed))
             ).astype(BF16)
 
 
-def shift(values, axis, by):
+def shift(values, axis, by, wrap=False):
     size = lax.axis_size(axis)
-    pairs = [(i, i + by) for i in range(size) if 0 <= i + by < size]
+    pairs = [(i, (i + by) % size) for i in range(size) if wrap or 0 <= i + by < size]
     return lax.ppermute(values, axis, pairs)
 
 
@@ -317,34 +341,36 @@
 ]
 
 
-def convs(packed, ahead, back):
+def convs(phase, flags, packed, ahead, back):
     got = exchange(packed)
     ahead_weight, back_weight = call(weights_kernel, WEIGHTS, ahead, back)
-    up = shift(got[:, H - 1], "seq", 1)
-    down = shift(got[:, 0], "seq", -1)
+    sent = got[:, :2] if phase == 1 else got[:, H - 2 :]
+    rows = shift(sent, "seq", -1 if phase == 1 else 1, wrap=True)
     own_ahead = call(
-        ahead_kernel,
+        functools.partial(ahead_kernel, phase),
         jax.ShapeDtypeStruct((SIZE, O), F32),
+        flags,
         got,
         ahead_weight,
         scratch=(pltpu.VMEM((WT, H * COLS, 3 * C), BF16),),
         flops=2 * SIZE * 27 * C * LANES,
     )
     own_back = call(
-        back_kernel,
+        functools.partial(back_kernel, phase),
         jax.ShapeDtypeStruct((SIZE, C), F32),
+        flags,
         got,
         back_weight,
         scratch=(pltpu.VMEM((WT, H * COLS, 3 * LANES), BF16),),
         flops=2 * SIZE * 27 * C * LANES,
     )
     summed = jax.ShapeDtypeStruct((X, BACK, W, C), BF16)
-    scratch = (pltpu.VMEM((2, WT, COLS, C), BF16), pltpu.VMEM((2, WT, COLS, LANES), BF16))
+    scratch = (pltpu.VMEM((3, WT, COLS, C), BF16), pltpu.VMEM((3, WT, COLS, LANES), BF16))
     summed = call(
-        edge_kernel,
+        functools.partial(edge_kernel, phase),
         summed,
-        up,
-        down,
+        flags,
+        rows,
         ahead_weight,
         back_weight,
         own_ahead,
@@ -357,6 +383,9 @@
 
 def body(latent, cotangent, gain_one, gain_two, kernel_one, kernel_two):
     gains = jnp.stack([gain_one, gain_two])
+    place = lax.axis_index("seq")
+    flags = jnp.stack([place != lax.axis_size("seq") - 1, place != 0]).astype(F32)
+    flags = jnp.broadcast_to(flags[:, None], (2, C))
     block = jax.ShapeDtypeStruct((T, H, W, C), BF16)
 
     before = shift(latent, "section", 1)
@@ -371,13 +400,13 @@
         far=2,
     )
     packed = pack(pack_kernel, gains, before, active, cot, after)
-    got = convs(packed, kernel_one, kernel_two)
+    got = convs(1, flags, packed, kernel_one, kernel_two)
     active, grad_inner = call(middle_kernel, [block, block], gains, got)
 
     before = shift(active, "section", 1)
     after = shift(grad_inner, "section", -1)
     packed = pack(functools.partial(pack_kernel, None), before, active, grad_inner, after)
-    got = convs(packed, kernel_two, kernel_one)
+    got = convs(2, flags, packed, kernel_two, kernel_one)
     return tuple(call(last_kernel, [block, block], gains, latent, cotangent, got))
 
 

time: 117 us -> 116 us (level)
  the two profiles are of different devices: /device:TPU:1 before, /device:TPU:256 now
where the time goes in v5:
time: 116 us; the launch traced here: 115 us
  blocking collectives  58.7 us (51%)
  waiting for transfers between devices  21.2 us (18%)
  starting transfers between devices  15.2 us (13%)
  Pallas kernels  15.1 us (13%)
  local copies, waits for them, and re-layouts  3.9 us (3%)
    all_to_all x4, blocking collectives, exchange(): lax.all_to_all(values, 'exp', split_axis=0, concat_axis=0, tiled=True)  58.7 us
    ppermute x6, waiting for transfers between devices, shift(): return lax.ppermute(values, axis, pairs)  21.2 us
    ppermute x6, starting transfers between devices, shift(): return lax.ppermute(values, axis, pairs)  15.2 us
    pallas_call x13, Pallas kernels, call(): pl.pallas_call(kernel, out_shape=out_shape, in_specs=places(near, pltpu.V...  15.1 us
  transfers between devices with their start and end apart: 6, of which 5 were waited for; matrix products, arithmetic and copies ran while one was open for 1% of the time, Pallas kernels for 8%

profile of v5, /device:TPU:256, one launch (start us, length us, event | category | flops | bytes accessed | tf_op | source)
XLA Modules:
  0.0 115.0 jit_solution(11670935615726987700)
XLA Ops:
  0.6 4.5 %collective-permute-start = (bf16[2,4,16,384]{3,2,1,0:T(8,128)(2,1)}, bf16[2,4,16,384]{3,2,1,0:T(8,128)(2,1)S(1)}, u32[]{:S(2)}, u32[]{:S(2)}) collective-permute-start(bf16[2,4,16,384]{3,2,1,0:T(8,128)(2,1)} %latent.1), channel_id=1, source_target_pairs={{0,128},{128,256},{256,384},{1,129},{129,257},{257,385},{2,130},{1... | collective-permute-start | bytes 294920 | tf_op jit(solution)/shard_map/ppermute | solution.py:316
  5.1 1.3 %collective-permute-start.1 = (bf16[2,4,16,384]{3,2,1,0:T(8,128)(2,1)}, bf16[2,4,16,384]{3,2,1,0:T(8,128)(2,1)S(1)}, u32[]{:S(2)}, u32[]{:S(2)}) collective-permute-start(bf16[2,4,16,384]{3,2,1,0:T(8,128)(2,1)} %cotangent.1), channel_id=1, source_target_pairs={{128,0},{256,128},{384,256},{129,1},{257,129},{385,257},{130,2},{2... | collective-permute-start | bytes 294920 | tf_op jit(solution)/shard_map/ppermute | solution.py:316
  6.4 0.7 stack.18
  7.1 0.7 stack.19
  7.8 1.1 shard_map.77
  8.9 0.0 collective-permute-done.before
  8.9 6.8 %collective-permute-done.1.after = bf16[2,4,16,384]{3,2,1,0:T(8,128)(2,1)S(1)} collective-permute-done((bf16[2,4,16,384]{3,2,1,0:T(8,128)(2,1)}, bf16[2,4,16,384]{3,2,1,0:T(8,128)(2,1)S(1)}, u32[]{:S(2)}, u32[]{:S(2)}) %collective-permute-start.1) | collective-permute-done | bytes 98336 | tf_op jit(solution)/shard_map/ppermute | solution.py:316
  15.7 0.0 copy-start
  15.7 1.1 shard_map.78
  16.8 18.8 %all_to_all.20.got = bf16[4,4,5,16,384]{4,3,2,1,0:T(8,128)(2,1)S(1)} all-to-all(bf16[4,4,5,16,384]{4,3,2,1,0:T(8,128)(2,1)} %shard_map.78), channel_id=1, replica_groups=mesh['section'=4,'seq'=32,'exp'=4] {'exp'}, dimensions={0} | all-to-all | bytes 1966080 | tf_op jit(solution)/shard_map/all_to_all | solution.py:320
  35.5 0.8 slice.8
  36.4 1.9 %collective-permute-start.2 = (bf16[4,2,5,16,384]{4,3,2,1,0:T(8,128)(2,1)}, bf16[4,2,5,16,384]{4,3,2,1,0:T(8,128)(2,1)S(1)}, u32[]{:S(2)}, u32[]{:S(2)}) collective-permute-start(bf16[4,2,5,16,384]{4,3,2,1,0:T(8,128)(2,1)} %slice.8), channel_id=1, source_target_pairs={{0,124},{4,0},{8,4},{12,8},{16,12},{20,16},{24,20},{28,24},{32,28}... | collective-permute-start | bytes 1474568 | tf_op jit(solution)/shard_map/ppermute | solution.py:316
  38.3 0.0 copy-done
  38.3 0.0 copy-start.1
  38.3 1.5 %copy-done.1 = bf16[3,3,3,96,384]{4,3,2,1,0:T(8,128)(2,1)S(1)} copy-done((bf16[3,3,3,96,384]{4,3,2,1,0:T(8,128)(2,1)S(1)}, bf16[3,3,3,96,384]{4,3,2,1,0:T(8,128)(2,1)}, u32[]{:S(2)}) %copy-start.1) | copy-done | bytes 1990680
  39.9 0.4 shard_map.79
  40.3 0.1 add_convert_fusion
  40.3 0.1 broadcast_in_dim.2.flags
  40.4 1.9 %shard_map.81.back = f32[512,384]{1,0:T(8,128)S(1)} custom-call(f32[2,384]{1,0:T(2,128)S(1)} %broadcast_in_dim.2.flags, bf16[4,4,5,16,384]{4,3,2,1,0:T(8,128)(2,1)S(1)} %all_to_all.20.got, bf16[3,384,1152]{2,1,0:T(8,128)(2,1)S(1)} %get-tuple-element.13.weight.back_weight), custom_call_target="tpu_custom_call" | custom-call | flops 1358954496 | bytes 4426752 | tf_op jit(solution)/shard_map/pallas_call | solution.py:36
  42.3 1.6 %shard_map.80.ahead = f32[512,96]{1,0:T(8,128)S(1)} custom-call(f32[2,384]{1,0:T(2,128)S(1)} %broadcast_in_dim.2.flags, bf16[4,4,5,16,384]{4,3,2,1,0:T(8,128)(2,1)S(1)} %all_to_all.20.got, bf16[3,288,1152]{2,1,0:T(8,128)(2,1)S(1)} %get-tuple-element.12.weight.ahead_weight), custom_call_target="tpu_custom_call" | custom-call | flops 1358954496 | bytes 3173376 | tf_op jit(solution)/shard_map/pallas_call | solution.py:36
  43.9 1.0 collective-permute-done.2.rows
  44.9 1.4 %shard_map.82 = bf16[4,10,16,384]{3,2,1,0:T(8,128)(2,1)S(1)} custom-call(f32[2,384]{1,0:T(2,128)S(1)} %broadcast_in_dim.2.flags, bf16[4,2,5,16,384]{4,3,2,1,0:T(8,128)(2,1)S(1)} %collective-permute-done.2.rows, bf16[3,288,1152]{2,1,0:T(8,128)(2,1)S(1)} %get-tuple-element.12.weight.ahead_weight, ...), custom_call_target="tpu_custom_call" | custom-call | flops 452984832 | bytes 6614016 | tf_op jit(solution)/shard_map/pallas_call | solution.py:36
  46.4 12.5 %all_to_all.21.got = bf16[4,10,16,384]{3,2,1,0:T(8,128)(2,1)S(1)} all-to-all(bf16[4,10,16,384]{3,2,1,0:T(8,128)(2,1)S(1)} %shard_map.82), channel_id=1, replica_groups=mesh['section'=4,'seq'=32,'exp'=4] {'exp'}, dimensions={0} | all-to-all | bytes 983040 | tf_op jit(solution)/shard_map/all_to_all | solution.py:320
  58.8 0.4 shard_map.83
  59.2 4.2 %collective-permute-start.3 = (bf16[2,4,16,384]{3,2,1,0:T(8,128)(2,1)S(1)}, bf16[2,4,16,384]{3,2,1,0:T(8,128)(2,1)S(1)}, u32[]{:S(2)}, u32[]{:S(2)}) collective-permute-start(bf16[2,4,16,384]{3,2,1,0:T(8,128)(2,1)S(1)} %get-tuple-element.14.own), channel_id=1, source_target_pairs={{0,128},{128,256},{256,384},{1,129},{129,257},{257,385},{2,130},{1... | collective-permute-start | bytes 294920 | tf_op jit(solution)/shard_map/ppermute | solution.py:316
  63.4 0.0 copy-start.2
  63.4 1.4 %collective-permute-start.4 = (bf16[2,4,16,384]{3,2,1,0:T(8,128)(2,1)S(1)}, bf16[2,4,16,384]{3,2,1,0:T(8,128)(2,1)S(1)}, u32[]{:S(2)}, u32[]{:S(2)}) collective-permute-start(bf16[2,4,16,384]{3,2,1,0:T(8,128)(2,1)S(1)} %get-tuple-element.15.cot), channel_id=1, source_target_pairs={{128,0},{256,128},{384,256},{129,1},{257,129},{385,257},{130,2},{2... | collective-permute-start | bytes 294920 | tf_op jit(solution)/shard_map/ppermute | solution.py:316
  64.8 0.7 collective-permute-done.3.before
  65.6 6.2 %collective-permute-done.4.after = bf16[2,4,16,384]{3,2,1,0:T(8,128)(2,1)S(1)} collective-permute-done((bf16[2,4,16,384]{3,2,1,0:T(8,128)(2,1)S(1)}, bf16[2,4,16,384]{3,2,1,0:T(8,128)(2,1)S(1)}, u32[]{:S(2)}, u32[]{:S(2)}) %collective-permute-start.4) | collective-permute-done | bytes 98336 | tf_op jit(solution)/shard_map/ppermute | solution.py:316
  71.7 1.1 shard_map.84
  72.8 17.2 %all_to_all.22.got = bf16[4,4,5,16,384]{4,3,2,1,0:T(8,128)(2,1)S(1)} all-to-all(bf16[4,4,5,16,384]{4,3,2,1,0:T(8,128)(2,1)} %shard_map.84), channel_id=1, replica_groups=mesh['section'=4,'seq'=32,'exp'=4] {'exp'}, dimensions={0} | all-to-all | bytes 1966080 | tf_op jit(solution)/shard_map/all_to_all | solution.py:320
  90.0 0.1 slice.9
  90.0 1.9 %collective-permute-start.5 = (bf16[4,2,5,16,384]{4,3,2,1,0:T(8,128)(2,1)S(1)}, bf16[4,2,5,16,384]{4,3,2,1,0:T(8,128)(2,1)S(1)}, u32[]{:S(2)}, u32[]{:S(2)}) collective-permute-start(bf16[4,2,5,16,384]{4,3,2,1,0:T(8,128)(2,1)S(1)} %slice.9), channel_id=1, source_target_pairs={{0,4},{4,8},{8,12},{12,16},{16,20},{20,24},{24,28},{28,32},{32,36}... | collective-permute-start | bytes 1474568 | tf_op jit(solution)/shard_map/ppermute | solution.py:316
  91.9 0.0 copy-done.2
  91.9 0.4 shard_map.85
  92.3 1.9 %shard_map.87.back = f32[512,384]{1,0:T(8,128)S(1)} custom-call(f32[2,384]{1,0:T(2,128)S(1)} %broadcast_in_dim.2.flags, bf16[4,4,5,16,384]{4,3,2,1,0:T(8,128)(2,1)S(1)} %all_to_all.22.got, bf16[3,384,1152]{2,1,0:T(8,128)(2,1)S(1)} %get-tuple-element.17.weight.back_weight), custom_call_target="tpu_custom_call" | custom-call | flops 1358954496 | bytes 4426752 | tf_op jit(solution)/shard_map/pallas_call | solution.py:36
  94.2 1.5 %shard_map.86.ahead = f32[512,96]{1,0:T(8,128)S(1)} custom-call(f32[2,384]{1,0:T(2,128)S(1)} %broadcast_in_dim.2.flags, bf16[4,4,5,16,384]{4,3,2,1,0:T(8,128)(2,1)S(1)} %all_to_all.22.got, bf16[3,288,1152]{2,1,0:T(8,128)(2,1)S(1)} %get-tuple-element.16.weight.ahead_weight), custom_call_target="tpu_custom_call" | custom-call | flops 1358954496 | bytes 3173376 | tf_op jit(solution)/shard_map/pallas_call | solution.py:36
  95.8 0.0 copy-start.3
  95.8 0.0 copy-start.4
  95.8 6.5 %collective-permute-done.5.rows = bf16[4,2,5,16,384]{4,3,2,1,0:T(8,128)(2,1)S(1)} collective-permute-done((bf16[4,2,5,16,384]{4,3,2,1,0:T(8,128)(2,1)S(1)}, bf16[4,2,5,16,384]{4,3,2,1,0:T(8,128)(2,1)S(1)}, u32[]{:S(2)}, u32[]{:S(2)}) %collective-permute-start.5) | collective-permute-done | bytes 491552 | tf_op jit(solution)/shard_map/ppermute | solution.py:316
  102.3 1.4 %shard_map.88 = bf16[4,10,16,384]{3,2,1,0:T(8,128)(2,1)S(1)} custom-call(f32[2,384]{1,0:T(2,128)S(1)} %broadcast_in_dim.2.flags, bf16[4,2,5,16,384]{4,3,2,1,0:T(8,128)(2,1)S(1)} %collective-permute-done.5.rows, bf16[3,288,1152]{2,1,0:T(8,128)(2,1)S(1)} %get-tuple-element.16.weight.ahead_weight, ...), custom_call_target="tpu_custom_call" | custom-call | flops 452984832 | bytes 6614016 | tf_op jit(solution)/shard_map/pallas_call | solution.py:36
  103.6 10.3 %all_to_all.23.got = bf16[4,10,16,384]{3,2,1,0:T(8,128)(2,1)S(1)} all-to-all(bf16[4,10,16,384]{3,2,1,0:T(8,128)(2,1)S(1)} %shard_map.88), channel_id=1, replica_groups=mesh['section'=4,'seq'=32,'exp'=4] {'exp'}, dimensions={0} | all-to-all | bytes 983040 | tf_op jit(solution)/shard_map/all_to_all | solution.py:320
  113.9 0.0 copy-done.3
  113.9 0.0 copy-done.4
  113.9 1.0 shard_map.89
  (1 shorter events, 0.0 us)
Async XLA Ops:
  0.6 8.3 %collective-permute-start = (bf16[2,4,16,384]{3,2,1,0:T(8,128)(2,1)}, bf16[2,4,16,384]{3,2,1,0:T(8,128)(2,1)S(1)}, u32[]{:S(2)}, u32[]{:S(2)}) collective-permute-start(bf16[2,4,16,384]{3,2,1,0:T(8,128)(2,1)} %latent.1), channel_id=1, source_target_pairs={{0,128},{128,256},{256,384},{1,129},{129,257},{257,385},{2,130},{1... | collective-permute-start | bytes 294920 | tf_op jit(solution)/shard_map/ppermute | solution.py:316
  5.1 10.5 %collective-permute-start.1 = (bf16[2,4,16,384]{3,2,1,0:T(8,128)(2,1)}, bf16[2,4,16,384]{3,2,1,0:T(8,128)(2,1)S(1)}, u32[]{:S(2)}, u32[]{:S(2)}) collective-permute-start(bf16[2,4,16,384]{3,2,1,0:T(8,128)(2,1)} %cotangent.1), channel_id=1, source_target_pairs={{128,0},{256,128},{384,256},{129,1},{257,129},{385,257},{130,2},{2... | collective-permute-start | bytes 294920 | tf_op jit(solution)/shard_map/ppermute | solution.py:316
  15.7 22.6 %copy-start = (bf16[3,3,3,96,384]{4,3,2,1,0:T(8,128)(2,1)S(1)}, bf16[3,3,3,96,384]{4,3,2,1,0:T(8,128)(2,1)}, u32[]{:S(2)}) copy-start(bf16[3,3,3,96,384]{4,3,2,1,0:T(8,128)(2,1)} %back.3) | copy-start | bytes 5971972
  36.4 8.6 %collective-permute-start.2 = (bf16[4,2,5,16,384]{4,3,2,1,0:T(8,128)(2,1)}, bf16[4,2,5,16,384]{4,3,2,1,0:T(8,128)(2,1)S(1)}, u32[]{:S(2)}, u32[]{:S(2)}) collective-permute-start(bf16[4,2,5,16,384]{4,3,2,1,0:T(8,128)(2,1)} %slice.8), channel_id=1, source_target_pairs={{0,124},{4,0},{8,4},{12,8},{16,12},{20,16},{24,20},{28,24},{32,28}... | collective-permute-start | bytes 1474568 | tf_op jit(solution)/shard_map/ppermute | solution.py:316
  38.3 1.6 %copy-start.1 = (bf16[3,3,3,96,384]{4,3,2,1,0:T(8,128)(2,1)S(1)}, bf16[3,3,3,96,384]{4,3,2,1,0:T(8,128)(2,1)}, u32[]{:S(2)}) copy-start(bf16[3,3,3,96,384]{4,3,2,1,0:T(8,128)(2,1)} %ahead.3) | copy-start | bytes 5971972
  59.2 6.4 %collective-permute-start.3 = (bf16[2,4,16,384]{3,2,1,0:T(8,128)(2,1)S(1)}, bf16[2,4,16,384]{3,2,1,0:T(8,128)(2,1)S(1)}, u32[]{:S(2)}, u32[]{:S(2)}) collective-permute-start(bf16[2,4,16,384]{3,2,1,0:T(8,128)(2,1)S(1)} %get-tuple-element.14.own), channel_id=1, source_target_pairs={{0,128},{128,256},{256,384},{1,129},{129,257},{257,385},{2,130},{1... | collective-permute-start | bytes 294920 | tf_op jit(solution)/shard_map/ppermute | solution.py:316
  63.4 28.6 %copy-start.2 = (bf16[3,3,3,96,384]{4,3,2,1,0:T(8,128)(2,1)S(1)}, bf16[3,3,3,96,384]{4,3,2,1,0:T(8,128)(2,1)}, u32[]{:S(2)}) copy-start(bf16[3,3,3,96,384]{4,3,2,1,0:T(8,128)(2,1)} %ahead.3) | copy-start | bytes 5971972
  63.4 8.3 %collective-permute-start.4 = (bf16[2,4,16,384]{3,2,1,0:T(8,128)(2,1)S(1)}, bf16[2,4,16,384]{3,2,1,0:T(8,128)(2,1)S(1)}, u32[]{:S(2)}, u32[]{:S(2)}) collective-permute-start(bf16[2,4,16,384]{3,2,1,0:T(8,128)(2,1)S(1)} %get-tuple-element.15.cot), channel_id=1, source_target_pairs={{128,0},{256,128},{384,256},{129,1},{257,129},{385,257},{130,2},{2... | collective-permute-start | bytes 294920 | tf_op jit(solution)/shard_map/ppermute | solution.py:316
  90.0 12.3 %collective-permute-start.5 = (bf16[4,2,5,16,384]{4,3,2,1,0:T(8,128)(2,1)S(1)}, bf16[4,2,5,16,384]{4,3,2,1,0:T(8,128)(2,1)S(1)}, u32[]{:S(2)}, u32[]{:S(2)}) collective-permute-start(bf16[4,2,5,16,384]{4,3,2,1,0:T(8,128)(2,1)S(1)} %slice.9), channel_id=1, source_target_pairs={{0,4},{4,8},{8,12},{12,16},{16,20},{20,24},{24,28},{28,32},{32,36}... | collective-permute-start | bytes 1474568 | tf_op jit(solution)/shard_map/ppermute | solution.py:316
  95.8 18.2 %copy-start.3 = (bf16[2,4,16,384]{3,2,1,0:T(8,128)(2,1)S(1)}, bf16[2,4,16,384]{3,2,1,0:T(8,128)(2,1)}, u32[]{:S(2)}) copy-start(bf16[2,4,16,384]{3,2,1,0:T(8,128)(2,1)} %latent.1) | copy-start | bytes 294916
  95.8 18.2 %copy-start.4 = (bf16[2,4,16,384]{3,2,1,0:T(8,128)(2,1)S(1)}, bf16[2,4,16,384]{3,2,1,0:T(8,128)(2,1)}, u32[]{:S(2)}) copy-start(bf16[2,4,16,384]{3,2,1,0:T(8,128)(2,1)} %cotangent.1) | copy-start | bytes 294916
